TPU v7x, 32 devices: a whole 2x2x4 slice. The times are simulated.
32 devices in a mesh: dp: 8 (over z, x), tensor: 4 (over y, core).
Axes of the slice: x: 2, y: 2, z: 4, core: 2. Of those that a mesh axis runs over, the one named last changes fastest.
Arguments:
- layer_input: bfloat16 [8192, 2048], P(('dp', 'tensor')), may hold values from -6 to 6
- out_grad: bfloat16 [8192, 2048], P(('dp', 'tensor')), may hold values from -6 to 6
- doc_starts: int32 [6], replicated, may hold values from 0 to 8191, as said below
- mixer_gain: bfloat16 [2048], P('dp'), may hold values from 0.099609375 to 1.8984375
- branch_gate: bfloat16 [2048, 2560], P('dp', 'tensor'), may hold values from -0.125 to 0.125
- branch_input: bfloat16 [2048, 2560], P('dp', 'tensor'), may hold values from -0.125 to 0.125
- conv_taps: bfloat16 [4, 16, 160], P(None, 'tensor', 'dp'), may hold values from -3 to 3
- rate_gate: bfloat16 [16, 160, 160], P('tensor', 'dp'), may hold values from -0.5 to 0.5
- input_gate: bfloat16 [16, 160, 160], P('tensor', 'dp'), may hold values from -0.5 to 0.5
- decay_param: bfloat16 [16, 160], P('tensor', 'dp'), may hold values from 3 to 30
- mixer_out: bfloat16 [2560, 2048], P('tensor', 'dp'), may hold values from -0.125 to 0.125
- feed_gain: bfloat16 [2048], P('dp'), may hold values from 0.099609375 to 1.8984375
- feed_gate: bfloat16 [2048, 6144], P('dp', 'tensor'), may hold values from -0.125 to 0.125
- feed_up: bfloat16 [2048, 6144], P('dp', 'tensor'), may hold values from -0.125 to 0.125
- feed_down: bfloat16 [6144, 2048], P('tensor', 'dp'), may hold values from -0.078125 to 0.078125
Outputs:
- layer_output: bfloat16 [8192, 2048], P(('dp', 'tensor'))
- input_grad: bfloat16 [8192, 2048], P(('dp', 'tensor'))
- mixer_gain_grad: float32 [2048], P('dp')
- branch_gate_grad: float32 [2048, 2560], P('dp', 'tensor')
- branch_input_grad: float32 [2048, 2560], P('dp', 'tensor')
- conv_taps_grad: float32 [4, 16, 160], P(None, 'tensor', 'dp')
- rate_gate_grad: float32 [16, 160, 160], P('tensor', 'dp')
- input_gate_grad: float32 [16, 160, 160], P('tensor', 'dp')
- decay_param_grad: float32 [16, 160], P('tensor', 'dp')
- mixer_out_grad: float32 [2560, 2048], P('tensor', 'dp')
- feed_gain_grad: float32 [2048], P('dp')
- feed_gate_grad: float32 [2048, 6144], P('dp', 'tensor')
- feed_up_grad: float32 [2048, 6144], P('dp', 'tensor')
- feed_down_grad: float32 [6144, 2048], P('tensor', 'dp')
Inputs may be any that keep to these rules, and one draw needn't show every extreme that they name: `doc_starts`: the starts rise strictly and the first is 0. One document, which one drawn from the seed, begins within the first 1024 positions and reaches position 7168; every other start lies within the first or the last 1024 positions.
All inputs are finite; a program needn't handle non-finite values.
Results may differ from a plain program's by a relative error of at most 0.02.
Values may be sent and summed in bfloat16 or wider, within the bound.
A program may use at most 256 MiB of HBM per device.

v0:
```python
import jax
import jax.numpy as jnp
from jax import lax
from jax.sharding import PartitionSpec as P

TAPS = 4


EPSILON = 1e-06
GUARD = 0.001


def shifted(value, axis, steps):
    count = lax.axis_size(axis)
    initial, last = (max(0, -steps), min(count, count - steps))
    return lax.ppermute(value, axis, [(source, source + steps) for source in range(initial, last)])


def entering(value, axis, join, neutral, backward):
    count, mine = (lax.axis_size(axis), lax.axis_index(axis))
    pieces = jax.tree.map(lambda part: lax.all_gather(part, axis), value)
    if backward:
        pieces = jax.tree.map(lambda part: part[::-1], pieces)
        mine = count - 1 - mine
    subtotal = jax.tree.map(
        lambda part, zero: jnp.full_like(part, 0) + jnp.asarray(zero, part.dtype), value, neutral
    )

    def hop(position, subtotal):
        longer = join(subtotal, jax.tree.map(lambda part: part[position], pieces))
        return jax.tree.map(lambda new, old: jnp.where(position < mine, new, old), longer, subtotal)

    return lax.fori_loop(0, count - 1, hop, subtotal)


def pair_join(earlier, later):
    return (earlier[0] * later[0], earlier[1] * later[0] + later[1])


def doc_index(places, doc_starts):
    return jnp.sum((doc_starts[None, :] <= places[:, None]).astype(jnp.int32), axis=1)


def norm_back(grad_unit, unit_rows, scale_rows):
    return scale_rows * (
        grad_unit - unit_rows * jnp.mean(grad_unit * unit_rows, axis=1, keepdims=True)
    )


def shards(
    layer_input,
    out_grad,
    doc_starts,
    mixer_gain,
    branch_gate,
    branch_input,
    conv_taps,
    rate_gate,
    input_gate,
    decay_param,
    mixer_out,
    feed_gain,
    feed_gate,
    feed_up,
    feed_down,
):
    gathered = (
        lax.all_gather(mixer_gain, "dp", axis=0, tiled=True),
        lax.all_gather(branch_gate, "dp", axis=0, tiled=True),
        lax.all_gather(branch_input, "dp", axis=0, tiled=True),
        lax.all_gather(conv_taps, "dp", axis=2, tiled=True),
        lax.all_gather(rate_gate, "dp", axis=1, tiled=True),
        lax.all_gather(input_gate, "dp", axis=1, tiled=True),
        lax.all_gather(decay_param, "dp", axis=1, tiled=True),
        lax.all_gather(mixer_out, "dp", axis=1, tiled=True),
        lax.all_gather(feed_gain, "dp", axis=0, tiled=True),
        lax.all_gather(feed_gate, "dp", axis=0, tiled=True),
        lax.all_gather(feed_up, "dp", axis=0, tiled=True),
        lax.all_gather(feed_down, "dp", axis=1, tiled=True),
    )
    (
        gain_one,
        gate_weights,
        entry_weights,
        tap_weights,
        rate_weights,
        inlet_weights,
        decay_values,
        outlet_weights,
        gain_two,
        gating_weights,
        lifting_weights,
        lowering_weights,
    ) = gathered
    row_count = layer_input.shape[0]
    feature_count = layer_input.shape[1]
    tensor_count = lax.axis_size("tensor")
    block_rows = row_count * tensor_count
    head_count = rate_weights.shape[0]
    lane_count = head_count * rate_weights.shape[2]
    first_row = lax.axis_index("tensor") * row_count
    anchor = lax.axis_index("dp") * block_rows
    lead_rows = TAPS - 1
    all_rows, cot_all = (
        lax.all_gather(layer_input, "tensor", axis=0, tiled=True),
        lax.all_gather(out_grad, "tensor", axis=0, tiled=True),
    )
    residual = all_rows.astype(jnp.float32)
    scale_one = lax.rsqrt(jnp.mean(residual * residual, axis=1, keepdims=True) + EPSILON)
    unit_one = residual * scale_one
    gain_first = gain_one.astype(jnp.float32)
    normed_one = (unit_one * gain_first).astype(jnp.bfloat16)
    gate_pre = jnp.dot(normed_one, gate_weights, preferred_element_type=jnp.float32)
    entry_pre = jnp.dot(normed_one, entry_weights, preferred_element_type=jnp.float32)
    before = shifted(entry_pre[block_rows - lead_rows :], "dp", 1)
    extended = jnp.concatenate([before, entry_pre], axis=0)
    seg_back = doc_index(anchor + jnp.arange(-lead_rows, block_rows, dtype=jnp.int32), doc_starts)
    tap_table = tap_weights.astype(jnp.float32).reshape(TAPS, lane_count)
    convolved = jnp.zeros((block_rows, lane_count), jnp.float32)
    same_masks = []
    for offset in range(TAPS):
        same_doc = (
            seg_back[lead_rows - offset : lead_rows - offset + block_rows] == seg_back[lead_rows:]
        ).astype(jnp.float32)[:, None]
        same_masks.append(same_doc)
        convolved = (
            convolved
            + tap_table[offset]
            * extended[lead_rows - offset : lead_rows - offset + block_rows]
            * same_doc
        )
    conv_low = convolved.astype(jnp.bfloat16)
    blocked = conv_low.reshape(block_rows, head_count, -1)
    rate_pre = jnp.einsum(
        "thc,hcd->thd", blocked, rate_weights, preferred_element_type=jnp.float32
    ).reshape(block_rows, lane_count)
    inlet_pre = jnp.einsum(
        "thc,hcd->thd", blocked, inlet_weights, preferred_element_type=jnp.float32
    ).reshape(block_rows, lane_count)
    places = anchor + jnp.arange(block_rows, dtype=jnp.int32)
    starts_here = jnp.any(doc_starts[None, :] == places[:, None], axis=1)[:, None]
    open_mask = 1.0 - starts_here.astype(jnp.float32)
    decay_flat = decay_values.astype(jnp.float32).reshape(lane_count)
    softened = jax.nn.softplus(-decay_flat)
    recur_gate = jax.nn.sigmoid(rate_pre)
    admit_gate = jax.nn.sigmoid(inlet_pre)
    log_decay = -8.0 * recur_gate * softened
    decays = jnp.exp(log_decay)
    root_norm = jnp.sqrt(GUARD - jnp.expm1(2.0 * log_decay))
    carry_decay = decays * open_mask
    norm_root = jnp.where(starts_here, 1.0, root_norm)
    products, local_state = lax.associative_scan(
        pair_join, (carry_decay, norm_root * admit_gate * convolved), axis=0
    )
    identity = (jnp.ones((lane_count,), jnp.float32), jnp.zeros((lane_count,), jnp.float32))
    unused_prod, state_in = entering(
        (products[block_rows - 1], local_state[block_rows - 1]), "dp", pair_join, identity, False
    )
    state = local_state + products * state_in[None, :]
    gate_act, gate_pull = jax.vjp(jax.nn.gelu, gate_pre)
    merged = (state * gate_act).astype(jnp.bfloat16)
    mixer_part = jnp.dot(merged, outlet_weights, preferred_element_type=jnp.float32)
    hidden_one = residual + lax.psum(mixer_part, "tensor")
    scale_two = lax.rsqrt(jnp.mean(hidden_one * hidden_one, axis=1, keepdims=True) + EPSILON)
    unit_two = hidden_one * scale_two
    gain_second = gain_two.astype(jnp.float32)
    normed_two = (unit_two * gain_second).astype(jnp.bfloat16)
    gating_pre = jnp.dot(normed_two, gating_weights, preferred_element_type=jnp.float32)
    lifting_pre = jnp.dot(normed_two, lifting_weights, preferred_element_type=jnp.float32)
    gating_act, gating_pull = jax.vjp(jax.nn.gelu, gating_pre)
    hidden = (gating_act * lifting_pre).astype(jnp.bfloat16)
    feed_rows = lax.psum_scatter(
        jnp.dot(hidden, lowering_weights, preferred_element_type=jnp.float32).astype(jnp.bfloat16),
        "tensor",
        scatter_dimension=0,
        tiled=True,
    ).astype(jnp.float32)
    hidden_own = lax.dynamic_slice_in_dim(hidden_one, first_row, row_count, 0)
    layer_output = (hidden_own + feed_rows).astype(jnp.bfloat16)
    lowering_grad = jnp.einsum("tf,td->fd", hidden, cot_all, preferred_element_type=jnp.float32)
    grad_hidden = jnp.einsum(
        "td,fd->tf", cot_all, lowering_weights, preferred_element_type=jnp.float32
    )
    grad_gating = gating_pull(grad_hidden * lifting_pre)[0].astype(jnp.bfloat16)
    grad_lifting = (grad_hidden * gating_act).astype(jnp.bfloat16)
    gating_grad = jnp.einsum(
        "td,tf->df", normed_two, grad_gating, preferred_element_type=jnp.float32
    )
    lifting_grad = jnp.einsum(
        "td,tf->df", normed_two, grad_lifting, preferred_element_type=jnp.float32
    )
    grad_normed_two = lax.psum_scatter(
        (
            jnp.einsum("tf,df->td", grad_gating, gating_weights, preferred_element_type=jnp.float32)
            + jnp.einsum(
                "tf,df->td", grad_lifting, lifting_weights, preferred_element_type=jnp.float32
            )
        ).astype(jnp.bfloat16),
        "tensor",
        scatter_dimension=0,
        tiled=True,
    ).astype(jnp.float32)
    unit_two_own = lax.dynamic_slice_in_dim(unit_two, first_row, row_count, 0)
    scale_two_own = lax.dynamic_slice_in_dim(scale_two, first_row, row_count, 0)
    gain_two_part = jnp.sum(grad_normed_two * unit_two_own, axis=0)
    grad_hidden_one = out_grad.astype(jnp.float32) + norm_back(
        grad_normed_two * gain_second, unit_two_own, scale_two_own
    )
    back_low = lax.all_gather(grad_hidden_one.astype(jnp.bfloat16), "tensor", axis=0, tiled=True)
    outlet_grad = jnp.einsum("tr,td->rd", merged, back_low, preferred_element_type=jnp.float32)
    grad_merged = jnp.einsum(
        "td,rd->tr", back_low, outlet_weights, preferred_element_type=jnp.float32
    )
    grad_gate_pre = gate_pull(grad_merged * state)[0].astype(jnp.bfloat16)
    grad_direct = grad_merged * gate_act
    next_decay = jnp.concatenate([carry_decay[1:], jnp.ones((1, lane_count), jnp.float32)], axis=0)
    rev_products, rev_local = lax.associative_scan(
        pair_join, (jnp.flip(next_decay, 0), jnp.flip(grad_direct, 0)), axis=0
    )
    rev_products = jnp.flip(rev_products, 0)
    rev_local = jnp.flip(rev_local, 0)
    unused_back, grad_in = entering(
        (carry_decay[0] * rev_products[0], carry_decay[0] * rev_local[0]),
        "dp",
        pair_join,
        identity,
        True,
    )
    grad_state = rev_local + rev_products * grad_in[None, :]
    previous = jnp.concatenate([state_in[None, :], state[:-1]], axis=0)
    grad_log = open_mask * (
        grad_state * previous * decays
        - grad_state * admit_gate * convolved * decays * decays / root_norm
    )
    decay_grad = (
        -jax.nn.sigmoid(-decay_flat) * jnp.sum(grad_log * (-8.0 * recur_gate), axis=0)
    ).reshape(head_count, -1)
    grad_recur = (
        (grad_log * (-8.0 * softened) * recur_gate * (1.0 - recur_gate))
        .astype(jnp.bfloat16)
        .reshape(block_rows, head_count, -1)
    )
    grad_admit = (
        (grad_state * norm_root * convolved * admit_gate * (1.0 - admit_gate))
        .astype(jnp.bfloat16)
        .reshape(block_rows, head_count, -1)
    )
    rate_grad = jnp.einsum("thc,thd->hcd", blocked, grad_recur, preferred_element_type=jnp.float32)
    inlet_grad = jnp.einsum("thc,thd->hcd", blocked, grad_admit, preferred_element_type=jnp.float32)
    grad_conv = grad_state * norm_root * admit_gate + (
        jnp.einsum("thd,hcd->thc", grad_recur, rate_weights, preferred_element_type=jnp.float32)
        + jnp.einsum("thd,hcd->thc", grad_admit, inlet_weights, preferred_element_type=jnp.float32)
    ).reshape(block_rows, lane_count)
    after_rows = shifted(grad_conv[:lead_rows], "dp", -1)
    grad_ext = jnp.concatenate([grad_conv, after_rows], axis=0)
    seg_fore = doc_index(anchor + jnp.arange(block_rows + lead_rows, dtype=jnp.int32), doc_starts)
    grad_entry = jnp.zeros((block_rows, lane_count), jnp.float32)
    tap_grads = []
    for offset in range(TAPS):
        ahead_doc = (seg_fore[offset : offset + block_rows] == seg_fore[:block_rows]).astype(
            jnp.float32
        )[:, None]
        grad_entry = (
            grad_entry + tap_table[offset] * grad_ext[offset : offset + block_rows] * ahead_doc
        )
        tap_grads.append(
            jnp.sum(
                grad_conv
                * extended[lead_rows - offset : lead_rows - offset + block_rows]
                * same_masks[offset],
                axis=0,
            )
        )
    taps_grad = jnp.stack(tap_grads, axis=0).reshape(TAPS, head_count, -1)
    entry_low = grad_entry.astype(jnp.bfloat16)
    gate_grad = jnp.einsum(
        "td,tr->dr", normed_one, grad_gate_pre, preferred_element_type=jnp.float32
    )
    entry_grad = jnp.einsum("td,tr->dr", normed_one, entry_low, preferred_element_type=jnp.float32)
    part_one = jnp.einsum(
        "tr,dr->td", grad_gate_pre, gate_weights, preferred_element_type=jnp.float32
    ) + jnp.einsum("tr,dr->td", entry_low, entry_weights, preferred_element_type=jnp.float32)
    gain_one_part = jnp.sum(part_one * unit_one, axis=0)
    gain_terms = jnp.broadcast_to(
        jnp.stack([gain_one_part, gain_two_part], axis=0)[None], (tensor_count, 2, feature_count)
    )
    grad_normed_one, gain_sums = (
        lax.psum_scatter(
            part_one.astype(jnp.bfloat16), "tensor", scatter_dimension=0, tiled=True
        ).astype(jnp.float32),
        lax.psum_scatter(
            gain_terms.astype(jnp.bfloat16), "tensor", scatter_dimension=0, tiled=True
        ).astype(jnp.float32),
    )
    gain_one_grad = gain_sums[0, 0]
    gain_two_grad = gain_sums[0, 1]
    unit_one_own = lax.dynamic_slice_in_dim(unit_one, first_row, row_count, 0)
    scale_one_own = lax.dynamic_slice_in_dim(scale_one, first_row, row_count, 0)
    input_grad = (
        grad_hidden_one + norm_back(grad_normed_one * gain_first, unit_one_own, scale_one_own)
    ).astype(jnp.bfloat16)
    results = tuple(
        (
            lax.psum_scatter(
                gain_one_grad.astype(jnp.bfloat16), "dp", scatter_dimension=0, tiled=True
            ).astype(jnp.float32),
            lax.psum_scatter(
                gate_grad.astype(jnp.bfloat16), "dp", scatter_dimension=0, tiled=True
            ).astype(jnp.float32),
            lax.psum_scatter(
                entry_grad.astype(jnp.bfloat16), "dp", scatter_dimension=0, tiled=True
            ).astype(jnp.float32),
            lax.psum_scatter(
                taps_grad.astype(jnp.bfloat16), "dp", scatter_dimension=2, tiled=True
            ).astype(jnp.float32),
            lax.psum_scatter(
                rate_grad.astype(jnp.bfloat16), "dp", scatter_dimension=1, tiled=True
            ).astype(jnp.float32),
            lax.psum_scatter(
                inlet_grad.astype(jnp.bfloat16), "dp", scatter_dimension=1, tiled=True
            ).astype(jnp.float32),
            lax.psum_scatter(
                decay_grad.astype(jnp.bfloat16), "dp", scatter_dimension=1, tiled=True
            ).astype(jnp.float32),
            lax.psum_scatter(
                outlet_grad.astype(jnp.bfloat16), "dp", scatter_dimension=1, tiled=True
            ).astype(jnp.float32),
            lax.psum_scatter(
                gain_two_grad.astype(jnp.bfloat16), "dp", scatter_dimension=0, tiled=True
            ).astype(jnp.float32),
            lax.psum_scatter(
                gating_grad.astype(jnp.bfloat16), "dp", scatter_dimension=0, tiled=True
            ).astype(jnp.float32),
            lax.psum_scatter(
                lifting_grad.astype(jnp.bfloat16), "dp", scatter_dimension=0, tiled=True
            ).astype(jnp.float32),
            lax.psum_scatter(
                lowering_grad.astype(jnp.bfloat16), "dp", scatter_dimension=1, tiled=True
            ).astype(jnp.float32),
        )
    )
    return (layer_output, input_grad) + results


def solution(mesh):
    placed = (
        P(("dp", "tensor"), None),
        P(("dp", "tensor"), None),
        P(),
        P("dp"),
        P("dp", "tensor"),
        P("dp", "tensor"),
        P(None, "tensor", "dp"),
        P("tensor", "dp", None),
        P("tensor", "dp", None),
        P("tensor", "dp"),
        P("tensor", "dp"),
        P("dp"),
        P("dp", "tensor"),
        P("dp", "tensor"),
        P("tensor", "dp"),
    )
    return jax.shard_map(
        shards,
        mesh=mesh,
        in_specs=placed,
        out_specs=(
            P(("dp", "tensor"), None),
            P(("dp", "tensor"), None),
            P("dp"),
            P("dp", "tensor"),
            P("dp", "tensor"),
            P(None, "tensor", "dp"),
            P("tensor", "dp", None),
            P("tensor", "dp", None),
            P("tensor", "dp"),
            P("tensor", "dp"),
            P("dp"),
            P("dp", "tensor"),
            P("dp", "tensor"),
            P("tensor", "dp"),
        ),
        check_vma=False,
    )
```

profile of v0, /device:TPU:0, one launch (start us, length us, event | category | flops | bytes accessed | tf_op | source)
XLA Modules:
  0.0 1930.3 jit_solution(1484584056231576739)
XLA Ops:
  10.7 22.2 %all-gather = bf16[8,1,256]{2,1,0:T(2,128)(2,1)S(1)} all-gather(bf16[1,1,256]{2,1,0:T(2,128)(2,1)S(1)} %reshape.189), channel_id=1, replica_groups=mesh['dp'=8,'tensor'=4] {'dp'}, dimensions={0}, use_global_device_ids=true | all-gather | bytes 4608 | tf_op jit(solution)/shard_map/all_gather | solution.py:68
  35.8 30.9 %all_gather.60 = bf16[4,4,160]{1,0,2:T(4,128)(2,1)S(1)} all-gather(bf16[4,4,20]{1,0,2:T(4,128)(2,1)S(1)} %copy.137), channel_id=1, replica_groups=mesh['dp'=8,'tensor'=4] {'dp'}, dimensions={2}, use_global_device_ids=true | all-gather | bytes 5760 | tf_op jit(solution)/shard_map/all_gather | solution.py:71
  67.6 31.6 %all_gather.63 = bf16[4,160,160]{2,0,1:T(4,128)(2,1)S(1)} all-gather(bf16[4,20,160]{2,0,1:T(4,128)(2,1)S(1)} %copy-done.60), channel_id=1, replica_groups=mesh['dp'=8,'tensor'=4] {'dp'}, dimensions={1}, use_global_device_ids=true | all-gather | bytes 230400 | tf_op jit(solution)/shard_map/all_gather | solution.py:72
  99.9 16.5 all-gather.1
  131.0 32.2 %all_gather.65 = bf16[4,160,160]{2,0,1:T(4,128)(2,1)S(1)} all-gather(bf16[4,20,160]{2,0,1:T(4,128)(2,1)S(1)} %copy-done.61), channel_id=1, replica_groups=mesh['dp'=8,'tensor'=4] {'dp'}, dimensions={1}, use_global_device_ids=true | all-gather | bytes 230400 | tf_op jit(solution)/shard_map/all_gather | solution.py:73
  388.7 30.2 %all-gather.3 = f32[8,1,640]{2,1,0:T(1,128)S(1)} all-gather(f32[1,1,640]{2,1,0:T(1,128)S(1)} %add_bitcast_fusion), channel_id=1, replica_groups=mesh['dp'=8,'tensor'=4] {'dp'}, dimensions={0}, use_global_device_ids=true | all-gather | bytes 23040 | tf_op jit(solution)/shard_map/all_gather | solution.py:21
  430.5 30.2 %all-gather.2 = f32[8,1,640]{2,1,0:T(1,128)S(1)} all-gather(f32[1,1,640]{2,1,0:T(1,128)S(1)} %add_bitcast_fusion.1), channel_id=1, replica_groups=mesh['dp'=8,'tensor'=4] {'dp'}, dimensions={0}, use_global_device_ids=true | all-gather | bytes 23040 | tf_op jit(solution)/shard_map/all_gather | solution.py:21
  461.2 12.4 multiply_convert_fusion.6
  473.6 7.8 fusion.100
  484.3 16.3 all-gather.4
  500.6 131.0 %all-reduce.94.cloned.1.call-done = f32[1024,2048]{1,0:T(8,128)} async-done(((f32[1024,2048]{1,0:T(8,128)}), f32[1024,2048]{1,0:T(8,128)}) %all-reduce.94.cloned.1.call-update) | async-done | bytes 8388624 | tf_op jit(solution)/shard_map/psum | solution.py:163
  646.5 86.3 %all-gather.25.cloned.1.call-done = bf16[2048,1536]{1,0:T(8,128)(2,1)} async-done(((bf16[256,1536]{1,0:T(8,128)(2,1)}), bf16[2048,1536]{1,0:T(8,128)(2,1)}) %all-gather.25.cloned.1.call-update) | async-done | bytes 6291472 | tf_op jit(solution)/shard_map/all_gather | solution.py:77
  732.8 11.9 fusion.101
  744.8 87.5 %all-gather.27.cloned.1.call-done = bf16[2048,1536]{1,0:T(8,128)(2,1)} async-done(((bf16[256,1536]{1,0:T(8,128)(2,1)}), bf16[2048,1536]{1,0:T(8,128)(2,1)}) %all-gather.27.cloned.1.call-update) | async-done | bytes 6291472 | tf_op jit(solution)/shard_map/all_gather | solution.py:78
  832.3 11.6 fusion.102
  843.9 22.6 %all-gather.31.cloned.1.call-done = bf16[1024,2048]{1,0:T(8,128)(2,1)} async-done(((bf16[256,2048]{1,0:T(8,128)(2,1)}), bf16[1024,2048]{1,0:T(8,128)(2,1)}) %all-gather.31.cloned.1.call-update) | async-done | bytes 4194320 | tf_op jit(solution)/shard_map/all_gather | solution.py:106
  866.5 102.0 %all-gather.29.cloned.1.call-done = bf16[1536,2048]{1,0:T(8,128)(2,1)} async-done(((bf16[1536,256]{1,0:T(8,128)(2,1)}), bf16[1536,2048]{1,0:T(8,128)(2,1)}) %all-gather.29.cloned.1.call-update) | async-done | bytes 6291472 | tf_op jit(solution)/shard_map/all_gather | solution.py:79
  968.5 18.0 multiply_convert_fusion.2
  986.6 11.4 fusion.103
  998.0 8.3 add_convert_fusion
  1006.5 42.7 %reduce-scatter.14.cloned.1.call-done = bf16[256,2048]{1,0:T(8,128)(2,1)} async-done(((bf16[1024,2048]{1,0:T(8,128)(2,1)}), bf16[256,2048]{1,0:T(8,128)(2,1)}) %reduce-scatter.14.cloned.1.call-update) | async-done | bytes 1048592 | tf_op jit(solution)/shard_map/reduce_scatter | solution.py:192
  1055.7 11.1 convolution_convert_fusion.3
  1068.7 11.0 convolution_convert_fusion.2
  1081.5 11.4 convolution_convert_fusion.1
  1094.8 10.8 convolution_convert_fusion
  1131.0 10.7 slice.820
  1141.7 10.7 slice.826
  1152.5 11.0 slice.894
  1163.5 11.4 fusion.41
  1188.9 10.7 slice.817
  1199.6 10.7 slice.822
  1372.9 9.1 pad.325
  1395.7 9.1 pad.305
  1404.8 11.2 slice.896
  1422.2 9.3 pad.304
  1433.9 9.2 pad.324
  1450.3 30.5 %all-gather.5 = f32[8,1,640]{2,1,0:T(1,128)S(1)} all-gather(f32[1,1,640]{2,1,0:T(1,128)S(1)} %get-tuple-element.334), channel_id=1, replica_groups=mesh['dp'=8,'tensor'=4] {'dp'}, dimensions={0}, use_global_device_ids=true | all-gather | bytes 23040 | tf_op jit(solution)/shard_map/all_gather | solution.py:21
  1480.9 30.9 %all-gather.6 = f32[8,1,640]{2,1,0:T(1,128)S(1)} all-gather(f32[1,1,640]{2,1,0:T(1,128)S(1)} %get-tuple-element.333), channel_id=1, replica_groups=mesh['dp'=8,'tensor'=4] {'dp'}, dimensions={0}, use_global_device_ids=true | all-gather | bytes 23040 | tf_op jit(solution)/shard_map/all_gather | solution.py:21
  1511.9 20.8 %rev.16 = f32[1024,640]{1,0:T(8,128)} reverse(f32[1024,640]{1,0:T(8,128)} %add.758), dimensions={0} | reverse | bytes 5242880 | tf_op jit(solution)/shard_map/jit(_flip)/rev | solution.py:220
  1532.8 21.1 %rev.15 = f32[1024,640]{1,0:T(8,128)} reverse(f32[1024,640]{1,0:T(8,128)} %add.748), dimensions={0} | reverse | bytes 5242880 | tf_op jit(solution)/shard_map/jit(_flip)/rev | solution.py:221
  1554.4 9.2 multiply_convert_fusion.4
  1584.2 7.9 convolution_convert_fusion.6
  1649.5 10.4 all-reduce.82
  1660.7 36.0 %all-reduce.89 = (bf16[2048]{0:T(1024)(128)(2,1)S(1)}, bf16[4,4,160]{2,1,0:T(4,128)(2,1)S(1)}, bf16[4,160]{1,0:T(4,128)(2,1)S(1)}, bf16[2048]{0:T(1024)(128)(2,1)S(1)}) all-reduce(bf16[2048]{0:T(1024)(128)(2,1)S(1)} %get-tuple-element.275, ...), channel_id=6, replica_groups=mesh['dp'=8,'tensor'=4] {'dp'}, use_global_device_ids=true, to_apply=%region_18.19.clone | all-reduce | flops 7296 | bytes 29184
  1702.1 21.9 %reduce-scatter.22.cloned.1.call-done = bf16[640,256]{1,0:T(8,128)(2,1)} async-done(((bf16[640,2048]{1,0:T(8,128)(2,1)}), bf16[640,256]{1,0:T(8,128)(2,1)}) %reduce-scatter.22.cloned.1.call-update) | async-done | bytes 327696 | tf_op jit(solution)/shard_map/reduce_scatter | solution.py:325
  1725.8 71.5 %reduce-scatter.18.cloned.1.call-done = bf16[256,640]{1,0:T(8,128)(2,1)} async-done(((bf16[2048,640]{1,0:T(8,128)(2,1)}), bf16[256,640]{1,0:T(8,128)(2,1)}) %reduce-scatter.18.cloned.1.call-update) | async-done | bytes 327696 | tf_op jit(solution)/shard_map/reduce_scatter | solution.py:307
  1799.2 71.4 %reduce-scatter.20.cloned.1.call-done = bf16[256,640]{1,0:T(8,128)(2,1)} async-done(((bf16[2048,640]{1,0:T(8,128)(2,1)}), bf16[256,640]{1,0:T(8,128)(2,1)}) %reduce-scatter.20.cloned.1.call-update) | async-done | bytes 327696 | tf_op jit(solution)/shard_map/reduce_scatter | solution.py:310
  1872.5 44.1 %reduce-scatter.16.cloned.1.call-done = bf16[256,2048]{1,0:T(8,128)(2,1)} async-done(((bf16[1024,2048]{1,0:T(8,128)(2,1)}), bf16[256,2048]{1,0:T(8,128)(2,1)}) %reduce-scatter.16.cloned.1.call-update) | async-done | bytes 1048592 | tf_op jit(solution)/shard_map/reduce_scatter | solution.py:288
  (755 shorter events, 615.9 us)
Async XLA Ops:
  7.2 92.0 %copy-start.112 = (s32[6]{0:T(128)S(1)}, s32[6]{0:T(128)}, u32[]{:S(2)}) copy-start(s32[6]{0:T(128)} %param.21) | copy-start | bytes 76
  7.2 60.4 %copy-start.60 = (bf16[4,20,160]{2,0,1:T(4,128)(2,1)S(1)}, bf16[4,20,160]{2,0,1:T(4,128)(2,1)}, u32[]{:S(2)}) copy-start(bf16[4,20,160]{2,0,1:T(4,128)(2,1)} %param.26) | copy-start | bytes 76804
  7.2 92.7 %copy-start.113 = (bf16[4,20]{1,0:T(4,128)(2,1)S(1)}, bf16[4,20]{1,0:T(4,128)(2,1)}, u32[]{:S(2)}) copy-start(bf16[4,20]{1,0:T(4,128)(2,1)} %param.28) | copy-start | bytes 484
  7.2 109.9 %all-gather.17.cloned.1.call-start = ((), (), s32[]{:S(2)}) async-start(), calls=%async_computation.9 | async-start | bytes 5242880 | tf_op jit(solution)/shard_map/all_gather | solution.py:105
  7.9 112.3 %all-gather.19.cloned.1.call-start = ((), (), s32[]{:S(2)}) async-start(), calls=%async_computation.10 | async-start | bytes 2949120 | tf_op jit(solution)/shard_map/all_gather | solution.py:70
  8.7 452.5 %all-gather.21.cloned.1.call-start = ((), (), s32[]{:S(2)}) async-start(), calls=%async_computation.11 | async-start | bytes 2949120 | tf_op jit(solution)/shard_map/all_gather | solution.py:69
  9.4 464.2 %all-gather.23.cloned.1.call-start = ((), (), s32[]{:S(2)}) async-start(), calls=%async_computation.12 | async-start | bytes 2949120 | tf_op jit(solution)/shard_map/all_gather | solution.py:75
  10.0 621.6 %all-reduce.94.cloned.1.call-start = ((), (), s32[]{:S(2)}) async-start(), calls=%async_computation.13 | async-start | bytes 16777216 | tf_op jit(solution)/shard_map/psum | solution.py:163
  33.0 87.3 %copy-start.48 = (f32[8,1,256]{2,1,0:T(1,128)}, f32[8,1,256]{2,1,0:T(1,128)S(1)}, u32[]{:S(2)}) copy-start(f32[8,1,256]{2,1,0:T(1,128)S(1)} %convert_element_type.249) | copy-start | bytes 24580
  35.0 133.0 %copy-start.64 = (f32[1024]{0:T(1024)}, f32[1024]{0:T(1024)S(1)}, u32[]{:S(2)}) copy-start(f32[1024]{0:T(1024)S(1)} %get-tuple-element.416) | copy-start | bytes 12292
  35.0 133.0 %copy-start.66 = (f32[1024]{0:T(1024)}, f32[1024]{0:T(1024)S(1)}, u32[]{:S(2)}) copy-start(f32[1024]{0:T(1024)S(1)} %get-tuple-element.417) | copy-start | bytes 12292
  99.2 75.1 %copy-start.33 = (bf16[4,160,160]{2,0,1:T(4,128)(2,1)}, bf16[4,160,160]{2,0,1:T(4,128)(2,1)S(1)}, u32[]{:S(2)}) copy-start(bf16[4,160,160]{2,0,1:T(4,128)(2,1)S(1)} %all_gather.63) | copy-start | bytes 614404
  99.9 84.9 %copy-start.62 = (f32[1024]{0:T(1024)}, f32[1024]{0:T(1024)S(1)}, u32[]{:S(2)}) copy-start(f32[1024]{0:T(1024)S(1)} %convert_subtract_fusion) | copy-start | bytes 12292
  117.1 67.7 %copy-start.52 = (f32[640]{0:T(1024)}, f32[640]{0:T(1024)S(1)}, u32[]{:S(2)}) copy-start(f32[640]{0:T(1024)S(1)} %fusion.62) | copy-start | bytes 7684
  126.6 45.2 %copy-start.10 = (f32[1024,640]{1,0:T(8,128)}, f32[1024,640]{1,0:T(8,128)S(1)}, u32[]{:S(2)}) copy-start(f32[1024,640]{1,0:T(8,128)S(1)} %fusion.84) | copy-start | bytes 7864324
  127.3 40.7 %collective-permute-start = (f32[3,640]{1,0:T(4,128)}, f32[3,640]{1,0:T(4,128)S(1)}, u32[]{:S(2)}, u32[]{:S(2)}) collective-permute-start(f32[3,640]{1,0:T(4,128)} %slice.930), channel_id=1, source_target_pairs={{0,4},{4,8},{8,12},{12,16},{16,20},{20,24},{24,28},{1,5},{5,9},{9,... | collective-permute-start | bytes 23048 | tf_op jit(solution)/shard_map/ppermute | solution.py:16
  382.7 36.2 %copy-start.22 = (f32[511,640]{1,0:T(8,128)S(1)}, f32[511,640]{1,0:T(8,128)}, u32[]{:S(2)}) copy-start(f32[511,640]{1,0:T(8,128)} %get-tuple-element.340) | copy-start | bytes 3924484
  424.4 36.8 %copy-start.49 = (f32[8,1,256]{2,1,0:T(1,128)S(1)}, f32[8,1,256]{2,1,0:T(1,128)}, u32[]{:S(2)}) copy-start(f32[8,1,256]{2,1,0:T(1,128)} %copy-done.48) | copy-start | bytes 24580
  424.4 36.8 %copy-start.77 = (f32[1024]{0:T(1024)S(1)}, f32[1024]{0:T(1024)}, u32[]{:S(2)}) copy-start(f32[1024]{0:T(1024)} %copy-done.76) | copy-start | bytes 12292
  481.5 251.4 %all-gather.25.cloned.1.call-start = ((), (), s32[]{:S(2)}) async-start(), calls=%async_computation.14 | async-start | bytes 7077888 | tf_op jit(solution)/shard_map/all_gather | solution.py:77
  482.0 350.2 %all-gather.27.cloned.1.call-start = ((), (), s32[]{:S(2)}) async-start(), calls=%async_computation.15 | async-start | bytes 7077888 | tf_op jit(solution)/shard_map/all_gather | solution.py:78
  482.8 383.8 %all-gather.31.cloned.1.call-start = ((), (), s32[]{:S(2)}) async-start(), calls=%async_computation.18 | async-start | bytes 5242880 | tf_op jit(solution)/shard_map/all_gather | solution.py:106
  483.5 485.0 %all-gather.29.cloned.1.call-start = ((), (), s32[]{:S(2)}) async-start(), calls=%async_computation.16 | async-start | bytes 7077888 | tf_op jit(solution)/shard_map/all_gather | solution.py:79
  484.3 564.9 %reduce-scatter.14.cloned.1.call-start = ((), (), s32[]{:S(2)}) async-start(), calls=%async_computation.19 | async-start | bytes 5242880 | tf_op jit(solution)/shard_map/reduce_scatter | solution.py:192
  500.6 551.8 %copy-start.42 = (f32[8,1,256]{2,1,0:T(1,128)}, f32[8,1,256]{2,1,0:T(1,128)S(1)}, u32[]{:S(2)}) copy-start(f32[8,1,256]{2,1,0:T(1,128)S(1)} %convert_element_type.251) | copy-start | bytes 24580
  1006.3 46.1 %copy-start.15 = (bf16[256,2048]{1,0:T(8,128)(2,1)S(1)}, bf16[256,2048]{1,0:T(8,128)(2,1)}, u32[]{:S(2)}) copy-start(bf16[256,2048]{1,0:T(8,128)(2,1)} %param.20) | copy-start | bytes 3145732
  1006.4 157.1 %all-gather.33.cloned.1.call-start = ((), (), s32[]{:S(2)}) async-start(), calls=%async_computation.20 | async-start | bytes 5242880 | tf_op jit(solution)/shard_map/all_gather | solution.py:209
  1006.5 49.1 %copy-start.108 = (f32[256]{0:T(256)}, f32[256]{0:T(256)S(1)}, u32[]{:S(2)}) copy-start(f32[256]{0:T(256)S(1)} %dynamic-slice.6) | copy-start | bytes 3076
  1055.7 582.8 %reduce-scatter.12.cloned.1.call-start = ((), (), s32[]{:S(2)}) async-start(), calls=%async_computation.17 | async-start | bytes 5242880 | tf_op jit(solution)/shard_map/reduce_scatter | solution.py:172
  1066.8 574.8 %reduce-scatter.24.cloned.1.call-start = ((), (), s32[]{:S(2)}) async-start(), calls=%async_computation.25 | async-start | bytes 7077888 | tf_op jit(solution)/shard_map/reduce_scatter | solution.py:331
  1079.7 564.4 %reduce-scatter.26.cloned.1.call-start = ((), (), s32[]{:S(2)}) async-start(), calls=%async_computation.26 | async-start | bytes 7077888 | tf_op jit(solution)/shard_map/reduce_scatter | solution.py:334
  1093.0 553.6 %reduce-scatter.28.cloned.1.call-start = ((), (), s32[]{:S(2)}) async-start(), calls=%async_computation.27 | async-start | bytes 7077888 | tf_op jit(solution)/shard_map/reduce_scatter | solution.py:337
  1105.7 593.6 %all-reduce.96.cloned.1.call-start = ((), (), s32[]{:S(2)}) async-start(), calls=%async_computation.28 | async-start | bytes 1310720
  1532.8 21.6 %copy-start.2 = (f32[1024,640]{1,0:T(8,128)S(1)}, f32[1024,640]{1,0:T(8,128)}, u32[]{:S(2)}) copy-start(f32[1024,640]{1,0:T(8,128)} %copy-done.1) | copy-start | bytes 7864324
  1532.8 21.6 %copy-start.53 = (f32[640]{0:T(1024)S(1)}, f32[640]{0:T(1024)}, u32[]{:S(2)}) copy-start(f32[640]{0:T(1024)} %copy-done.52) | copy-start | bytes 7684
  1532.8 21.6 %copy-start.63 = (f32[1024]{0:T(1024)S(1)}, f32[1024]{0:T(1024)}, u32[]{:S(2)}) copy-start(f32[1024]{0:T(1024)} %copy-done.62) | copy-start | bytes 12292
  1532.8 21.6 %copy-start.85 = (pred[1024]{0:T(1024)(128)(4,1)S(1)}, pred[1024]{0:T(1024)(128)(4,1)}, u32[]{:S(2)}) copy-start(pred[1024]{0:T(1024)(128)(4,1)} %copy-done.83) | copy-start | bytes 3076
  1532.8 21.6 %copy-start.86 = (f32[1,640]{1,0:T(1,128)S(1)}, f32[1,640]{1,0:T(1,128)}, u32[]{:S(2)}) copy-start(f32[1,640]{1,0:T(1,128)} %broadcast_in_dim.24) | copy-start | bytes 7684
  1576.5 147.5 %reduce-scatter.22.cloned.1.call-start = ((), (), s32[]{:S(2)}) async-start(), calls=%async_computation.24 | async-start | bytes 2949120 | tf_op jit(solution)/shard_map/reduce_scatter | solution.py:325
  1583.6 213.7 %reduce-scatter.18.cloned.1.call-start = ((), (), s32[]{:S(2)}) async-start(), calls=%async_computation.22 | async-start | bytes 2949120 | tf_op jit(solution)/shard_map/reduce_scatter | solution.py:307
  1592.1 278.5 %reduce-scatter.20.cloned.1.call-start = ((), (), s32[]{:S(2)}) async-start(), calls=%async_computation.23 | async-start | bytes 2949120 | tf_op jit(solution)/shard_map/reduce_scatter | solution.py:310
  1607.8 5.6 collective-permute-start.1
  1621.6 294.9 %reduce-scatter.16.cloned.1.call-start = ((), (), s32[]{:S(2)}) async-start(), calls=%async_computation.21 | async-start | bytes 5242880 | tf_op jit(solution)/shard_map/reduce_scatter | solution.py:288
  1725.8 193.1 %copy-start.14 = (bf16[256,2048]{1,0:T(8,128)(2,1)S(1)}, bf16[256,2048]{1,0:T(8,128)(2,1)}, u32[]{:S(2)}) copy-start(bf16[256,2048]{1,0:T(8,128)(2,1)} %reduce-scatter.14.cloned.1.call-done) | copy-start | bytes 3145732
  1725.8 193.1 %copy-start.16 = (bf16[256,2048]{1,0:T(8,128)(2,1)S(1)}, bf16[256,2048]{1,0:T(8,128)(2,1)}, u32[]{:S(2)}) copy-start(bf16[256,2048]{1,0:T(8,128)(2,1)} %param.20) | copy-start | bytes 3145732
  1725.8 193.1 %copy-start.43 = (f32[8,1,256]{2,1,0:T(1,128)S(1)}, f32[8,1,256]{2,1,0:T(1,128)}, u32[]{:S(2)}) copy-start(f32[8,1,256]{2,1,0:T(1,128)} %copy-done.42) | copy-start | bytes 24580
  1725.8 193.1 %copy-start.109 = (f32[256]{0:T(256)S(1)}, f32[256]{0:T(256)}, u32[]{:S(2)}) copy-start(f32[256]{0:T(256)} %copy-done.108) | copy-start | bytes 3076
  1725.8 193.1 %copy-start.111 = (f32[256]{0:T(256)S(1)}, f32[256]{0:T(256)}, u32[]{:S(2)}) copy-start(f32[256]{0:T(256)} %copy-done.110) | copy-start | bytes 3076
  (99 other events, 699.4 us)
Sparse Core Ops, SparseCore 0:
  9.6 37.1 all-gather.16
  49.0 57.2 all-gather.18
  108.5 56.0 all-gather.20
  166.5 56.0 all-gather.22
  481.6 150.0 all-reduce.93
  633.6 99.1 all-gather.24
  735.0 97.1 all-gather.26
  833.8 32.6 all-gather.30
  868.6 99.9 all-gather.28
  1006.5 42.6 reduce-scatter.13
  1055.8 34.4 all-gather.32
  1092.8 44.5 reduce-scatter.11
  1141.0 117.9 reduce-scatter.23
  1262.4 117.0 reduce-scatter.25
  1382.9 117.6 reduce-scatter.27
  1576.6 73.2 all-reduce.95
  1653.7 70.2 reduce-scatter.21
  1727.7 69.5 reduce-scatter.17
  1801.2 69.3 reduce-scatter.19
  1873.1 43.3 reduce-scatter.15
where the time goes:
time: 1950 us; the launch traced here: 1930 us
  waiting for transfers between devices  691 us (35%)
  local copies, waits for them, and re-layouts  530 us (27%)
  blocking collectives  318 us (16%)
  matrix products  190 us (10%)
  other arithmetic  177 us (9%)
    slice x73, local copies, waits for them, and re-layouts, shards(): lax.associative_scan(pair_join, (jnp.flip(next_decay, 0), jnp.flip(grad_d...  202 us
    psum x1, waiting for transfers between devices, shards(): hidden_one = residual + lax.psum(mixer_part, 'tensor')  131 us
    slice x68, local copies, waits for them, and re-layouts, shards(): lax.associative_scan(pair_join, (carry_decay, norm_root * admit_gate * co...  130 us
    all_gather x4, blocking collectives, entering(): pieces = jax.tree.map(lambda part: lax.all_gather(part, axis), value)  122 us
    all_gather x1, waiting for transfers between devices, shards(): lax.all_gather(feed_down, 'dp', axis=1, tiled=True)  102 us
    all_gather x1, waiting for transfers between devices, shards(): lax.all_gather(feed_up, 'dp', axis=0, tiled=True)  87.5 us
    all_gather x1, waiting for transfers between devices, shards(): lax.all_gather(feed_gate, 'dp', axis=0, tiled=True)  86.3 us
    reduce_scatter x1, waiting for transfers between devices, shards(): lax.psum_scatter(gate_grad.astype(jnp.bfloat16), 'dp', scatter_dimension=...  71.5 us
  transfers between devices with their start and end apart: 22, of which 11 were waited for; matrix products, arithmetic and copies ran while one was open for 43% of the time, Pallas kernels for 0%

commit v1 on v0

v1 whole, which is shorter than its diff:
```python
import functools

import jax
import jax.numpy as jnp
from jax import lax
from jax.experimental import pallas as pl
from jax.experimental.pallas import tpu as pltpu
from jax.sharding import PartitionSpec as P

TAPS = 4
EPSILON = 1e-06
GUARD = 0.001
GELU_SCALE = 0.7978845608028654
GELU_CUBE = 0.044715
MESH = pl.DeviceIdType.MESH
F32, BF16 = jnp.float32, jnp.bfloat16
ANY = pl.BlockSpec(memory_space=pl.ANY)
VMEM = pl.BlockSpec(memory_space=pltpu.VMEM)
GRANT = 60 * 1024 * 1024
NT = (((1,), (1,)), ((), ()))
TN = (((0,), (0,)), ((), ()))
CHUNK = 256


def spot():
    dp, tensor = lax.axis_index("dp"), lax.axis_index("tensor")
    return dp // 2, dp % 2, tensor // 2, tensor % 2


def seat(line, side, deck, core):
    return (line * 2 + side, deck * 2 + core)


def rank(side, deck, core):
    return side * 4 + deck * 2 + core


def greet(peers):
    barrier = pltpu.get_barrier_semaphore()
    for peer in peers:
        pl.semaphore_signal(barrier, inc=1, device_id=peer, device_id_type=MESH)
    pl.semaphore_wait(barrier, len(peers))


def remote(source, target, send, receive, peer):
    return pltpu.make_async_remote_copy(
        src_ref=source,
        dst_ref=target,
        send_sem=send,
        recv_sem=receive,
        device_id=peer,
        device_id_type=MESH,
    )


def line_peers(count):
    line, side, deck, core = spot()
    return [seat((line + k) % count, side, deck, core) for k in range(1, count)]


def group_peers():
    line, side, deck, core = spot()
    return [
        seat(line, side, deck, 1 - core),
        seat(line, 1 - side, deck, core),
        seat(line, side, 1 - deck, core),
    ]


PIECES = 2


class LineGather:
    def __init__(self, count, source, target, sems):
        self.count, self.source, self.target = count, source, target
        self.send, self.receive, self.local = sems
        self.here = spot()

    @staticmethod
    def scratch(count):
        steps = 5 if count == 4 else count - 1
        return [
            pltpu.SemaphoreType.DMA((steps, PIECES)),
            pltpu.SemaphoreType.DMA((count, PIECES)),
            pltpu.SemaphoreType.DMA,
        ]

    def part(self, ref, piece):
        rows = self.source.shape[0] // PIECES
        return ref.at[pl.ds(piece * rows, rows)]

    def copy(self, origin, place, index, piece, source):
        line, side, deck, core = self.here
        return remote(
            source,
            self.part(self.target.at[origin], piece),
            self.send.at[index, piece],
            self.receive.at[origin, piece],
            seat(place, side, deck, core),
        )

    def own(self, place, index, piece):
        return self.copy(self.here[0], place, index, piece, self.part(self.source, piece))

    def arrival(self, origin, piece):
        return self.copy(origin, origin, 0, piece, self.part(self.source, piece))

    def keep(self):
        return pltpu.make_async_copy(self.source, self.target.at[self.here[0]], self.local)

    def steps(self):
        if self.count == 4:
            return [1, -1, 2, -2]
        return list(range(1, self.count))

    def guarded(self, index, step, action):
        line = self.here[0]
        if self.count == 4:
            place = line + step

            @pl.when((place >= 0) & (place < self.count))
            def _():
                action(place)

        else:
            action((line + step) % self.count)

    def start(self):
        for piece in range(PIECES):
            for index, step in enumerate(self.steps()):
                self.guarded(
                    index, step, lambda place, i=index, p=piece: self.own(place, i, p).start()
                )
        self.keep().start()

    def middle(self, action):
        line = self.here[0]
        if self.count == 4:

            @pl.when((line == 1) | (line == 2))
            def _():
                action(6 - 3 * line, 3 * line - 3)

    def onward(self, origin, place, piece):
        return self.copy(origin, place, 4, piece, self.part(self.target.at[origin], piece))

    def forward(self):
        for piece in range(PIECES):

            def action(origin, place, piece=piece):
                self.arrival(origin, piece).wait_recv()
                self.onward(origin, place, piece).start()

            self.middle(action)

    def finish(self):
        line = self.here[0]
        for piece in range(PIECES):
            for index, step in enumerate(self.steps()):
                self.guarded(
                    index, step, lambda place, i=index, p=piece: self.own(place, i, p).wait_send()
                )
            self.middle(
                lambda origin, place, p=piece: self.onward(origin, place, p).wait_send()
            )
            for origin in range(self.count):
                pending = line != origin
                if self.count == 4 and origin == 0:
                    pending = pending & (line != 2)
                if self.count == 4 and origin == 3:
                    pending = pending & (line != 1)

                @pl.when(pending)
                def _(origin=origin, piece=piece):
                    self.arrival(origin, piece).wait_recv()

        self.keep().wait()


def call(kernel, outs, ins, scratch, identity, name):
    results = pl.pallas_call(
        kernel,
        out_shape=[jax.ShapeDtypeStruct(shape, kind) for shape, kind, _ in outs],
        in_specs=[space for _, space in ins],
        out_specs=[space for _, _, space in outs],
        scratch_shapes=scratch,
        compiler_params=pltpu.CompilerParams(
            collective_id=identity, has_side_effects=True, vmem_limit_bytes=GRANT
        ),
        name=name,
    )(*[value for value, _ in ins])
    return list(results)


def spread_kernel(count, halves, small, pair, everyone, send, receive, local):
    dp, tensor = lax.axis_index("dp"), lax.axis_index("tensor")
    line, side, deck, core = spot()
    greet([((dp + k) % count, tensor) for k in range(1, count)])
    copies = [
        remote(
            small,
            everyone.at[dp],
            send.at[k],
            receive.at[k],
            ((dp + k) % count, tensor),
        )
        for k in range(1, count)
    ]
    copies.append(
        remote(
            halves.at[1 - side],
            pair.at[side],
            send.at[0],
            receive.at[0],
            seat(line, 1 - side, deck, core),
        )
    )
    copies.append(pltpu.make_async_copy(small, everyone.at[dp], local.at[0]))
    copies.append(pltpu.make_async_copy(halves.at[side], pair.at[side], local.at[1]))
    for copy in copies:
        copy.start()
    for copy in copies:
        copy.wait()


def spread(count, halves, small):
    return call(
        functools.partial(spread_kernel, count),
        [(halves.shape, BF16, ANY), ((count,) + small.shape, BF16, ANY)],
        [(halves, ANY), (small, ANY)],
        [
            pltpu.SemaphoreType.DMA((count,)),
            pltpu.SemaphoreType.DMA((count,)),
            pltpu.SemaphoreType.DMA((2,)),
        ],
        0,
        "spread",
    )


class GroupGather:
    def __init__(self, source, target, send, receive, local):
        self.source, self.target = source, target
        self.send, self.receive = send, receive
        self.local = local
        self.here = spot()

    @staticmethod
    def scratch():
        return [
            pltpu.SemaphoreType.DMA((11,)),
            pltpu.SemaphoreType.DMA((11,)),
            pltpu.SemaphoreType.DMA,
        ]

    def half(self, ref, h):
        rows = self.source.shape[0] // 2
        return ref.at[pl.ds(h * rows, rows)]

    def make(self):
        line, side, deck, core = self.here
        sibling, across, above = group_peers()
        mine = rank(side, deck, core)
        beside = rank(1 - side, deck, core)
        over = rank(side, 1 - deck, core)
        corner = rank(1 - side, 1 - deck, core)

        def own(h, peer, index):
            return remote(
                self.half(self.source, h),
                self.half(self.target.at[mine], h),
                self.send.at[index],
                self.receive.at[index],
                peer,
            )

        def relay(block, h, peer, index):
            ref = self.half(self.target.at[block], h)
            return remote(ref, ref, self.send.at[index], self.receive.at[index], peer)

        self.keep = pltpu.make_async_copy(self.source, self.target.at[mine], self.local)
        self.first = [
            own(0, across, 0),
            own(1, above, 1),
            own(0, above, 2),
            own(1, across, 3),
        ]
        self.near = remote(
            self.source, self.target.at[mine], self.send.at[4], self.receive.at[4], sibling
        )
        self.second = [relay(beside, 0, above, 5), relay(over, 1, across, 6)]
        self.last = [
            relay(beside, 0, sibling, 7),
            relay(over, 1, sibling, 8),
            relay(over, 0, sibling, 9),
            relay(beside, 1, sibling, 10),
        ]
        self.corner = corner

    def start(self):
        self.make()
        for copy in self.first:
            copy.start()
        self.near.start()
        self.keep.start()

    def forward(self):
        for k in range(2):
            self.first[k].wait_recv()
            self.second[k].start()
            self.last[k].start()
        for k in range(2, 4):
            self.first[k].wait_recv()
            self.last[k].start()


def corner_relay(gather, send, receive):
    sibling = group_peers()[0]
    out = []
    for h in range(2):
        ref = gather.half(gather.target.at[gather.corner], h)
        out.append(remote(ref, ref, send.at[h], receive.at[h], sibling))
    return out


def group_finish(gather, send, receive):
    relays = corner_relay(gather, send, receive)
    for k in range(2):
        gather.second[k].wait_recv()
        relays[k].start()
    gather.keep.wait()
    gather.near.wait()
    for copy in gather.first:
        copy.wait_send()
    for copy in gather.second:
        copy.wait_send()
    for copy in gather.last:
        copy.wait()
    for copy in relays:
        copy.wait()


def rows_scratch():
    return GroupGather.scratch() + [
        pltpu.SemaphoreType.DMA((2,)),
        pltpu.SemaphoreType.DMA((2,)),
    ]


def rows_kernel(count, swaps, *refs):
    rows, block = refs[0], refs[1]
    halves = refs[2 : 2 + swaps]
    outs = refs[2 + swaps : 4 + swaps + swaps]
    sems = refs[4 + swaps + swaps :]
    everything, blocks = outs[:2]
    pairs = outs[2:]
    gather = GroupGather(rows, everything, *sems[:3])
    corner = sems[3:5]
    freight = LineGather(count, block, blocks, sems[5:8])
    line, side, deck, core = spot()
    greet(group_peers() + line_peers(count))
    gather.start()
    freight.start()
    moves = []
    if swaps:
        send, receive, local = sems[8:]
        for k in range(swaps):
            moves.append(
                remote(
                    halves[k].at[1 - side],
                    pairs[k].at[side],
                    send.at[k],
                    receive.at[k],
                    seat(line, 1 - side, deck, core),
                )
            )
            moves.append(
                pltpu.make_async_copy(halves[k].at[side], pairs[k].at[side], local.at[k])
            )
        for move in moves:
            move.start()
    gather.forward()
    freight.forward()
    group_finish(gather, *corner)
    for move in moves:
        move.wait()
    freight.finish()


def gather_rows(count, rows, block, identity, halves=()):
    scratch = rows_scratch() + LineGather.scratch(count)
    if halves:
        scratch += [pltpu.SemaphoreType.DMA((len(halves),))] * 3
    out = call(
        functools.partial(rows_kernel, count, len(halves)),
        [((8,) + rows.shape, BF16, ANY), ((count,) + block.shape, BF16, ANY)]
        + [(half.shape, BF16, ANY) for half in halves],
        [(rows, ANY), (block, ANY)] + [(half, ANY) for half in halves],
        scratch,
        identity,
        "gather_rows",
    )
    full = out[0].reshape(-1, rows.shape[1])
    line = out[1].reshape(-1, block.shape[1])
    return [full, line] + [pair.reshape(-1, pair.shape[2]) for pair in out[2:]]


def plain_rows_kernel(rows, everything, *sems):
    gather = GroupGather(rows, everything, *sems[:3])
    greet(group_peers())
    gather.start()
    gather.forward()
    group_finish(gather, *sems[3:5])


def gather_plain(rows, identity):
    out = call(
        plain_rows_kernel,
        [((8,) + rows.shape, BF16, ANY)],
        [(rows, ANY)],
        rows_scratch(),
        identity,
        "gather_rows",
    )
    return out[0].reshape(-1, rows.shape[1])


def fold_kernel(count, pairs, cargo, *refs):
    lefts, rights = refs[:pairs], refs[pairs : 2 * pairs]
    refs = refs[2 * pairs :]
    block = None
    if cargo:
        block, refs = refs[0], refs[1:]
    out, refs = refs[0], refs[1:]
    if cargo:
        blocks, refs = refs[0], refs[1:]
    mine, stage, near, leaving, arriving, refs = *refs[:5], refs[5:]
    send, receive, near_send, near_receive = refs[:4]
    line, side, deck, core = spot()
    sibling, across, above = group_peers()
    if cargo:
        freight = LineGather(count, block, blocks, refs[4:])
        greet(group_peers() + line_peers(count))
        freight.start()
    else:
        greet(group_peers())
    rows = out.shape[0]
    half = rows // 2
    width = out.shape[1]
    step = 512

    def product(which, store):
        base = pl.multiple_of(which * rows, rows)

        def body(j, carry):
            columns = pl.ds(pl.multiple_of(j * step, step), step)
            total = None
            for left, right in zip(lefts, rights):
                part = lax.dot_general(
                    left[pl.ds(base, rows), :],
                    right[columns, :],
                    NT,
                    preferred_element_type=F32,
                )
                total = part if total is None else total + part
            store(columns, total)
            return carry

        lax.fori_loop(0, width // step, body, 0)

    def sweep(action):
        def body(i, carry):
            action(pl.multiple_of(i * 16, 16))
            return carry

        lax.fori_loop(0, half // 16, body, 0)

    def chip_sum(q, h, r):
        place = pl.ds(h * half + r, 16)
        return mine[q, place, :] + near[q, place, :].astype(F32)

    def ship(index, peer):
        return remote(
            leaving.at[index], arriving.at[index], send.at[index], receive.at[index], peer
        )

    ships = [ship(k, peer) for k, peer in enumerate((above, across, above, across, across, above))]
    OWN, ACROSS, ABOVE, CORNER = 0, 1, 2, 3
    seats = {
        CORNER: (1 - side, 1 - deck),
        ABOVE: (side, 1 - deck),
        ACROSS: (1 - side, deck),
        OWN: (side, deck),
    }
    nears = []
    for q in (CORNER, ABOVE, ACROSS, OWN):
        s, d = seats[q]

        def put_stage(columns, total, q=q):
            stage[q, :, columns] = total.astype(BF16)

        def put_mine(columns, total, q=q):
            mine[q, :, columns] = total

        product(rank(s, d, 1 - core), put_stage)
        copy = remote(stage.at[q], near.at[q], near_send.at[q], near_receive.at[q], sibling)
        copy.start()
        nears.append(copy)
        product(rank(s, d, core), put_mine)
        copy.wait_recv()
        if q == CORNER:

            def corner_sum(r):
                for h in range(2):
                    leaving[h, pl.ds(r, 16), :] = chip_sum(CORNER, h, r).astype(BF16)

            sweep(corner_sum)
            ships[0].start()
            ships[1].start()
        if q == ABOVE:

            def above_sum(r):
                leaving[2, pl.ds(r, 16), :] = chip_sum(ABOVE, 0, r).astype(BF16)

            sweep(above_sum)
            ships[2].start()
        if q == ACROSS:

            def across_sum(r):
                leaving[3, pl.ds(r, 16), :] = chip_sum(ACROSS, 1, r).astype(BF16)

            sweep(across_sum)
            ships[3].start()
    if cargo:
        freight.forward()
    ships[0].wait_recv()

    def pass_across(r):
        total = chip_sum(ACROSS, 0, r) + arriving[0, pl.ds(r, 16), :].astype(F32)
        leaving[4, pl.ds(r, 16), :] = total.astype(BF16)

    sweep(pass_across)
    ships[4].start()
    ships[1].wait_recv()

    def pass_above(r):
        total = chip_sum(ABOVE, 1, r) + arriving[1, pl.ds(r, 16), :].astype(F32)
        leaving[5, pl.ds(r, 16), :] = total.astype(BF16)

    sweep(pass_above)
    ships[5].start()
    for k in range(2, 6):
        ships[k].wait_recv()

    def finish(r):
        place = pl.ds(r, 16)
        first = arriving[2, place, :].astype(F32) + arriving[4, place, :].astype(F32)
        out[place, :] = chip_sum(OWN, 0, r) + first
        second = arriving[3, place, :].astype(F32) + arriving[5, place, :].astype(F32)
        out[pl.ds(half + r, 16), :] = chip_sum(OWN, 1, r) + second

    sweep(finish)
    for k in range(6):
        ships[k].wait_send()
    for copy in nears:
        copy.wait_send()
    if cargo:
        freight.finish()


def fold(count, lefts, rights, identity, block=None):
    rows, width = lefts[0].shape[0] // 8, rights[0].shape[0]
    outs = [((rows, width), F32, VMEM)]
    ins = [(value, VMEM) for value in list(lefts) + list(rights)]
    scratch = [
        pltpu.VMEM((4, rows, width), F32),
        pltpu.VMEM((4, rows, width), BF16),
        pltpu.VMEM((4, rows, width), BF16),
        pltpu.VMEM((6, rows // 2, width), BF16),
        pltpu.VMEM((6, rows // 2, width), BF16),
        pltpu.SemaphoreType.DMA((6,)),
        pltpu.SemaphoreType.DMA((6,)),
        pltpu.SemaphoreType.DMA((4,)),
        pltpu.SemaphoreType.DMA((4,)),
    ]
    if block is not None:
        outs.append(((count,) + block.shape, BF16, ANY))
        ins.append((block, ANY))
        scratch += LineGather.scratch(count)
    out = call(
        functools.partial(fold_kernel, count, len(lefts), block is not None),
        outs,
        ins,
        scratch,
        identity,
        "fold",
    )
    if block is not None:
        return out[0], out[1].reshape(-1, block.shape[1])
    return out[0]


def gelu_both(value):
    square = value * value
    bend = jnp.tanh(GELU_SCALE * value * (1.0 + GELU_CUBE * square))
    act = 0.5 * value * (1.0 + bend)
    slope = 0.5 * (1.0 + bend) + 0.5 * value * (1.0 - bend * bend) * GELU_SCALE * (
        1.0 + 3.0 * GELU_CUBE * square
    )
    return act, slope


def chunks(rows, action, size=CHUNK):
    def body(i, carry):
        action(pl.multiple_of(i * size, size))
        return carry

    lax.fori_loop(0, rows // size, body, 0)


def tile_scan(mults, adds, rows, width, backward):
    place = lax.broadcasted_iota(jnp.int32, (8, width), 0)

    def inside(base):
        where = pl.ds(base, 8)
        a, b = mults[where, :], adds[where, :]
        for k in (1, 2, 4):
            if backward:
                away, mask = pltpu.roll(a, 8 - k, 0), place < 8 - k
                back = pltpu.roll(b, 8 - k, 0)
            else:
                away, mask = pltpu.roll(a, k, 0), place >= k
                back = pltpu.roll(b, k, 0)
            b = jnp.where(mask, b + a * back, b)
            a = jnp.where(mask, a * away, a)
        return where, a, b

    unroll = 4
    tiles = rows // 8

    def body(i, carry):
        prod, total = carry
        work = []
        for u in range(unroll):
            index = i * unroll + u
            if backward:
                index = tiles - 1 - index
            work.append(inside(pl.multiple_of(index * 8, 8)))
        for where, a, b in work:
            edge = 0 if backward else 7
            adds[where, :] = b + a * total
            mults[where, :] = a * prod
            whole = jnp.broadcast_to(a[edge : edge + 1, :], (8, width))
            extra = jnp.broadcast_to(b[edge : edge + 1, :], (8, width))
            total = extra + whole * total
            prod = whole * prod
        return prod, total

    return lax.fori_loop(
        0, tiles // unroll, body, (jnp.ones((8, width), F32), jnp.zeros((8, width), F32))
    )


def pool(count, prod, total, outgoing, slots, send, receive, backward):
    line, side, deck, core = spot()
    outgoing[0:8, :] = prod
    outgoing[8:16, :] = total
    slots[line, 0:8, :] = prod
    slots[line, 8:16, :] = total
    copies = []
    for k in range(1, count):
        copy = remote(
            outgoing,
            slots.at[line],
            send.at[k],
            receive.at[k],
            seat((line + k) % count, side, deck, core),
        )
        copy.start()
        copies.append(copy)
    for copy in copies:
        copy.wait()
    entering = jnp.zeros_like(prod)
    order = range(count - 1, -1, -1) if backward else range(count)
    for place in order:
        longer = slots[place, 8:16, :] + slots[place, 0:8, :] * entering
        before = (line < place) if backward else (line > place)
        entering = jnp.where(before, longer, entering)
    return entering


def gates(values, soft):
    recur = values
    low = -8.0 * recur * soft
    decay = jnp.exp(low)
    root = jnp.sqrt((1.0 + GUARD) - decay * decay)
    return decay, root


def scan_kernel(
    count,
    pre,
    masks,
    table,
    gate_weights,
    block,
    conv,
    recur_out,
    admit_out,
    state,
    merged,
    entry,
    blocks,
    prods,
    sums,
    halo,
    outgoing,
    slots,
    edge_sems,
    send,
    receive,
    *sems,
):
    line, side, deck, core = spot()
    rows, width = conv.shape
    freight = LineGather(count, block, blocks, sems)
    greet(line_peers(count))

    def edge(place):
        return remote(
            pre.at[pl.ds(rows - 8, 8), pl.ds(width, width)],
            halo,
            edge_sems.at[0],
            edge_sems.at[1],
            seat(place, side, deck, core),
        )

    @pl.when(line < count - 1)
    def _():
        edge(line + 1).start()

    freight.start()

    def copy_entry(r):
        entry[pl.ds(r + 8, CHUNK), :] = pre[pl.ds(r, CHUNK), width:]

    chunks(rows, copy_entry)

    @pl.when(line > 0)
    def _():
        edge(line - 1).wait_recv()
        entry[0:8, :] = halo[...]

    @pl.when(line == 0)
    def _():
        entry[0:8, :] = jnp.zeros((8, width), F32)

    @pl.when(line < count - 1)
    def _():
        edge(line + 1).wait_send()

    def gate_chunk(r):
        wide = entry[pl.ds(r, CHUNK + 8), :]
        mask = masks[pl.ds(r, CHUNK), :]
        value = table[0:1, :] * wide[8:, :]
        for k in range(1, TAPS):
            value = (
                value + table[k : k + 1, :] * wide[8 - k : 8 - k + CHUNK, :] * mask[:, k - 1 : k]
            )
        where = pl.ds(r, CHUNK)
        conv[where, :] = value
        both = jnp.dot(value.astype(BF16), gate_weights[...], preferred_element_type=F32)
        recur = jax.nn.sigmoid(both[:, :width])
        admit = jax.nn.sigmoid(both[:, width:])
        recur_out[where, :] = recur
        admit_out[where, :] = admit
        decay, root = gates(recur, table[4:5, :])
        opened = mask[:, 3:4]
        norm = root * opened + (1.0 - opened)
        prods[where, :] = decay * opened
        sums[where, :] = norm * admit * value

    chunks(rows, gate_chunk)
    prod, total = tile_scan(prods, sums, rows, width, False)
    entering = pool(count, prod, total, outgoing, slots, send, receive, False)
    state[0:8, :] = entering

    def state_chunk(r):
        where = pl.ds(r, CHUNK)
        value = sums[where, :] + prods[where, :] * entering[0:1, :]
        state[pl.ds(r + 8, CHUNK), :] = value
        act, _ = gelu_both(pre[where, :width])
        merged[where, :] = (value * act).astype(BF16)

    chunks(rows, state_chunk)
    freight.forward()
    freight.finish()


def scan_forward(count, pre, masks, table, gate_weights, block):
    rows, width = pre.shape[0], pre.shape[1] // 2
    out = call(
        functools.partial(scan_kernel, count),
        [
            ((rows, width), F32, VMEM),
            ((rows, width), F32, VMEM),
            ((rows, width), F32, VMEM),
            ((rows + 8, width), F32, VMEM),
            ((rows, width), BF16, VMEM),
            ((rows + 8, width), F32, VMEM),
            ((count,) + block.shape, BF16, ANY),
        ],
        [(pre, VMEM), (masks, VMEM), (table, VMEM), (gate_weights, VMEM), (block, ANY)],
        [
            pltpu.VMEM((rows, width), F32),
            pltpu.VMEM((rows, width), F32),
            pltpu.VMEM((8, width), F32),
            pltpu.VMEM((16, width), F32),
            pltpu.VMEM((count, 16, width), F32),
            pltpu.SemaphoreType.DMA((2,)),
            pltpu.SemaphoreType.DMA((count,)),
            pltpu.SemaphoreType.DMA((count,)),
        ]
        + LineGather.scratch(count),
        2,
        "scan_forward",
    )
    return out[:-1] + [out[-1].reshape(-1, block.shape[1])]


def back_kernel(
    count,
    pre,
    grad_merged,
    conv,
    recur_in,
    admit_in,
    state,
    entry,
    masks,
    table,
    gate_weights,
    grad_pre,
    grad_gates,
    grad_table,
    prods,
    sums,
    mixes,
    outgoing,
    slots,
    edge_sems,
    send,
    receive,
):
    line, side, deck, core = spot()
    rows, width = conv.shape
    greet(line_peers(count))

    def direct_chunk(r):
        where = pl.ds(r, CHUNK)
        act, slope = gelu_both(pre[where, :width])
        grad = grad_merged[where, :]
        grad_pre[where, :width] = (grad * state[pl.ds(r + 8, CHUNK), :] * slope).astype(BF16)
        direct = grad * act
        decay, _ = gates(recur_in[where, :], table[4:5, :])
        carry = decay * masks[where, 3:4]
        mixes[where, :] = direct
        prods[where, :] = carry
        sums[where, :] = carry * direct

    chunks(rows, direct_chunk)
    prods[rows : rows + 8, :] = jnp.ones((8, width), F32)
    sums[rows : rows + 8, :] = jnp.zeros((8, width), F32)
    prod, total = tile_scan(prods, sums, rows, width, True)
    entering = pool(count, prod, total, outgoing, slots, send, receive, True)
    grad_gates[...] = jnp.zeros_like(grad_gates)
    grad_table[...] = jnp.zeros_like(grad_table)

    def fold_rows(value):
        return jnp.sum(value, axis=0, keepdims=True)

    def gate_chunk(r):
        where = pl.ds(r, CHUNK)
        wide = pl.ds(r, CHUNK + 8)
        later = sums[wide, :] + prods[wide, :] * entering[0:1, :]
        grad = mixes[where, :] + later[1 : CHUNK + 1, :]
        before = state[wide, :][7 : CHUNK + 7, :]
        soft = table[4:5, :]
        recur, admit, value = recur_in[where, :], admit_in[where, :], conv[where, :]
        decay, root = gates(recur, soft)
        opened = masks[where, 3:4]
        norm = root * opened + (1.0 - opened)
        flow = grad * admit
        grad_log = opened * (grad * before * decay - flow * value * decay * decay / root)
        grad_table[4:5, :] += fold_rows(grad_log * (-8.0 * recur))
        grad_rate = (grad_log * (-8.0 * soft) * recur * (1.0 - recur)).astype(BF16)
        grad_inlet = (flow * norm * value * (1.0 - admit)).astype(BF16)
        both = jnp.concatenate([grad_rate, grad_inlet], axis=1)
        grad_gates[...] += lax.dot_general(
            value.astype(BF16), both, TN, preferred_element_type=F32
        )
        mixes[where, :] = flow * norm + lax.dot_general(
            both, gate_weights[...], NT, preferred_element_type=F32
        )

    gate_chunk(0)

    def edge(place):
        return remote(
            mixes.at[pl.ds(0, 8)],
            mixes.at[pl.ds(rows, 8)],
            edge_sems.at[0],
            edge_sems.at[1],
            seat(place, side, deck, core),
        )

    @pl.when(line > 0)
    def _():
        edge(line - 1).start()

    def other(i, carry):
        gate_chunk(pl.multiple_of(i * CHUNK, CHUNK))
        return carry

    lax.fori_loop(1, rows // CHUNK, other, 0)

    @pl.when(line < count - 1)
    def _():
        edge(line + 1).wait_recv()

    @pl.when(line == count - 1)
    def _():
        mixes[rows : rows + 8, :] = jnp.zeros((8, width), F32)

    def entry_chunk(r):
        where, wide = pl.ds(r, CHUNK), pl.ds(r, CHUNK + 8)
        ahead, mask = mixes[wide, :], masks[where, :]
        source = entry[wide, :]
        here = ahead[:CHUNK, :]
        total = table[0:1, :] * here
        grad_table[0:1, :] += fold_rows(here * source[8:, :])
        for k in range(1, TAPS):
            total = total + table[k : k + 1, :] * ahead[k : k + CHUNK, :] * mask[:, 3 + k : 4 + k]
            grad_table[k : k + 1, :] += fold_rows(
                here * source[8 - k : 8 - k + CHUNK, :] * mask[:, k - 1 : k]
            )
        grad_pre[where, width:] = total.astype(BF16)

    chunks(rows, entry_chunk)

    @pl.when(line > 0)
    def _():
        edge(line - 1).wait_send()


def scan_backward(count, pre, grad_merged, saved, masks, table, gate_weights):
    rows, width = grad_merged.shape
    values = [pre, grad_merged, *saved, masks, table, gate_weights]
    return call(
        functools.partial(back_kernel, count),
        [
            ((rows, 2 * width), BF16, VMEM),
            ((width, 2 * width), F32, VMEM),
            ((8, width), F32, VMEM),
        ],
        [(value, VMEM) for value in values],
        [
            pltpu.VMEM((rows + 8, width), F32),
            pltpu.VMEM((rows + 8, width), F32),
            pltpu.VMEM((rows + 8, width), F32),
            pltpu.VMEM((16, width), F32),
            pltpu.VMEM((count, 16, width), F32),
            pltpu.SemaphoreType.DMA((2,)),
            pltpu.SemaphoreType.DMA((count,)),
            pltpu.SemaphoreType.DMA((count,)),
        ],
        7,
        "scan_backward",
    )


def doc_index(places, doc_starts):
    return jnp.sum((doc_starts[None, :] <= places[:, None]).astype(jnp.int32), axis=1)


def norm_back(grad_unit, unit_rows, scale_rows):
    return scale_rows * (
        grad_unit - unit_rows * jnp.mean(grad_unit * unit_rows, axis=1, keepdims=True)
    )


def unit_norm(values):
    scale = lax.rsqrt(jnp.mean(values * values, axis=1, keepdims=True) + EPSILON)
    return values * scale, scale


def split_columns(value):
    rows, columns = value.shape
    return value.reshape(rows, 2, columns // 2).transpose(1, 0, 2)


def widen(value, width):
    return jnp.pad(value, [(0, 0)] * (value.ndim - 1) + [(0, width - value.shape[-1])])


def by_rows(left, right):
    return lax.dot_general(left, right, TN, preferred_element_type=F32).astype(BF16)


def shards(
    layer_input,
    out_grad,
    doc_starts,
    mixer_gain,
    branch_gate,
    branch_input,
    conv_taps,
    rate_gate,
    input_gate,
    decay_param,
    mixer_out,
    feed_gain,
    feed_gate,
    feed_up,
    feed_down,
):
    shares = lax.axis_size("dp")
    count = shares // 2
    side = lax.axis_index("dp") % 2
    slim, feature_count = mixer_gain.shape[0], layer_input.shape[1]
    heads, piece, head_width = rate_gate.shape
    half_heads = heads // 2
    lanes = half_heads * head_width
    width = -(-lanes // 128) * 128
    row_count = layer_input.shape[0]
    rows = row_count * 8
    line_groups = [[2 * k + s for k in range(count)] for s in range(2)]

    branch_halves = jnp.concatenate(
        [split_columns(branch_gate), split_columns(branch_input)], axis=2
    )
    mixer_halves = widen(split_columns(mixer_out.T), width)
    gate_halves, up_halves = split_columns(feed_gate), split_columns(feed_up)
    down_halves = split_columns(feed_down.T)
    flat = jnp.concatenate(
        [
            mixer_gain,
            feed_gain,
            rate_gate.reshape(-1),
            input_gate.reshape(-1),
            conv_taps.reshape(-1),
            decay_param.reshape(-1),
        ]
    )
    small_rows = -(-flat.shape[0] // (128 * 16)) * 16
    small = jnp.pad(flat, (0, small_rows * 128 - flat.shape[0])).reshape(small_rows, 128)
    branch_pair, small_all = spread(shares, branch_halves, small)

    small_all = small_all.reshape(shares, -1)
    cuts = [slim, slim, rate_gate.size, input_gate.size, conv_taps.size, decay_param.size]
    parts, start = [], 0
    for size in cuts:
        parts.append(small_all[:, start : start + size])
        start += size
    gain_first = parts[0].reshape(feature_count).astype(F32)
    gain_second = parts[1].reshape(feature_count).astype(F32)

    def own_heads(value, axis):
        return lax.dynamic_slice_in_dim(value, side * half_heads, half_heads, axis)

    rate_weights, inlet_weights = [
        own_heads(
            part.reshape(shares, heads, piece, head_width)
            .transpose(1, 0, 2, 3)
            .reshape(heads, shares * piece, head_width),
            0,
        )
        for part in parts[2:4]
    ]
    taps = own_heads(
        parts[4].reshape(shares, TAPS, heads, piece).transpose(1, 2, 0, 3), 1
    ).reshape(TAPS, lanes)
    decay_flat = own_heads(
        parts[5].reshape(shares, heads, piece).transpose(1, 0, 2), 0
    ).reshape(lanes).astype(F32)
    table = widen(
        jnp.concatenate(
            [
                taps.astype(F32),
                jax.nn.softplus(-decay_flat)[None],
                jnp.zeros((3, lanes), F32),
            ]
        ),
        width,
    )

    def diagonal(blocks):
        bands = [
            jnp.pad(
                blocks[h],
                ((0, 0), (h * head_width, width - (h + 1) * head_width)),
            )
            for h in range(half_heads)
        ]
        return jnp.pad(jnp.concatenate(bands, axis=0), ((0, width - lanes), (0, 0)))

    gate_weights = jnp.concatenate([diagonal(rate_weights), diagonal(inlet_weights)], axis=1)

    anchor = lax.axis_index("dp") // 2 * rows
    places = anchor + jnp.arange(rows, dtype=jnp.int32)
    here = doc_index(places, doc_starts)
    columns = [doc_index(places - k, doc_starts) == here for k in range(1, TAPS)]
    columns.append(~jnp.any(doc_starts[None, :] == places[:, None], axis=1))
    columns += [doc_index(places + k, doc_starts) == here for k in range(1, TAPS)]
    columns.append(columns[0])
    masks = jnp.stack(columns, axis=1).astype(F32)

    residual = layer_input.astype(F32)
    unit_one, scale_one = unit_norm(residual)
    normed_own = (unit_one * gain_first).astype(BF16)
    normed_one, branch_all, mixer_pair, gate_pair, up_pair, down_pair = gather_rows(
        count,
        normed_own,
        branch_pair.reshape(-1, 2 * lanes),
        1,
        (mixer_halves, gate_halves, up_halves, down_halves),
    )
    branch_wide = jnp.concatenate(
        [widen(branch_all[:, :lanes], width), widen(branch_all[:, lanes:], width)], axis=1
    )
    pre = jnp.dot(normed_one, branch_wide, preferred_element_type=F32)
    conv, recur, admit, state, merged, entry, mixer_all = scan_forward(
        count, pre, masks, table, gate_weights, mixer_pair
    )
    mixer_own, gating_weights = fold(count, [merged], [mixer_all], 3, gate_pair)
    hidden_one = residual + mixer_own
    unit_two, scale_two = unit_norm(hidden_one)
    normed_two, lifting_weights = gather_rows(
        count, (unit_two * gain_second).astype(BF16), up_pair, 4
    )
    cot_all, lowering_weights = gather_rows(count, out_grad, down_pair, 5)

    gating_pre = jnp.dot(normed_two, gating_weights, preferred_element_type=F32)
    lifting_pre = jnp.dot(normed_two, lifting_weights, preferred_element_type=F32)
    gating_act, gating_slope = gelu_both(gating_pre)
    hidden = (gating_act * lifting_pre).astype(BF16)

    def line_sum(value):
        return lax.psum_scatter(
            value, "dp", scatter_dimension=0, axis_index_groups=line_groups, tiled=True
        )

    down_sum = line_sum(by_rows(cot_all, hidden))
    grad_hidden = lax.dot_general(cot_all, lowering_weights, (((1,), (0,)), ((), ())), preferred_element_type=F32)
    grad_gating = (grad_hidden * lifting_pre * gating_slope).astype(BF16)
    grad_lifting = (grad_hidden * gating_act).astype(BF16)
    gate_sum = line_sum(by_rows(normed_two, grad_gating))
    up_sum = line_sum(by_rows(normed_two, grad_lifting))
    grad_normed_two = fold(
        count, [grad_gating, grad_lifting], [gating_weights, lifting_weights], 6
    )
    grad_hidden_one = out_grad.astype(F32) + norm_back(
        grad_normed_two * gain_second, unit_two, scale_two
    )
    back_low = gather_plain(grad_hidden_one.astype(BF16), 8)
    outlet_sum = line_sum(by_rows(back_low, merged))
    grad_merged = jnp.dot(back_low, mixer_all, preferred_element_type=F32)
    grad_pre, grad_gates, grad_table = scan_backward(
        count, pre, grad_merged, [conv, recur, admit, state, entry], masks, table, gate_weights
    )
    branch_grads = by_rows(normed_one, grad_pre)
    branch_sum = line_sum(
        jnp.concatenate([branch_grads[:, :lanes], branch_grads[:, width : width + lanes]], axis=1)
    )
    feed_own = fold(count, [hidden], [lowering_weights], 9)
    layer_output = (hidden_one + feed_own).astype(BF16)
    grad_normed_one = fold(count, [grad_pre], [branch_wide], 10)
    input_grad = (
        grad_hidden_one + norm_back(grad_normed_one * gain_first, unit_one, scale_one)
    ).astype(BF16)

    gains = jnp.stack(
        [jnp.sum(grad_normed_one * unit_one, axis=0), jnp.sum(grad_normed_two * unit_two, axis=0)]
    )
    gains = lax.psum(gains, ("dp", "tensor"))
    gains = lax.dynamic_slice_in_dim(gains, lax.axis_index("dp") * slim, slim, 1)

    def spots(value):
        blocks = [
            value[
                h * head_width : (h + 1) * head_width, h * head_width : (h + 1) * head_width
            ].reshape(shares, -1)
            for h in range(half_heads)
        ]
        return jnp.concatenate(blocks, axis=1)

    grad_decay = -jax.nn.sigmoid(-decay_flat) * grad_table[4, :lanes]
    grad_small = jnp.concatenate(
        [
            spots(grad_gates[:, :width]),
            spots(grad_gates[:, width:]),
            grad_table[:TAPS, :lanes]
            .reshape(TAPS * half_heads, shares, piece)
            .transpose(1, 0, 2)
            .reshape(shares, -1),
            grad_decay.reshape(half_heads, shares, piece).transpose(1, 0, 2).reshape(shares, -1),
        ],
        axis=1,
    )
    flat_size = grad_small.shape[1]
    small_rows = -(-flat_size // (128 * 16)) * 16
    grad_small = widen(grad_small, small_rows * 128).reshape(shares * small_rows, 128)
    small_sum = line_sum(grad_small.astype(BF16)).astype(F32)

    def swap(value):
        pair = value.reshape(2, -1, value.shape[1])
        kept = lax.dynamic_index_in_dim(pair, side, 0, False)
        given = lax.dynamic_index_in_dim(pair, 1 - side, 0, False)
        other = lax.ppermute(given, "dp", [(k, k ^ 1) for k in range(shares)])
        first = jnp.where(side == 0, kept, other).astype(F32)
        second = jnp.where(side == 0, other, kept).astype(F32)
        return first, second

    def joined(value):
        return jnp.concatenate(swap(value), axis=1)

    branch_first, branch_second = swap(branch_sum)
    branch_gate_grad = jnp.concatenate([branch_first[:, :lanes], branch_second[:, :lanes]], axis=1)
    branch_input_grad = jnp.concatenate([branch_first[:, lanes:], branch_second[:, lanes:]], axis=1)
    outlet_first, outlet_second = swap(outlet_sum)
    mixer_out_grad = jnp.concatenate([outlet_first[:, :lanes], outlet_second[:, :lanes]], axis=1).T

    smalls = [value.reshape(-1)[:flat_size] for value in swap(small_sum.astype(BF16))]
    one = half_heads * piece * head_width
    tap_size = TAPS * half_heads * piece
    rate_grad = jnp.concatenate([v[:one].reshape(half_heads, piece, head_width) for v in smalls])
    inlet_grad = jnp.concatenate(
        [v[one : 2 * one].reshape(half_heads, piece, head_width) for v in smalls]
    )
    taps_grad = jnp.concatenate(
        [v[2 * one : 2 * one + tap_size].reshape(TAPS, half_heads, piece) for v in smalls], axis=1
    )
    decay_grad = jnp.concatenate(
        [v[2 * one + tap_size :].reshape(half_heads, piece) for v in smalls]
    )
    return (
        layer_output,
        input_grad,
        gains[0],
        branch_gate_grad,
        branch_input_grad,
        taps_grad,
        rate_grad,
        inlet_grad,
        decay_grad,
        mixer_out_grad,
        gains[1],
        joined(gate_sum),
        joined(up_sum),
        joined(down_sum).T,
    )


def solution(mesh):
    placed = (
        P(("dp", "tensor"), None),
        P(("dp", "tensor"), None),
        P(),
        P("dp"),
        P("dp", "tensor"),
        P("dp", "tensor"),
        P(None, "tensor", "dp"),
        P("tensor", "dp", None),
        P("tensor", "dp", None),
        P("tensor", "dp"),
        P("tensor", "dp"),
        P("dp"),
        P("dp", "tensor"),
        P("dp", "tensor"),
        P("tensor", "dp"),
    )
    return jax.shard_map(
        shards,
        mesh=mesh,
        in_specs=placed,
        out_specs=(
            P(("dp", "tensor"), None),
            P(("dp", "tensor"), None),
            P("dp"),
            P("dp", "tensor"),
            P("dp", "tensor"),
            P(None, "tensor", "dp"),
            P("tensor", "dp", None),
            P("tensor", "dp", None),
            P("tensor", "dp"),
            P("tensor", "dp"),
            P("dp"),
            P("dp", "tensor"),
            P("dp", "tensor"),
            P("tensor", "dp"),
        ),
        check_vma=False,
    )
```

time: 1950 us -> 906 us (0.46)
  waiting for transfers between devices: 691 us -> 77.8 us
  Pallas kernels: 0 us -> 559 us
  local copies, waits for them, and re-layouts: 530 us -> 44.3 us
  blocking collectives: 318 us -> 41.1 us
  other arithmetic: 177 us -> 37.5 us
  matrix products: 190 us -> 113 us
    pallas_call x0 -> x11, Pallas kernels: none -> 559 us  [call(): pl.pallas_call(kernel, out_shape=[jax.ShapeDtypeStruct(shape, kind) for s...]
    slice x150 -> x18, local copies, waits for them, and re-layouts: 337 us -> 5.98 us  [the longest x1 2.33 us: shards(): branch_all[:, lanes:]]
    all_gather x9 -> x0, waiting for transfers between devices: 299 us -> none  [the longest x1 102 us: shards(): lax.all_gather(feed_down, 'dp', axis=1, tiled=True)]
    all_gather x10 -> x0, blocking collectives: 271 us -> none  [the longest x4 122 us: entering(): pieces = jax.tree.map(lambda part: lax.all_gather(part, axis), value)]
    reduce_scatter x9 -> x6, waiting for transfers between devices: 252 us -> 63 us  [line_sum(): lax.psum_scatter(value, 'dp', scatter_dimension=0, axis_index_groups=line...]
    psum x1 -> x0, waiting for transfers between devices: 131 us -> none  [shards(): hidden_one = residual + lax.psum(mixer_part, 'tensor')]
    pad x72 -> x3, local copies, waits for them, and re-layouts: 107 us -> 2.35 us  [widen(): jnp.pad(value, [(0, 0)] * (value.ndim - 1) + [(0, width - value.shape[-1])])]
    dot_general x24 -> x10, matrix products: 190 us -> 113 us  [the longest x5 53.9 us: by_rows(): lax.dot_general(left, right, TN, preferred_element_type=F32).astype(BF16)]
  transfers between devices with their start and end apart: 22 -> 12, of which waited for: 11 -> 5; matrix products, arithmetic and copies ran while one was open for 43% -> 10% of each run, Pallas kernels for 0% -> 10%
where the time goes in v1:
time: 906 us; the launch traced here: 897 us
  Pallas kernels  559 us (62%)
  matrix products  113 us (12%)
  waiting for transfers between devices  77.8 us (9%)
  local copies, waits for them, and re-layouts  44.3 us (5%)
  blocking collectives  41.1 us (5%)
  other arithmetic  37.5 us (4%)
  between operations  15.5 us (2%)
  starting transfers between devices  9.21 us (1%)
    pallas_call x11, Pallas kernels, call(): pl.pallas_call(kernel, out_shape=[jax.ShapeDtypeStruct(shape, kind) for s...  559 us
    reduce_scatter x6, waiting for transfers between devices, line_sum(): lax.psum_scatter(value, 'dp', scatter_dimension=0, axis_index_groups=line...  63 us
    dot_general x5, matrix products, by_rows(): lax.dot_general(left, right, TN, preferred_element_type=F32).astype(BF16)  53.9 us
    psum x1, blocking collectives, shards(): gains = lax.psum(gains, ('dp', 'tensor'))  41.1 us
    dot_general x1, matrix products, shards(): lax.dot_general(cot_all, lowering_weights, (((1,), (0,)), ((), ())), pref...  18.5 us
  transfers between devices with their start and end apart: 12, of which 5 were waited for; matrix products, arithmetic and copies ran while one was open for 10% of the time, Pallas kernels for 10%

profile of v1, /device:TPU:0, one launch (start us, length us, event | category | flops | bytes accessed | tf_op | source)
XLA Modules:
  0.0 897.5 jit_solution(8216509034336321219)
XLA Ops:
  13.9 19.0 %spread.1 = (bf16[2,256,640]{2,1,0:T(8,128)(2,1)}, bf16[8,208,128]{2,1,0:T(8,128)(2,1)}) custom-call(bf16[2,256,640]{2,1,0:T(8,128)(2,1)} %pad_maximum_fusion.1.halves, bf16[208,128]{1,0:T(8,128)(2,1)} %pad_bitcast_fusion.small), custom_call_target="tpu_custom_call" | custom-call | tf_op jit(solution)/shard_map/spread/pallas_call | solution.py:181
  41.4 1.4 copy.162
  45.3 1.3 fusion.6.refs_0_
  47.4 96.5 %gather_rows.4 = (bf16[8,256,2048]{2,1,0:T(8,128)(2,1)}, bf16[4,512,640]{2,1,0:T(8,128)(2,1)}, bf16[2,256,384]{2,1,0:T(8,128)(2,1)}, bf16[2,256,768]{2,1,0:T(8,1...) custom-call(bf16[256,2048]{1,0:T(8,128)(2,1)} %fusion.6.refs_0_, bf16[512,640]{1,0:T(8,128)(2,1)} %bitcast.182, ...), custom_call_target="tpu_custom_call" | custom-call | tf_op jit(solution)/shard_map/gather_rows/pallas_call | solution.py:181
  143.9 2.3 slice.174
  147.7 10.7 %fusion.42.pre = f32[2048,768]{1,0:T(8,128)} fusion(bf16[2048,2048]{1,0:T(8,128)(2,1)} %bitcast.213, bf16[2048,320]{1,0:T(8,128)(2,1)S(1)} %slice.174, bf16[2048,384]{1,0:T(8,128)(2,1)S(1)} %slice_select_fusion), kind=kOutput, calls=%fused_computation.138 | convolution fusion | flops 6451888128 | bytes 17563648 | tf_op jit(solution)/shard_map/dot_general | solution.py:1131
  158.5 49.5 %scan_forward.1 = (f32[2048,384]{1,0:T(8,128)}, f32[2048,384]{1,0:T(8,128)}, f32[2048,384]{1,0:T(8,128)}, f32[2056,384]{1,0:T(8,128)}, bf16[2048,384]{1,0:T(8,12...) custom-call(f32[2048,768]{1,0:T(8,128)} %fusion.42.pre, f32[2048,8]{1,0:T(8,128)} %convert_element_type.169.masks, ...), custom_call_target="tpu_custom_call" | custom-call | tf_op jit(solution)/shard_map/scan_forward/pallas_call | solution.py:181
  208.0 58.2 %fold.4 = (f32[256,2048]{1,0:T(8,128)}, bf16[4,512,768]{2,1,0:T(8,128)(2,1)}) custom-call(bf16[2048,384]{1,0:T(8,128)(2,1)} %get-tuple-element.43.refs_0_, bf16[2048,384]{1,0:T(8,128)(2,1)} %bitcast.165, bf16[512,768]{1,0:T(8,128)(2,1)} %bitcast.180), custom_call_target="tpu_custom_call" | custom-call | tf_op jit(solution)/shard_map/fold/pallas_call | solution.py:181
  266.2 1.9 multiply_reduce_fusion.2
  268.2 1.2 multiply_convert_fusion.3.refs_0_
  269.4 58.9 %gather_rows.5 = (bf16[8,256,2048]{2,1,0:T(8,128)(2,1)}, bf16[4,512,768]{2,1,0:T(8,128)(2,1)}) custom-call(bf16[256,2048]{1,0:T(8,128)(2,1)} %multiply_convert_fusion.3.refs_0_, bf16[512,768]{1,0:T(8,128)(2,1)} %bitcast.175), custom_call_target="tpu_custom_call" | custom-call | tf_op jit(solution)/shard_map/gather_rows/pallas_call | solution.py:181
  328.3 11.9 %fusion.54 = f32[2048,768]{1,0:T(8,128)} fusion(bf16[2048,2048]{1,0:T(8,128)(2,1)} %bitcast.215, bf16[2048,768]{1,0:T(8,128)(2,1)} %bitcast.150), kind=kOutput, calls=%fused_computation.149 | convolution fusion | flops 6442450944 | bytes 17825792 | tf_op jit(solution)/shard_map/dot_general | solution.py:1144
  340.2 8.5 fusion.53
  348.7 59.1 %gather_rows.6 = (bf16[8,256,2048]{2,1,0:T(8,128)(2,1)}, bf16[4,512,768]{2,1,0:T(8,128)(2,1)}) custom-call(bf16[256,2048]{1,0:T(8,128)(2,1)} %refs_0_.1, bf16[512,768]{1,0:T(8,128)(2,1)} %bitcast.174), custom_call_target="tpu_custom_call" | custom-call | tf_op jit(solution)/shard_map/gather_rows/pallas_call | solution.py:181
  407.8 18.5 %multiply_convert_fusion = (bf16[2048,768]{1,0:T(8,128)(2,1)}, bf16[2048,768]{1,0:T(8,128)(2,1)}, bf16[2048,768]{1,0:T(8,128)(2,1)}) fusion(f32[2048,768]{1,0:T(8,128)} %fusion.53, f32[2048,768]{1,0:T(8,128)} %fusion.54, bf16[2048,2048]{1,0:T(8,128)(2,1)} %bitcast.219, bf16[2048,768]{1,0:T(8,128)(2,1)} %bitcast.154), kind=kOutput, calls=%fused_computation.1 | convolution fusion | flops 6480199680 | bytes 33554432 | tf_op jit(solution)/shard_map/dot_general | solution.py:1154
  426.3 49.4 %fold.6 = f32[256,2048]{1,0:T(8,128)} custom-call(bf16[2048,768]{1,0:T(8,128)(2,1)} %get-tuple-element.146.refs_0_, bf16[2048,768]{1,0:T(8,128)(2,1)} %get-tuple-element.145.refs_1_, bf16[2048,768]{1,0:T(8,128)(2,1)} %bitcast.148, bf16[2048,768]{1,0:T(8,128)(2,1)} %bitcast.151), custom_call_target="tpu_custom_call" | custom-call | tf_op jit(solution)/shard_map/fold/pallas_call | solution.py:181
  475.8 2.3 multiply_reduce_fusion
  478.2 1.6 fusion.41.rows
  479.9 39.4 %gather_rows.7 = bf16[8,256,2048]{2,1,0:T(8,128)(2,1)} custom-call(bf16[256,2048]{1,0:T(8,128)(2,1)} %fusion.41.rows), custom_call_target="tpu_custom_call" | custom-call | tf_op jit(solution)/shard_map/gather_rows/pallas_call | solution.py:181
  519.3 10.0 %fusion.55.grad_merged = f32[2048,384]{1,0:T(8,128)} fusion(bf16[2048,2048]{1,0:T(8,128)(2,1)} %bitcast.144, bf16[2048,384]{1,0:T(8,128)(2,1)} %bitcast.166), kind=kOutput, calls=%fused_computation.150 | convolution fusion | flops 3221225472 | bytes 13107200 | tf_op jit(solution)/shard_map/dot_general | solution.py:1167
  529.3 37.1 %scan_backward.1 = (bf16[2048,768]{1,0:T(8,128)(2,1)}, f32[384,768]{1,0:T(8,128)}, f32[8,384]{1,0:T(8,128)}) custom-call(f32[2048,768]{1,0:T(8,128)} %fusion.42.pre, f32[2048,384]{1,0:T(8,128)} %fusion.55.grad_merged, f32[2048,384]{1,0:T(8,128)} %get-tuple-element.54.conv, f32[2048,384]{1,0:T(8,128)} %get-tuple-element.55.recur_in, ...), custom_call_target="tpu_custom_call" | custom-call | tf_op jit(solution)/shard_map/scan_backward/pallas_call | solution.py:181
  568.5 1.3 convert.40
  570.8 1.5 concatenate.76
  574.2 9.5 %convolution_convert_fusion.4 = bf16[2048,384]{1,0:T(8,128)(2,1)} fusion(bf16[2048,2048]{1,0:T(8,128)(2,1)} %bitcast.145, bf16[2048,384]{1,0:T(8,128)(2,1)} %get-tuple-element.43.refs_0_), kind=kOutput, calls=%fused_computation.19 | convolution fusion | flops 3222011904 | bytes 11534336 | tf_op jit(solution)/shard_map/dot_general | solution.py:1007
  583.8 10.2 %convolution_convert_fusion.3 = bf16[2048,768]{0,1:T(8,128)(2,1)S(1)} fusion(bf16[2048,2048]{1,0:T(8,128)(2,1)} %bitcast.214, bf16[2048,768]{1,0:T(8,128)(2,1)} %get-tuple-element.59.refs_0_), kind=kOutput, calls=%fused_computation.10 | convolution fusion | flops 6444023808 | bytes 14680064 | tf_op jit(solution)/shard_map/dot_general | solution.py:1007
  594.2 1.9 pad_maximum_fusion
  596.1 11.4 %convolution_convert_fusion.1 = bf16[2048,768]{1,0:T(8,128)(2,1)} fusion(bf16[2048,2048]{1,0:T(8,128)(2,1)} %bitcast.216, bf16[2048,768]{1,0:T(8,128)(2,1)} %get-tuple-element.145.refs_1_), kind=kOutput, calls=%fused_computation.8 | convolution fusion | flops 6444023808 | bytes 14680064 | tf_op jit(solution)/shard_map/dot_general | solution.py:1007
  607.8 11.4 %convolution_convert_fusion = bf16[2048,768]{1,0:T(8,128)(2,1)} fusion(bf16[2048,2048]{1,0:T(8,128)(2,1)} %bitcast.220, bf16[2048,768]{1,0:T(8,128)(2,1)} %get-tuple-element.147.refs_0_), kind=kOutput, calls=%fused_computation.7 | convolution fusion | flops 6444023808 | bytes 14680064 | tf_op jit(solution)/shard_map/dot_general | solution.py:1007
  619.3 11.4 %convolution_convert_fusion.2 = bf16[2048,768]{1,0:T(8,128)(2,1)} fusion(bf16[2048,2048]{1,0:T(8,128)(2,1)} %bitcast.217, bf16[2048,768]{1,0:T(8,128)(2,1)} %get-tuple-element.146.refs_0_), kind=kOutput, calls=%fused_computation.9 | convolution fusion | flops 6444023808 | bytes 14680064 | tf_op jit(solution)/shard_map/dot_general | solution.py:1007
  630.7 45.4 %fold.5 = f32[256,2048]{1,0:T(8,128)} custom-call(bf16[2048,768]{1,0:T(8,128)(2,1)} %get-tuple-element.147.refs_0_, bf16[2048,768]{1,0:T(8,128)(2,1)} %bitcast.155), custom_call_target="tpu_custom_call" | custom-call | tf_op jit(solution)/shard_map/fold/pallas_call | solution.py:181
  676.1 4.0 fusion.1.refs_1_
  680.1 46.1 %fold.7 = f32[256,2048]{1,0:T(8,128)} custom-call(bf16[2048,768]{1,0:T(8,128)(2,1)} %get-tuple-element.59.refs_0_, bf16[2048,768]{1,0:T(8,128)(2,1)} %fusion.1.refs_1_), custom_call_target="tpu_custom_call" | custom-call | tf_op jit(solution)/shard_map/fold/pallas_call | solution.py:181
  726.2 2.2 fusion.12
  728.5 41.1 %psum.7 = f32[2,2048]{1,0:T(2,128)S(1)} all-reduce(f32[2,2048]{1,0:T(2,128)S(1)} %pad_maximum_fusion.6), channel_id=1, replica_groups=mesh['dp'=8,'tensor'=4] {'dp','tensor'}, use_global_device_ids=true, to_apply=%region_14.15 | all-reduce | flops 4096 | bytes 32768 | tf_op jit(solution)/shard_map/psum | solution.py:1185
  769.6 5.6 fusion.11
  776.0 2.3 collective-permute-start.1
  783.6 2.1 collective-permute-start.2
  787.8 2.0 reshape.430
  789.8 1.4 constant_dynamic-slice_fusion.12
  793.9 5.3 collective-permute-done
  804.1 3.6 reduce-scatter.17.cloned.1.call-done
  809.1 1.5 collective-permute-start.5
  811.0 59.3 %reduce-scatter.13.cloned.1.call-done = bf16[512,768]{1,0:T(8,128)(2,1)} async-done(((bf16[2048,768]{1,0:T(8,128)(2,1)}), bf16[512,768]{1,0:T(8,128)(2,1)}) %reduce-scatter.13.cloned.1.call-update) | async-done | bytes 786448 | tf_op jit(solution)/shard_map/reduce_scatter | solution.py:1149
  872.4 1.5 collective-permute-start.3
  875.3 8.2 collective-permute-done.3
  884.5 1.6 copy.187
  886.3 1.6 copy.186
  888.9 1.3 convert_bitcast_fusion
  (206 shorter events, 48.5 us)
Async XLA Ops:
  7.2 4.7 copy-start.14
  7.2 4.8 copy-start.20
  7.2 4.9 copy-start.16
  7.2 4.9 copy-start.17
  7.2 768.0 %reduce-scatter.9.cloned.1.call-start = ((), (), s32[]{:S(2)}) async-start(), calls=%async_computation.7 | async-start | bytes 286720 | tf_op jit(solution)/shard_map/reduce_scatter | solution.py:1149
  32.8 3.4 copy-start.15
  34.6 4.9 copy-start.1
  35.3 4.6 copy-start.7
  39.6 5.7 copy-start.10
  39.9 5.4 copy-start.12
  40.2 3.7 copy-start.8
  40.2 4.9 copy-start.9
  47.4 98.8 %copy-start.18 = (pred[384]{0:T(512)(128)(4,1)S(1)}, pred[384]{0:T(512)(128)(4,1)}, u32[]{:S(2)}) copy-start(pred[384]{0:T(512)(128)(4,1)} %constant.93.clone.1) | copy-start | bytes 1156
  143.9 2.4 copy-start.5
  146.2 12.3 %copy-start.3 = (bf16[2048,320]{1,0:T(8,128)(2,1)}, bf16[2048,320]{1,0:T(8,128)(2,1)S(1)}, u32[]{:S(2)}) copy-start(bf16[2048,320]{1,0:T(8,128)(2,1)S(1)} %slice.174) | copy-start | bytes 3932164
  146.4 12.1 %copy-start.4 = (bf16[2048,384]{1,0:T(8,128)(2,1)}, bf16[2048,384]{1,0:T(8,128)(2,1)S(1)}, u32[]{:S(2)}) copy-start(bf16[2048,384]{1,0:T(8,128)(2,1)S(1)} %slice_select_fusion) | copy-start | bytes 4718596
  328.3 11.9 %copy-start.6 = (bf16[4,512,768]{2,1,0:T(8,128)(2,1)S(1)}, bf16[4,512,768]{2,1,0:T(8,128)(2,1)}, u32[]{:S(2)}) copy-start(bf16[4,512,768]{2,1,0:T(8,128)(2,1)} %get-tuple-element.49) | copy-start | bytes 9437188
  328.3 11.9 %copy-start.19 = (bf16[8,256,2048]{2,1,0:T(8,128)(2,1)S(1)}, bf16[8,256,2048]{2,1,0:T(8,128)(2,1)}, u32[]{:S(2)}) copy-start(bf16[8,256,2048]{2,1,0:T(8,128)(2,1)} %get-tuple-element.48) | copy-start | bytes 25165828
  475.8 2.4 copy-start
  475.8 2.5 copy-start.2
  574.0 208.4 %reduce-scatter.11.cloned.1.call-start = ((), (), s32[]{:S(2)}) async-start(), calls=%async_computation.8 | async-start | bytes 1966080 | tf_op jit(solution)/shard_map/reduce_scatter | solution.py:1149
  583.7 204.0 %reduce-scatter.7.cloned.1.call-start = ((), (), s32[]{:S(2)}) async-start(), calls=%async_computation.6 | async-start | bytes 3276800 | tf_op jit(solution)/shard_map/reduce_scatter | solution.py:1149
  596.1 204.6 %reduce-scatter.15.cloned.1.call-start = ((), (), s32[]{:S(2)}) async-start(), calls=%async_computation.10 | async-start | bytes 3932160 | tf_op jit(solution)/shard_map/reduce_scatter | solution.py:1149
  607.6 200.2 %reduce-scatter.17.cloned.1.call-start = ((), (), s32[]{:S(2)}) async-start(), calls=%async_computation.11 | async-start | bytes 3932160 | tf_op jit(solution)/shard_map/reduce_scatter | solution.py:1149
  619.2 251.1 %reduce-scatter.13.cloned.1.call-start = ((), (), s32[]{:S(2)}) async-start(), calls=%async_computation.9 | async-start | bytes 3932160 | tf_op jit(solution)/shard_map/reduce_scatter | solution.py:1149
  680.1 46.1 %copy-start.11 = (f32[1,2,8,128]{3,1,2,0:T(2,128)S(1)}, f32[1,2,8,128]{3,1,2,0:T(2,128)}, u32[]{:S(2)}) copy-start(f32[1,2,8,128]{3,1,2,0:T(2,128)} %copy-done.10) | copy-start | bytes 24580
  680.1 46.1 %copy-start.13 = (f32[256]{0:T(256)S(1)}, f32[256]{0:T(256)}, u32[]{:S(2)}) copy-start(f32[256]{0:T(256)} %copy-done.12) | copy-start | bytes 3076
  776.0 4.1 collective-permute-start.1
  783.6 8.6 collective-permute-start.2
  792.1 7.1 collective-permute-start
  802.0 72.1 %collective-permute-start.4 = (bf16[256,768]{0,1:T(8,128)(2,1)S(1)}, bf16[256,768]{0,1:T(8,128)(2,1)}, u32[]{:S(2)}, u32[]{:S(2)}) collective-permute-start(bf16[256,768]{0,1:T(8,128)(2,1)S(1)} %bitcast.187), channel_id=1, source_target_pairs={{0,4},{4,0},{8,12},{12,8},{16,20},{20,16},{24,28},{28,24},{1,5},{5... | collective-permute-start | bytes 1179656 | tf_op jit(solution)/shard_map/ppermute | solution.py:1219
  809.1 78.8 %collective-permute-start.5 = (bf16[256,768]{0,1:T(8,128)(2,1)S(1)}, bf16[256,768]{0,1:T(8,128)(2,1)}, u32[]{:S(2)}, u32[]{:S(2)}) collective-permute-start(bf16[256,768]{0,1:T(8,128)(2,1)S(1)} %bitcast.186), channel_id=1, source_target_pairs={{0,4},{4,0},{8,12},{12,8},{16,20},{20,16},{24,28},{28,24},{1,5},{5... | collective-permute-start | bytes 1179656 | tf_op jit(solution)/shard_map/ppermute | solution.py:1219
  872.4 11.0 %collective-permute-start.3 = (bf16[256,768]{0,1:T(8,128)(2,1)}, bf16[256,768]{0,1:T(8,128)(2,1)}, u32[]{:S(2)}, u32[]{:S(2)}) collective-permute-start(bf16[256,768]{0,1:T(8,128)(2,1)} %bitcast.59), channel_id=1, source_target_pairs={{0,4},{4,0},{8,12},{12,8},{16,20},{20,16},{24,28},{28,24},{1,5},{5... | collective-permute-start | bytes 1179656 | tf_op jit(solution)/shard_map/ppermute | solution.py:1219
Sparse Core Ops, SparseCore 0:
  574.1 18.4 reduce-scatter.8
  595.6 33.5 reduce-scatter.10
  631.6 51.1 reduce-scatter.6
  685.0 59.9 reduce-scatter.14
  747.2 60.5 reduce-scatter.16
  810.0 60.2 reduce-scatter.12

commit v2 on v1

--- a/solution.py
+++ b/solution.py
@@ -67,114 +67,178 @@
     ]
 
 
-PIECES = 2
-
-
-class LineGather:
-    def __init__(self, count, source, target, sems):
-        self.count, self.source, self.target = count, source, target
-        self.send, self.receive, self.local = sems
-        self.here = spot()
+class Freight:
+    def __init__(self, count, halves, target, sems, start=0):
+        self.count, self.halves, self.target = count, halves, target
+        self.start_column = start
+        self.cross, self.local, self.send, self.receive = sems
+        self.line, self.side, self.deck, self.core = spot()
 
     @staticmethod
     def scratch(count):
         steps = 5 if count == 4 else count - 1
         return [
-            pltpu.SemaphoreType.DMA((steps, PIECES)),
-            pltpu.SemaphoreType.DMA((count, PIECES)),
+            pltpu.SemaphoreType.DMA((2,)),
             pltpu.SemaphoreType.DMA,
+            pltpu.SemaphoreType.DMA((steps, 2)),
+            pltpu.SemaphoreType.DMA((count, 2)),
         ]
 
-    def part(self, ref, piece):
-        rows = self.source.shape[0] // PIECES
-        return ref.at[pl.ds(piece * rows, rows)]
-
-    def copy(self, origin, place, index, piece, source):
-        line, side, deck, core = self.here
+    def half(self, which):
+        if len(self.halves.shape) == 3:
+            return self.halves.at[which]
+        offset = which * (self.halves.shape[1] // 2) + self.start_column
+        return self.halves.at[:, pl.ds(pl.multiple_of(offset, 128), self.target.shape[2])]
+
+    def place(self, origin, part):
+        rows = self.target.shape[1] // 2
+        return self.target.at[origin, pl.ds(pl.multiple_of(part * rows, rows), rows)]
+
+    def seat(self, line):
+        return seat(line, self.side, self.deck, self.core)
+
+    def swap(self):
+        return remote(
+            self.half(1 - self.side),
+            self.place(self.line, self.side),
+            self.cross.at[0],
+            self.cross.at[1],
+            seat(self.line, 1 - self.side, self.deck, self.core),
+        )
+
+    def keep(self):
+        return pltpu.make_async_copy(
+            self.half(self.side), self.place(self.line, self.side), self.local
+        )
+
+    def copy(self, origin, line, index, part, source):
         return remote(
             source,
-            self.part(self.target.at[origin], piece),
-            self.send.at[index, piece],
-            self.receive.at[origin, piece],
-            seat(place, side, deck, core),
+            self.place(origin, part),
+            self.send.at[index, part],
+            self.receive.at[origin, part],
+            self.seat(line),
         )
 
-    def own(self, place, index, piece):
-        return self.copy(self.here[0], place, index, piece, self.part(self.source, piece))
-
-    def arrival(self, origin, piece):
-        return self.copy(origin, origin, 0, piece, self.part(self.source, piece))
-
-    def keep(self):
-        return pltpu.make_async_copy(self.source, self.target.at[self.here[0]], self.local)
-
-    def steps(self):
+    def own(self, line, index, part):
+        source = self.half(self.side)
+        if part is not self.side:
+            source = self.place(self.line, part)
+        return self.copy(self.line, line, index, part, source)
+
+    def arrival(self, origin, part):
+        return self.copy(origin, origin, 0, part, self.half(self.side))
+
+    def each_step(self, action, phases=(0, 1)):
         if self.count == 4:
-            return [1, -1, 2, -2]
-        return list(range(1, self.count))
-
-    def guarded(self, index, step, action):
-        line = self.here[0]
+            line = self.line
+            for index, step in enumerate((1, -1, 2, -2)):
+                if index == 0:
+                    when = [line == 2, line < 2]
+                elif index == 1:
+                    when = [line == 1, line > 1]
+                else:
+                    when = [(line + step >= 0) & (line + step < 4), None]
+                for phase in phases:
+                    if when[phase] is not None:
+
+                        @pl.when(when[phase])
+                        def _(index=index, step=step):
+                            action(index, line + step)
+
+        elif 0 in phases:
+            for step in range(1, self.count):
+                action(step - 1, (self.line + step) % self.count)
+
+    def start(self):
+        self.swap().start()
+        self.each_step(lambda index, line: self.own(line, index, self.side).start(), (0,))
+        self.keep().start()
+
+    def second(self):
+        self.swap().wait_recv()
+        self.each_step(lambda index, line: self.own(line, index, 1 - self.side).start(), (0,))
+
+    def middle(self, action):
         if self.count == 4:
-            place = line + step
-
-            @pl.when((place >= 0) & (place < self.count))
+
+            @pl.when((self.line == 1) | (self.line == 2))
             def _():
-                action(place)
-
-        else:
-            action((line + step) % self.count)
-
-    def start(self):
-        for piece in range(PIECES):
-            for index, step in enumerate(self.steps()):
-                self.guarded(
-                    index, step, lambda place, i=index, p=piece: self.own(place, i, p).start()
-                )
-        self.keep().start()
-
-    def middle(self, action):
-        line = self.here[0]
-        if self.count == 4:
-
-            @pl.when((line == 1) | (line == 2))
-            def _():
-                action(6 - 3 * line, 3 * line - 3)
-
-    def onward(self, origin, place, piece):
-        return self.copy(origin, place, 4, piece, self.part(self.target.at[origin], piece))
+                action(6 - 3 * self.line, 3 * self.line - 3)
+
+    def onward(self, origin, line, part):
+        return self.copy(origin, line, 4, part, self.place(origin, part))
 
     def forward(self):
-        for piece in range(PIECES):
-
-            def action(origin, place, piece=piece):
-                self.arrival(origin, piece).wait_recv()
-                self.onward(origin, place, piece).start()
+        for part in (self.side, 1 - self.side):
+            self.each_step(
+                lambda index, line, part=part: self.own(line, index, part).start(), (1,)
+            )
+
+            def action(origin, line, part=part):
+                self.arrival(origin, part).wait_recv()
+                self.onward(origin, line, part).start()
 
             self.middle(action)
 
     def finish(self):
-        line = self.here[0]
-        for piece in range(PIECES):
-            for index, step in enumerate(self.steps()):
-                self.guarded(
-                    index, step, lambda place, i=index, p=piece: self.own(place, i, p).wait_send()
-                )
+        for part in (self.side, 1 - self.side):
+            self.each_step(
+                lambda index, line, part=part: self.own(line, index, part).wait_send()
+            )
             self.middle(
-                lambda origin, place, p=piece: self.onward(origin, place, p).wait_send()
+                lambda origin, line, part=part: self.onward(origin, line, part).wait_send()
             )
             for origin in range(self.count):
-                pending = line != origin
+                pending = self.line != origin
                 if self.count == 4 and origin == 0:
-                    pending = pending & (line != 2)
+                    pending = pending & (self.line != 2)
                 if self.count == 4 and origin == 3:
-                    pending = pending & (line != 1)
+                    pending = pending & (self.line != 1)
 
                 @pl.when(pending)
-                def _(origin=origin, piece=piece):
-                    self.arrival(origin, piece).wait_recv()
+                def _(origin=origin, part=part):
+                    self.arrival(origin, part).wait_recv()
 
         self.keep().wait()
+        self.swap().wait_send()
+
+
+def cargo_peers(count):
+    return group_peers() + line_peers(count)
+
+
+def piece_shape(count, piece):
+    if isinstance(piece, tuple):
+        return count, 2 * piece[0].shape[0], piece[2]
+    return count, 2 * piece.shape[1], piece.shape[2]
+
+
+def cargo_outs(count, cargo):
+    return [(piece_shape(count, piece), BF16, ANY) for piece in cargo]
+
+
+def cargo_ins(cargo):
+    return [(piece[0] if isinstance(piece, tuple) else piece, ANY) for piece in cargo]
+
+
+def cargo_starts(cargo):
+    return [piece[1] if isinstance(piece, tuple) else 0 for piece in cargo]
+
+
+def cargo_scratch(count, cargo):
+    return [sem for _ in cargo for sem in Freight.scratch(count)]
+
+
+def load(count, starts, halves, targets, sems):
+    return [
+        Freight(count, half, target, sems[4 * k : 4 * k + 4], starts[k])
+        for k, (half, target) in enumerate(zip(halves, targets))
+    ]
+
+
+def flat_rows(values):
+    return [value.reshape(-1, value.shape[2]) for value in values]
 
 
 def call(kernel, outs, ins, scratch, identity, name):
@@ -190,52 +254,6 @@
         name=name,
     )(*[value for value, _ in ins])
     return list(results)
-
-
-def spread_kernel(count, halves, small, pair, everyone, send, receive, local):
-    dp, tensor = lax.axis_index("dp"), lax.axis_index("tensor")
-    line, side, deck, core = spot()
-    greet([((dp + k) % count, tensor) for k in range(1, count)])
-    copies = [
-        remote(
-            small,
-            everyone.at[dp],
-            send.at[k],
-            receive.at[k],
-            ((dp + k) % count, tensor),
-        )
-        for k in range(1, count)
-    ]
-    copies.append(
-        remote(
-            halves.at[1 - side],
-            pair.at[side],
-            send.at[0],
-            receive.at[0],
-            seat(line, 1 - side, deck, core),
-        )
-    )
-    copies.append(pltpu.make_async_copy(small, everyone.at[dp], local.at[0]))
-    copies.append(pltpu.make_async_copy(halves.at[side], pair.at[side], local.at[1]))
-    for copy in copies:
-        copy.start()
-    for copy in copies:
-        copy.wait()
-
-
-def spread(count, halves, small):
-    return call(
-        functools.partial(spread_kernel, count),
-        [(halves.shape, BF16, ANY), ((count,) + small.shape, BF16, ANY)],
-        [(halves, ANY), (small, ANY)],
-        [
-            pltpu.SemaphoreType.DMA((count,)),
-            pltpu.SemaphoreType.DMA((count,)),
-            pltpu.SemaphoreType.DMA((2,)),
-        ],
-        0,
-        "spread",
-    )
 
 
 class GroupGather:
@@ -347,62 +365,191 @@
     ]
 
 
-def rows_kernel(count, swaps, *refs):
-    rows, block = refs[0], refs[1]
-    halves = refs[2 : 2 + swaps]
-    outs = refs[2 + swaps : 4 + swaps + swaps]
-    sems = refs[4 + swaps + swaps :]
-    everything, blocks = outs[:2]
-    pairs = outs[2:]
+SMALL_GAINS = 5
+
+
+def first_kernel(count, starts, small_top, *refs):
+    loads = len(starts)
+    rows, small = refs[:2]
+    halves, refs = refs[2 : 2 + loads], refs[2 + loads :]
+    everything, everyone, normed, pre = refs[:4]
+    targets, refs = refs[4 : 4 + loads], refs[4 + loads :]
+    incoming, table, weights, incoming_sems, out_sems, weight_sems = refs[:6]
+    sems = refs[6:]
+    dp, tensor = lax.axis_index("dp"), lax.axis_index("tensor")
     gather = GroupGather(rows, everything, *sems[:3])
     corner = sems[3:5]
-    freight = LineGather(count, block, blocks, sems[5:8])
+    send, receive, local = sems[5:8]
+    freights = load(count, starts, halves, targets, sems[8:])
+    shares = 2 * count
     line, side, deck, core = spot()
-    greet(group_peers() + line_peers(count))
+    greet(
+        [((dp + k) % shares, tensor) for k in range(1, shares)]
+        + [seat(line, side, deck, 1 - core), seat(line, side, 1 - deck, core)]
+    )
+    copies = [
+        remote(
+            small.at[(dp + k) % 2],
+            everyone.at[dp],
+            send.at[k],
+            receive.at[k],
+            ((dp + k) % shares, tensor),
+        )
+        for k in range(1, shares)
+    ]
+    copies.append(pltpu.make_async_copy(small.at[side], everyone.at[dp], local))
+    freights[0].start()
     gather.start()
-    freight.start()
-    moves = []
-    if swaps:
-        send, receive, local = sems[8:]
-        for k in range(swaps):
-            moves.append(
-                remote(
-                    halves[k].at[1 - side],
-                    pairs[k].at[side],
-                    send.at[k],
-                    receive.at[k],
-                    seat(line, 1 - side, deck, core),
-                )
-            )
-            moves.append(
-                pltpu.make_async_copy(halves[k].at[side], pairs[k].at[side], local.at[k])
-            )
-        for move in moves:
-            move.start()
+    for copy in copies:
+        copy.start()
+    for freight in freights[1:]:
+        freight.start()
+    for freight in freights:
+        freight.second()
     gather.forward()
-    freight.forward()
+    freights[0].forward()
     group_finish(gather, *corner)
-    for move in moves:
-        move.wait()
-    freight.finish()
-
-
-def gather_rows(count, rows, block, identity, halves=()):
-    scratch = rows_scratch() + LineGather.scratch(count)
-    if halves:
-        scratch += [pltpu.SemaphoreType.DMA((len(halves),))] * 3
+    for copy in copies:
+        copy.wait()
+
+    block_rows, features = rows.shape
+
+    def fetch(g):
+        slot = g % 2
+        return pltpu.make_async_copy(
+            everything.at[g], incoming.at[slot], incoming_sems.at[slot]
+        )
+
+    gain = jnp.concatenate(
+        [
+            everyone[k, small_top : small_top + 16, : features // shares].astype(F32)[
+                SMALL_GAINS : SMALL_GAINS + 1
+            ]
+            for k in range(shares)
+        ],
+        axis=1,
+    )
+    fetch(0).start()
+    for g in range(8):
+        fetch(g).wait()
+        if g < 7:
+            fetch(g + 1).start()
+
+        def norm_rows(i, carry, g=g):
+            r = pl.multiple_of(i * 32, 32)
+            value = incoming[g % 2, pl.ds(r, 32), :].astype(F32)
+            mean = jnp.mean(value * value, axis=1, keepdims=True)
+            unit = value * lax.rsqrt(mean + EPSILON)
+            table[pl.ds(g * block_rows + r, 32), :] = (unit * gain).astype(BF16)
+            return carry
+
+        lax.fori_loop(0, block_rows // 32, norm_rows, 0)
+        pltpu.make_async_copy(
+            table.at[pl.ds(g * block_rows, block_rows)],
+            normed.at[pl.ds(g * block_rows, block_rows)],
+            out_sems.at[g],
+        ).start()
+    for freight in freights[1:]:
+        freight.forward()
+    freights[0].finish()
+    depth = targets[0].shape[1]
+    loading = [
+        pltpu.make_async_copy(
+            targets[0].at[k], weights.at[pl.ds(k * depth, depth)], weight_sems.at[k]
+        )
+        for k in range(count)
+    ]
+    for copy in loading:
+        copy.start()
+    for copy in loading:
+        copy.wait()
+    lanes, width = weights.shape[1] // 2, pre.shape[1] // 2
+    shift = lanes - (2 * lanes - width)
+    inside = lax.broadcasted_iota(jnp.int32, (CHUNK, width), 1) < lanes
+
+    def product(r):
+        where = pl.ds(r, CHUNK)
+        both = jnp.dot(table[where, :], weights[...], preferred_element_type=F32)
+        pre[where, :width] = jnp.where(inside, both[:, :width], 0.0)
+        later = pltpu.roll(both[:, 2 * lanes - width :], width - shift, 1)
+        pre[where, width:] = jnp.where(inside, later, 0.0)
+
+    chunks(pre.shape[0], product)
+    for g in range(8):
+        pltpu.make_async_copy(
+            table.at[pl.ds(g * block_rows, block_rows)],
+            normed.at[pl.ds(g * block_rows, block_rows)],
+            out_sems.at[g],
+        ).wait()
+    for freight in freights[1:]:
+        freight.finish()
+
+
+def first(count, rows, small, cargo, width):
+    shares = 2 * count
+    total = 8 * rows.shape[0]
     out = call(
-        functools.partial(rows_kernel, count, len(halves)),
-        [((8,) + rows.shape, BF16, ANY), ((count,) + block.shape, BF16, ANY)]
-        + [(half.shape, BF16, ANY) for half in halves],
-        [(rows, ANY), (block, ANY)] + [(half, ANY) for half in halves],
-        scratch,
+        functools.partial(first_kernel, count, cargo_starts(cargo), small.shape[1] - 16),
+        [
+            ((8,) + rows.shape, BF16, ANY),
+            ((shares,) + small.shape[1:], BF16, VMEM),
+            ((total, rows.shape[1]), BF16, ANY),
+            ((total, 2 * width), F32, VMEM),
+        ]
+        + cargo_outs(count, cargo),
+        [(rows, ANY), (small, ANY)] + cargo_ins(cargo),
+        [
+            pltpu.VMEM((2,) + rows.shape, BF16),
+            pltpu.VMEM((total, rows.shape[1]), BF16),
+            pltpu.VMEM((rows.shape[1], cargo[0].shape[2]), BF16),
+            pltpu.SemaphoreType.DMA((2,)),
+            pltpu.SemaphoreType.DMA((8,)),
+            pltpu.SemaphoreType.DMA((count,)),
+        ]
+        + rows_scratch()
+        + [
+            pltpu.SemaphoreType.DMA((shares,)),
+            pltpu.SemaphoreType.DMA((shares,)),
+            pltpu.SemaphoreType.DMA,
+        ]
+        + cargo_scratch(count, cargo),
+        0,
+        "first",
+    )
+    return out[1:4] + flat_rows(out[4:])
+
+
+def rows_kernel(count, starts, *refs):
+    loads = len(starts)
+    rows, halves = refs[0], refs[1 : 1 + loads]
+    everything, targets = refs[1 + loads], refs[2 + loads : 2 + 2 * loads]
+    sems = refs[2 + 2 * loads :]
+    gather = GroupGather(rows, everything, *sems[:3])
+    freights = load(count, starts, halves, targets, sems[5:])
+    greet(cargo_peers(count))
+    gather.start()
+    for freight in freights:
+        freight.start()
+    for freight in freights:
+        freight.second()
+    gather.forward()
+    for freight in freights:
+        freight.forward()
+    group_finish(gather, *sems[3:5])
+    for freight in freights:
+        freight.finish()
+
+
+def gather_rows(count, rows, cargo, identity):
+    out = call(
+        functools.partial(rows_kernel, count, cargo_starts(cargo)),
+        [((8,) + rows.shape, BF16, ANY)] + cargo_outs(count, cargo),
+        [(rows, ANY)] + cargo_ins(cargo),
+        rows_scratch() + cargo_scratch(count, cargo),
         identity,
         "gather_rows",
     )
-    full = out[0].reshape(-1, rows.shape[1])
-    line = out[1].reshape(-1, block.shape[1])
-    return [full, line] + [pair.reshape(-1, pair.shape[2]) for pair in out[2:]]
+    return [out[0].reshape(-1, rows.shape[1])] + flat_rows(out[1:])
 
 
 def plain_rows_kernel(rows, everything, *sems):
@@ -425,25 +572,89 @@
     return out[0].reshape(-1, rows.shape[1])
 
 
-def fold_kernel(count, pairs, cargo, *refs):
-    lefts, rights = refs[:pairs], refs[pairs : 2 * pairs]
-    refs = refs[2 * pairs :]
-    block = None
-    if cargo:
-        block, refs = refs[0], refs[1:]
+def flip(value, bit):
+    return 1 - value if bit else value
+
+
+def whole_group():
+    line, side, deck, core = spot()
+    return [
+        seat(line, flip(side, k & 4), flip(deck, k & 2), flip(core, k & 1)) for k in range(1, 8)
+    ]
+
+
+class GainSum:
+    def __init__(self, count, gains, totals, near, far, send, receive, far_send, far_receive):
+        self.gains, self.totals, self.near, self.far = gains, totals, near, far
+        self.first = [
+            remote(gains, near.at[k], send.at[k], receive.at[k], peer)
+            for k, peer in enumerate(whole_group())
+        ]
+        self.second_copies = [
+            remote(far.at[0], far.at[1 + k], far_send.at[k], far_receive.at[k], peer)
+            for k, peer in enumerate(line_peers(count))
+        ]
+
+    @staticmethod
+    def scratch(count, gains):
+        return [
+            pltpu.VMEM((7,) + gains.shape, F32),
+            pltpu.VMEM((count,) + gains.shape, F32),
+            pltpu.SemaphoreType.DMA((7,)),
+            pltpu.SemaphoreType.DMA((7,)),
+            pltpu.SemaphoreType.DMA((count,)),
+            pltpu.SemaphoreType.DMA((count,)),
+        ]
+
+    def start(self):
+        for copy in self.first:
+            copy.start()
+
+    def second(self):
+        for copy in self.first:
+            copy.wait()
+        total = self.gains[...]
+        for k in range(7):
+            total = total + self.near[k]
+        self.far[0] = total
+        for copy in self.second_copies:
+            copy.start()
+
+    def finish(self):
+        for copy in self.second_copies:
+            copy.wait()
+        total = self.far[0]
+        for k in range(len(self.second_copies)):
+            total = total + self.far[1 + k]
+        self.totals[...] = total
+
+
+def fold_kernel(count, plan, starts, gained, *refs):
+    loads = len(starts)
+    lefts = refs[: plan[-1][0] + 1]
+    rights = refs[len(lefts) : len(lefts) + len(plan)]
+    refs = refs[len(lefts) + len(rights) :]
+    halves, refs = refs[:loads], refs[loads:]
+    gains = None
+    if gained:
+        gains, refs = refs[0], refs[1:]
     out, refs = refs[0], refs[1:]
-    if cargo:
-        blocks, refs = refs[0], refs[1:]
+    targets, refs = refs[:loads], refs[loads:]
+    if gained:
+        totals, refs = refs[0], refs[1:]
+        gain_sum = GainSum(count, gains, totals, *refs[-6:])
     mine, stage, near, leaving, arriving, refs = *refs[:5], refs[5:]
     send, receive, near_send, near_receive = refs[:4]
     line, side, deck, core = spot()
     sibling, across, above = group_peers()
-    if cargo:
-        freight = LineGather(count, block, blocks, refs[4:])
-        greet(group_peers() + line_peers(count))
+    freights = load(count, starts, halves, targets, refs[4:])
+    if gained:
+        greet(whole_group() + line_peers(count))
+        gain_sum.start()
+    else:
+        greet(cargo_peers(count) if loads else group_peers())
+    for freight in freights:
         freight.start()
-    else:
-        greet(group_peers())
     rows = out.shape[0]
     half = rows // 2
     width = out.shape[1]
@@ -455,9 +666,9 @@
         def body(j, carry):
             columns = pl.ds(pl.multiple_of(j * step, step), step)
             total = None
-            for left, right in zip(lefts, rights):
+            for (which_left, start), right in zip(plan, rights):
                 part = lax.dot_general(
-                    left[pl.ds(base, rows), :],
+                    lefts[which_left][pl.ds(base, rows), start : start + right.shape[1]],
                     right[columns, :],
                     NT,
                     preferred_element_type=F32,
@@ -524,6 +735,10 @@
 
             sweep(above_sum)
             ships[2].start()
+            for freight in freights:
+                freight.second()
+            if gained:
+                gain_sum.second()
         if q == ACROSS:
 
             def across_sum(r):
@@ -531,8 +746,6 @@
 
             sweep(across_sum)
             ships[3].start()
-    if cargo:
-        freight.forward()
     ships[0].wait_recv()
 
     def pass_across(r):
@@ -549,6 +762,10 @@
 
     sweep(pass_above)
     ships[5].start()
+    for freight in freights:
+        freight.forward()
+    if gained:
+        gain_sum.finish()
     for k in range(2, 6):
         ships[k].wait_recv()
 
@@ -564,11 +781,19 @@
         ships[k].wait_send()
     for copy in nears:
         copy.wait_send()
-    if cargo:
+    for freight in freights:
         freight.finish()
 
 
-def fold(count, lefts, rights, identity, block=None):
+def fold(count, pairs, identity, cargo=(), gains=None):
+    lefts, rights, plan = [], [], []
+    for k, (left, parts) in enumerate(pairs):
+        lefts.append(left)
+        start = 0
+        for part in parts:
+            rights.append(part)
+            plan.append((k, start))
+            start += part.shape[1]
     rows, width = lefts[0].shape[0] // 8, rights[0].shape[0]
     outs = [((rows, width), F32, VMEM)]
     ins = [(value, VMEM) for value in list(lefts) + list(rights)]
@@ -583,21 +808,24 @@
         pltpu.SemaphoreType.DMA((4,)),
         pltpu.SemaphoreType.DMA((4,)),
     ]
-    if block is not None:
-        outs.append(((count,) + block.shape, BF16, ANY))
-        ins.append((block, ANY))
-        scratch += LineGather.scratch(count)
+    outs += cargo_outs(count, cargo)
+    ins += cargo_ins(cargo)
+    scratch += cargo_scratch(count, cargo)
+    if gains is not None:
+        outs.append((gains.shape, F32, VMEM))
+        ins.append((gains, VMEM))
+        scratch += GainSum.scratch(count, gains)
     out = call(
-        functools.partial(fold_kernel, count, len(lefts), block is not None),
+        functools.partial(fold_kernel, count, plan, cargo_starts(cargo), gains is not None),
         outs,
         ins,
         scratch,
         identity,
         "fold",
     )
-    if block is not None:
-        return out[0], out[1].reshape(-1, block.shape[1])
-    return out[0]
+    if gains is not None:
+        return out
+    return out[:1] + flat_rows(out[1:])
 
 
 def gelu_both(value):
@@ -616,6 +844,14 @@
         return carry
 
     lax.fori_loop(0, rows // size, body, 0)
+
+
+def spans(low, high, action):
+    def body(i, carry):
+        action(pl.multiple_of(i * CHUNK, CHUNK))
+        return carry
+
+    lax.fori_loop(low, high, body, 0)
 
 
 def tile_scan(mults, adds, rows, width, backward):
@@ -689,42 +925,30 @@
     return entering
 
 
-def gates(values, soft):
-    recur = values
-    low = -8.0 * recur * soft
-    decay = jnp.exp(low)
-    root = jnp.sqrt((1.0 + GUARD) - decay * decay)
-    return decay, root
-
-
-def scan_kernel(
-    count,
-    pre,
-    masks,
-    table,
-    gate_weights,
-    block,
-    conv,
-    recur_out,
-    admit_out,
-    state,
-    merged,
-    entry,
-    blocks,
-    prods,
-    sums,
-    halo,
-    outgoing,
-    slots,
-    edge_sems,
-    send,
-    receive,
-    *sems,
-):
+def sigmoid(value):
+    return 0.5 + 0.5 * jnp.tanh(0.5 * value)
+
+
+def gates(recur, soft):
+    decay = jnp.exp(-8.0 * recur * soft)
+    square = (1.0 + GUARD) - decay * decay
+    inverse = lax.rsqrt(square)
+    return decay, square * inverse, inverse
+
+
+def scan_kernel(count, starts, *refs):
+    loads = len(starts)
+    pre, masks, table, gate_weights, cotangent = refs[:5]
+    halves, refs = refs[5 : 5 + loads], refs[5 + loads :]
+    conv, recur_out, admit_out, state, merged, entry, everything = refs[:7]
+    targets, refs = refs[7 : 7 + loads], refs[7 + loads :]
+    prods, sums, halo, outgoing, slots, edge_sems, send, receive = refs[:8]
+    sems = refs[8:]
     line, side, deck, core = spot()
     rows, width = conv.shape
-    freight = LineGather(count, block, blocks, sems)
-    greet(line_peers(count))
+    gather = GroupGather(cotangent, everything, *sems[:3])
+    freights = load(count, starts, halves, targets, sems[5:])
+    greet(cargo_peers(count))
 
     def edge(place):
         return remote(
@@ -739,7 +963,9 @@
     def _():
         edge(line + 1).start()
 
-    freight.start()
+    for freight in freights:
+        freight.start()
+    gather.start()
 
     def copy_entry(r):
         entry[pl.ds(r + 8, CHUNK), :] = pre[pl.ds(r, CHUNK), width:]
@@ -770,19 +996,25 @@
         where = pl.ds(r, CHUNK)
         conv[where, :] = value
         both = jnp.dot(value.astype(BF16), gate_weights[...], preferred_element_type=F32)
-        recur = jax.nn.sigmoid(both[:, :width])
-        admit = jax.nn.sigmoid(both[:, width:])
+        recur = sigmoid(both[:, :width])
+        admit = sigmoid(both[:, width:])
         recur_out[where, :] = recur
         admit_out[where, :] = admit
-        decay, root = gates(recur, table[4:5, :])
+        decay, root, _ = gates(recur, table[4:5, :])
         opened = mask[:, 3:4]
         norm = root * opened + (1.0 - opened)
         prods[where, :] = decay * opened
         sums[where, :] = norm * admit * value
 
-    chunks(rows, gate_chunk)
+    spans(0, rows // CHUNK // 2, gate_chunk)
+    for freight in freights:
+        freight.second()
+    spans(rows // CHUNK // 2, rows // CHUNK, gate_chunk)
+    gather.forward()
     prod, total = tile_scan(prods, sums, rows, width, False)
     entering = pool(count, prod, total, outgoing, slots, send, receive, False)
+    for freight in freights:
+        freight.forward()
     state[0:8, :] = entering
 
     def state_chunk(r):
@@ -793,14 +1025,15 @@
         merged[where, :] = (value * act).astype(BF16)
 
     chunks(rows, state_chunk)
-    freight.forward()
-    freight.finish()
-
-
-def scan_forward(count, pre, masks, table, gate_weights, block):
+    group_finish(gather, *sems[3:5])
+    for freight in freights:
+        freight.finish()
+
+
+def scan_forward(count, pre, masks, table, gate_weights, cotangent, cargo):
     rows, width = pre.shape[0], pre.shape[1] // 2
     out = call(
-        functools.partial(scan_kernel, count),
+        functools.partial(scan_kernel, count, cargo_starts(cargo)),
         [
             ((rows, width), F32, VMEM),
             ((rows, width), F32, VMEM),
@@ -808,9 +1041,11 @@
             ((rows + 8, width), F32, VMEM),
             ((rows, width), BF16, VMEM),
             ((rows + 8, width), F32, VMEM),
-            ((count,) + block.shape, BF16, ANY),
-        ],
-        [(pre, VMEM), (masks, VMEM), (table, VMEM), (gate_weights, VMEM), (block, ANY)],
+            ((8,) + cotangent.shape, BF16, ANY),
+        ]
+        + cargo_outs(count, cargo),
+        [(pre, VMEM), (masks, VMEM), (table, VMEM), (gate_weights, VMEM), (cotangent, ANY)]
+        + cargo_ins(cargo),
         [
             pltpu.VMEM((rows, width), F32),
             pltpu.VMEM((rows, width), F32),
@@ -821,11 +1056,12 @@
             pltpu.SemaphoreType.DMA((count,)),
             pltpu.SemaphoreType.DMA((count,)),
         ]
-        + LineGather.scratch(count),
+        + rows_scratch()
+        + cargo_scratch(count, cargo),
         2,
         "scan_forward",
     )
-    return out[:-1] + [out[-1].reshape(-1, block.shape[1])]
+    return out[:6] + [out[6].reshape(-1, cotangent.shape[1])] + flat_rows(out[7:])
 
 
 def back_kernel(
@@ -862,8 +1098,7 @@
         grad = grad_merged[where, :]
         grad_pre[where, :width] = (grad * state[pl.ds(r + 8, CHUNK), :] * slope).astype(BF16)
         direct = grad * act
-        decay, _ = gates(recur_in[where, :], table[4:5, :])
-        carry = decay * masks[where, 3:4]
+        carry = jnp.exp(-8.0 * recur_in[where, :] * table[4:5, :]) * masks[where, 3:4]
         mixes[where, :] = direct
         prods[where, :] = carry
         sums[where, :] = carry * direct
@@ -887,11 +1122,11 @@
         before = state[wide, :][7 : CHUNK + 7, :]
         soft = table[4:5, :]
         recur, admit, value = recur_in[where, :], admit_in[where, :], conv[where, :]
-        decay, root = gates(recur, soft)
+        decay, root, inverse = gates(recur, soft)
         opened = masks[where, 3:4]
         norm = root * opened + (1.0 - opened)
         flow = grad * admit
-        grad_log = opened * (grad * before * decay - flow * value * decay * decay / root)
+        grad_log = opened * (grad * before * decay - flow * value * decay * decay * inverse)
         grad_table[4:5, :] += fold_rows(grad_log * (-8.0 * recur))
         grad_rate = (grad_log * (-8.0 * soft) * recur * (1.0 - recur)).astype(BF16)
         grad_inlet = (flow * norm * value * (1.0 - admit)).astype(BF16)
@@ -977,6 +1212,110 @@
         7,
         "scan_backward",
     )
+
+
+def feed_kernel(count, early, starts, normed, cotangent, *refs):
+    loads = len(starts)
+    gate_parts, refs = refs[:2], refs[2:]
+    up_parts, refs = refs[:2], refs[2:]
+    down_parts, refs = refs[:early], refs[early:]
+    halves, refs = refs[:loads], refs[loads:]
+    hidden, grad_gating, grad_lifting = refs[:3]
+    targets, refs = refs[3 : 3 + loads], refs[3 + loads :]
+    table, acts, slopes, down, sems = *refs[:4], refs[4:]
+    table_sem, down_sems = sems[:2]
+    freights = load(count, starts, halves, targets, sems[2:])
+    greet(cargo_peers(count))
+    for freight in freights:
+        freight.start()
+    rows, width = hidden.shape
+    pieces = rows // CHUNK
+    first = pltpu.make_async_copy(normed, table, table_sem)
+    first.start()
+    first.wait()
+
+    def forward_chunk(r):
+        where = pl.ds(r, CHUNK)
+        start = 0
+        for gate_part, up_part in zip(gate_parts, up_parts):
+            columns = slice(start, start + gate_part.shape[1])
+            gating = jnp.dot(table[where, :], gate_part[...], preferred_element_type=F32)
+            lifting = jnp.dot(table[where, :], up_part[...], preferred_element_type=F32)
+            act, slope = gelu_both(gating)
+            hidden[where, columns] = (act * lifting).astype(BF16)
+            acts[where, columns] = act
+            slopes[where, columns] = lifting * slope
+            start += gate_part.shape[1]
+
+    spans(0, pieces // 4, forward_chunk)
+    for freight in freights:
+        freight.second()
+    spans(pieces // 4, pieces, forward_chunk)
+    second = pltpu.make_async_copy(cotangent, table, table_sem)
+    second.start()
+    for freight in freights:
+        freight.forward()
+    for freight in freights:
+        freight.finish()
+    rows_in = down.shape[0] // count
+    copies, start = [], 0
+    for k, part in enumerate(down_parts):
+        copies.append(
+            pltpu.make_async_copy(
+                part, down.at[:, pl.ds(start, part.shape[1])], down_sems.at[k]
+            )
+        )
+        start += part.shape[1]
+    for k, target in enumerate(targets):
+        for place in range(count):
+            copies.append(
+                pltpu.make_async_copy(
+                    target.at[place],
+                    down.at[pl.ds(place * rows_in, rows_in), pl.ds(start, target.shape[2])],
+                    down_sems.at[early + k * count + place],
+                )
+            )
+        start += target.shape[2]
+    for copy in copies:
+        copy.start()
+    second.wait()
+    for copy in copies:
+        copy.wait()
+
+    def back_chunk(r):
+        where = pl.ds(r, CHUNK)
+        for start in range(0, width, width // 3):
+            columns = slice(start, start + width // 3)
+            grad = jnp.dot(table[where, :], down[:, columns], preferred_element_type=F32)
+            grad_gating[where, columns] = (grad * slopes[where, columns]).astype(BF16)
+            grad_lifting[where, columns] = (grad * acts[where, columns]).astype(BF16)
+
+    chunks(rows, back_chunk)
+
+
+def feed(count, normed, cotangent, gate_parts, up_parts, down_parts, cargo):
+    rows = normed.shape[0]
+    width = sum(part.shape[1] for part in gate_parts)
+    out = call(
+        functools.partial(feed_kernel, count, len(down_parts), cargo_starts(cargo)),
+        [((rows, width), BF16, VMEM)] * 3 + cargo_outs(count, cargo),
+        [(normed, ANY), (cotangent, ANY)]
+        + [(part, VMEM) for part in list(gate_parts) + list(up_parts)]
+        + [(part, ANY) for part in down_parts]
+        + cargo_ins(cargo),
+        [
+            pltpu.VMEM(normed.shape, BF16),
+            pltpu.VMEM((rows, width), F32),
+            pltpu.VMEM((rows, width), F32),
+            pltpu.VMEM((normed.shape[1], width), BF16),
+            pltpu.SemaphoreType.DMA,
+            pltpu.SemaphoreType.DMA((len(down_parts) + count * len(cargo),)),
+        ]
+        + cargo_scratch(count, cargo),
+        5,
+        "feed",
+    )
+    return out[:3] + flat_rows(out[3:])
 
 
 def doc_index(places, doc_starts):
@@ -1040,71 +1379,70 @@
         [split_columns(branch_gate), split_columns(branch_input)], axis=2
     )
     mixer_halves = widen(split_columns(mixer_out.T), width)
-    gate_halves, up_halves = split_columns(feed_gate), split_columns(feed_up)
-    down_halves = split_columns(feed_down.T)
-    flat = jnp.concatenate(
+    down_rows = feed_down.T
+    narrow = feed_gate.shape[1] // 6
+    broad = 2 * narrow
+
+    mine = lax.axis_index("dp")
+    blocks = jnp.concatenate(
         [
-            mixer_gain,
-            feed_gain,
-            rate_gate.reshape(-1),
-            input_gate.reshape(-1),
-            conv_taps.reshape(-1),
-            decay_param.reshape(-1),
+            jnp.stack(
+                [
+                    jnp.pad(
+                        jnp.concatenate(
+                            [
+                                widen(jnp.pad(rate_gate[h], ((0, 0), (p, 0))), width),
+                                widen(jnp.pad(input_gate[h], ((0, 0), (p, 0))), width),
+                            ],
+                            axis=1,
+                        ),
+                        ((0, 0), (0, 0)),
+                    )
+                    for h, p in [(s * half_heads + k, k * head_width) for k in range(half_heads)]
+                ]
+            ).reshape(1, half_heads * piece, 2 * width)
+            for s in range(2)
         ]
     )
-    small_rows = -(-flat.shape[0] // (128 * 16)) * 16
-    small = jnp.pad(flat, (0, small_rows * 128 - flat.shape[0])).reshape(small_rows, 128)
-    branch_pair, small_all = spread(shares, branch_halves, small)
-
-    small_all = small_all.reshape(shares, -1)
-    cuts = [slim, slim, rate_gate.size, input_gate.size, conv_taps.size, decay_param.size]
-    parts, start = [], 0
-    for size in cuts:
-        parts.append(small_all[:, start : start + size])
-        start += size
-    gain_first = parts[0].reshape(feature_count).astype(F32)
-    gain_second = parts[1].reshape(feature_count).astype(F32)
-
-    def own_heads(value, axis):
-        return lax.dynamic_slice_in_dim(value, side * half_heads, half_heads, axis)
-
-    rate_weights, inlet_weights = [
-        own_heads(
-            part.reshape(shares, heads, piece, head_width)
-            .transpose(1, 0, 2, 3)
-            .reshape(heads, shares * piece, head_width),
-            0,
-        )
-        for part in parts[2:4]
-    ]
-    taps = own_heads(
-        parts[4].reshape(shares, TAPS, heads, piece).transpose(1, 2, 0, 3), 1
-    ).reshape(TAPS, lanes)
-    decay_flat = own_heads(
-        parts[5].reshape(shares, heads, piece).transpose(1, 0, 2), 0
-    ).reshape(lanes).astype(F32)
-    table = widen(
-        jnp.concatenate(
-            [
-                taps.astype(F32),
-                jax.nn.softplus(-decay_flat)[None],
-                jnp.zeros((3, lanes), F32),
-            ]
-        ),
-        width,
-    )
-
-    def diagonal(blocks):
-        bands = [
-            jnp.pad(
-                blocks[h],
-                ((0, 0), (h * head_width, width - (h + 1) * head_width)),
-            )
-            for h in range(half_heads)
+    own = jnp.concatenate([conv_taps, decay_param[None]], axis=0)
+    own = jnp.pad(own, ((0, 0), (0, 0), (0, head_width - piece)))
+    own = jnp.roll(own, mine * piece, axis=2)
+    own = own.reshape(TAPS + 1, 2, lanes).transpose(1, 0, 2)
+    gains_own = jnp.pad(
+        jnp.stack([mixer_gain, feed_gain]), ((0, 16 - TAPS - 3), (0, 2 * width - slim))
+    )
+    tail = jnp.concatenate(
+        [widen(own, 2 * width), jnp.broadcast_to(gains_own, (2,) + gains_own.shape)], axis=1
+    )
+    small_top = -(-half_heads * piece // 16) * 16
+    small = jnp.concatenate(
+        [jnp.pad(blocks, ((0, 0), (0, small_top - half_heads * piece), (0, 0))), tail], axis=1
+    )
+
+    small_all, normed_one, pre, branch_all, gate_first = first(
+        count, layer_input, small, [branch_halves, (feed_gate, 0, narrow)], width
+    )
+
+    tails = small_all[:, small_top:].astype(F32)
+    gain_first = tails[:, SMALL_GAINS, :slim].reshape(feature_count)
+    gain_second = tails[:, SMALL_GAINS + 1, :slim].reshape(feature_count)
+    sums = jnp.sum(tails[:, : TAPS + 1, :width], axis=0)
+    decay_flat = sums[TAPS, :lanes]
+    inside = (jnp.arange(width) < lanes)[None]
+    table = jnp.concatenate(
+        [
+            sums[:TAPS],
+            jnp.where(inside, jax.nn.softplus(-sums[TAPS:]), 0.0),
+            jnp.zeros((3, width), F32),
         ]
-        return jnp.pad(jnp.concatenate(bands, axis=0), ((0, width - lanes), (0, 0)))
-
-    gate_weights = jnp.concatenate([diagonal(rate_weights), diagonal(inlet_weights)], axis=1)
+    )
+    gate_weights = (
+        small_all[:, : half_heads * piece]
+        .reshape(shares, half_heads, piece, 2 * width)
+        .transpose(1, 0, 2, 3)
+        .reshape(lanes, 2 * width)
+    )
+    gate_weights = jnp.pad(gate_weights, ((0, width - lanes), (0, 0)))
 
     anchor = lax.axis_index("dp") // 2 * rows
     places = anchor + jnp.arange(rows, dtype=jnp.int32)
@@ -1117,73 +1455,79 @@
 
     residual = layer_input.astype(F32)
     unit_one, scale_one = unit_norm(residual)
-    normed_own = (unit_one * gain_first).astype(BF16)
-    normed_one, branch_all, mixer_pair, gate_pair, up_pair, down_pair = gather_rows(
-        count,
-        normed_own,
-        branch_pair.reshape(-1, 2 * lanes),
-        1,
-        (mixer_halves, gate_halves, up_halves, down_halves),
-    )
     branch_wide = jnp.concatenate(
         [widen(branch_all[:, :lanes], width), widen(branch_all[:, lanes:], width)], axis=1
     )
-    pre = jnp.dot(normed_one, branch_wide, preferred_element_type=F32)
-    conv, recur, admit, state, merged, entry, mixer_all = scan_forward(
-        count, pre, masks, table, gate_weights, mixer_pair
-    )
-    mixer_own, gating_weights = fold(count, [merged], [mixer_all], 3, gate_pair)
+    conv, recur, admit, state, merged, entry, cot_all, mixer_all, up_first = scan_forward(
+        count, pre, masks, table, gate_weights, out_grad, [mixer_halves, (feed_up, 0, narrow)]
+    )
+    mixer_own, gate_second, down_first = fold(
+        count, [(merged, [mixer_all])], 3, [(feed_gate, narrow, broad), (down_rows, 0, narrow)]
+    )
     hidden_one = residual + mixer_own
     unit_two, scale_two = unit_norm(hidden_one)
-    normed_two, lifting_weights = gather_rows(
-        count, (unit_two * gain_second).astype(BF16), up_pair, 4
-    )
-    cot_all, lowering_weights = gather_rows(count, out_grad, down_pair, 5)
-
-    gating_pre = jnp.dot(normed_two, gating_weights, preferred_element_type=F32)
-    lifting_pre = jnp.dot(normed_two, lifting_weights, preferred_element_type=F32)
-    gating_act, gating_slope = gelu_both(gating_pre)
-    hidden = (gating_act * lifting_pre).astype(BF16)
+    normed_two, up_second = gather_rows(
+        count, (unit_two * gain_second).astype(BF16), [(feed_up, narrow, broad)], 4
+    )
+    gate_parts, up_parts = [gate_first, gate_second], [up_first, up_second]
+    hidden, grad_gating, grad_lifting, down_second = feed(
+        count, normed_two, cot_all, gate_parts, up_parts, [down_first], [(down_rows, narrow, broad)]
+    )
+    down_parts = [down_first, down_second]
 
     def line_sum(value):
         return lax.psum_scatter(
             value, "dp", scatter_dimension=0, axis_index_groups=line_groups, tiled=True
         )
 
-    down_sum = line_sum(by_rows(cot_all, hidden))
-    grad_hidden = lax.dot_general(cot_all, lowering_weights, (((1,), (0,)), ((), ())), preferred_element_type=F32)
-    grad_gating = (grad_hidden * lifting_pre * gating_slope).astype(BF16)
-    grad_lifting = (grad_hidden * gating_act).astype(BF16)
-    gate_sum = line_sum(by_rows(normed_two, grad_gating))
-    up_sum = line_sum(by_rows(normed_two, grad_lifting))
-    grad_normed_two = fold(
-        count, [grad_gating, grad_lifting], [gating_weights, lifting_weights], 6
-    )
+    down_grads = by_rows(cot_all, hidden)
+    grad_gating, grad_lifting, down_grads = lax.optimization_barrier(
+        (grad_gating, grad_lifting, down_grads)
+    )
+    gate_grads = by_rows(normed_two, grad_gating)
+    up_grads = by_rows(normed_two, grad_lifting)
+    grad_gating, grad_lifting, down_grads, gate_grads, up_grads = lax.optimization_barrier(
+        (grad_gating, grad_lifting, down_grads, gate_grads, up_grads)
+    )
+    down_sum, gate_sum, up_sum = line_sum(down_grads), line_sum(gate_grads), line_sum(up_grads)
+    grad_normed_two = fold(count, [(grad_gating, gate_parts), (grad_lifting, up_parts)], 6)[0]
     grad_hidden_one = out_grad.astype(F32) + norm_back(
         grad_normed_two * gain_second, unit_two, scale_two
     )
+    grad_hidden_one, down_sum = lax.optimization_barrier((grad_hidden_one, down_sum))
     back_low = gather_plain(grad_hidden_one.astype(BF16), 8)
-    outlet_sum = line_sum(by_rows(back_low, merged))
+    outlet_grads = by_rows(back_low, merged)
     grad_merged = jnp.dot(back_low, mixer_all, preferred_element_type=F32)
+    grad_merged, outlet_grads, gate_sum = lax.optimization_barrier(
+        (grad_merged, outlet_grads, gate_sum)
+    )
+    outlet_sum = line_sum(outlet_grads)
     grad_pre, grad_gates, grad_table = scan_backward(
         count, pre, grad_merged, [conv, recur, admit, state, entry], masks, table, gate_weights
     )
     branch_grads = by_rows(normed_one, grad_pre)
-    branch_sum = line_sum(
-        jnp.concatenate([branch_grads[:, :lanes], branch_grads[:, width : width + lanes]], axis=1)
-    )
-    feed_own = fold(count, [hidden], [lowering_weights], 9)
+    branch_grads = jnp.concatenate(
+        [branch_grads[:, :lanes], branch_grads[:, width : width + lanes]], axis=1
+    )
+    grad_pre, branch_grads = lax.optimization_barrier((grad_pre, branch_grads))
+    branch_sum = line_sum(branch_grads)
+    grad_normed_one = fold(count, [(grad_pre, [branch_wide])], 10)[0]
+    hidden, grad_normed_one, up_sum = lax.optimization_barrier(
+        (hidden, grad_normed_one, up_sum)
+    )
+    gains = jnp.concatenate(
+        [
+            jnp.sum(grad_normed_one * unit_one, axis=0).reshape(shares, slim),
+            jnp.sum(grad_normed_two * unit_two, axis=0).reshape(shares, slim),
+        ]
+    )
+    feed_own, gains = fold(count, [(hidden, down_parts)], 9, gains=gains)
+    first_gain_grad = lax.dynamic_index_in_dim(gains, mine, 0, False)
+    second_gain_grad = lax.dynamic_index_in_dim(gains, shares + mine, 0, False)
     layer_output = (hidden_one + feed_own).astype(BF16)
-    grad_normed_one = fold(count, [grad_pre], [branch_wide], 10)
     input_grad = (
         grad_hidden_one + norm_back(grad_normed_one * gain_first, unit_one, scale_one)
     ).astype(BF16)
-
-    gains = jnp.stack(
-        [jnp.sum(grad_normed_one * unit_one, axis=0), jnp.sum(grad_normed_two * unit_two, axis=0)]
-    )
-    gains = lax.psum(gains, ("dp", "tensor"))
-    gains = lax.dynamic_slice_in_dim(gains, lax.axis_index("dp") * slim, slim, 1)
 
     def spots(value):
         blocks = [
@@ -1246,7 +1590,7 @@
     return (
         layer_output,
         input_grad,
-        gains[0],
+        first_gain_grad,
         branch_gate_grad,
         branch_input_grad,
         taps_grad,
@@ -1254,7 +1598,7 @@
         inlet_grad,
         decay_grad,
         mixer_out_grad,
-        gains[1],
+        second_gain_grad,
         joined(gate_sum),
         joined(up_sum),
         joined(down_sum).T,

time: 906 us -> 747 us (0.82)
  waiting for transfers between devices: 77.8 us -> 12.1 us
  matrix products: 113 us -> 63.5 us
  blocking collectives: 41.1 us -> 0 us
  other arithmetic: 37.5 us -> 49 us
  Pallas kernels: 559 us -> 548 us
    reduce_scatter x6, waiting for transfers between devices: 63 us -> 4.11 us  [line_sum(): lax.psum_scatter(value, 'dp', scatter_dimension=0, axis_index_groups=line...]
    dot_general x4 -> x0, matrix products: 49.5 us -> none  [the longest x1 18.5 us: shards(): lax.dot_general(cot_all, lowering_weights, (((1,), (0,)), ((), ())), pref...]
    psum x1 -> x0, blocking collectives: 41.1 us -> none  [shards(): gains = lax.psum(gains, ('dp', 'tensor'))]
    pallas_call x11 -> x10, Pallas kernels: 559 us -> 548 us  [call(): pl.pallas_call(kernel, out_shape=[jax.ShapeDtypeStruct(shape, kind) for s...]
  transfers between devices with their start and end apart: 12 -> 12, of which waited for: 5 -> 3; matrix products, arithmetic and copies ran while one was open for 10% -> 14% of each run, Pallas kernels for 10% -> 30%
where the time goes in v2:
time: 747 us; the launch traced here: 740 us
  Pallas kernels  548 us (73%)
  matrix products  63.5 us (9%)
  other arithmetic  49 us (7%)
  local copies, waits for them, and re-layouts  46.6 us (6%)
  between operations  15.4 us (2%)
  waiting for transfers between devices  12.1 us (2%)
    pallas_call x10, Pallas kernels, call(): pl.pallas_call(kernel, out_shape=[jax.ShapeDtypeStruct(shape, kind) for s...  548 us
    dot_general x5, matrix products, by_rows(): lax.dot_general(left, right, TN, preferred_element_type=F32).astype(BF16)  53.5 us
  transfers between devices with their start and end apart: 12, of which 3 were waited for; matrix products, arithmetic and copies ran while one was open for 14% of the time, Pallas kernels for 30%

profile of v2, /device:TPU:0, one launch (start us, length us, event | category | flops | bytes accessed | tf_op | source)
XLA Modules:
  0.0 740.2 jit_solution(4533156227796281625)
XLA Ops:
  15.5 91.9 %first.1 = (bf16[8,256,2048]{2,1,0:T(8,128)(2,1)}, bf16[8,64,768]{2,1,0:T(8,128)(2,1)}, bf16[2048,2048]{1,0:T(8,128)(2,1)}, f32[2048,768]{1,0:T(8,128)}, bf16[4,...) custom-call(bf16[256,2048]{1,0:T(8,128)(2,1)} %refs_0_.1, bf16[2,64,768]{2,1,0:T(8,128)(2,1)} %fusion.19.refs_1_, ...), custom_call_target="tpu_custom_call" | custom-call | tf_op jit(solution)/shard_map/first/pallas_call | solution.py:245
  115.8 64.7 %scan_forward.1 = (f32[2048,384]{1,0:T(8,128)}, f32[2048,384]{1,0:T(8,128)}, f32[2048,384]{1,0:T(8,128)}, f32[2056,384]{1,0:T(8,128)}, bf16[2048,384]{1,0:T(8,12...) custom-call(f32[2048,768]{1,0:T(8,128)} %get-tuple-element.60.refs_0, ...), custom_call_target="tpu_custom_call" | custom-call | tf_op jit(solution)/shard_map/scan_forward/pallas_call | solution.py:245
  180.4 58.1 %fold.4 = (f32[256,2048]{1,0:T(8,128)}, bf16[4,512,512]{2,1,0:T(8,128)(2,1)}, bf16[4,512,256]{2,1,0:T(8,128)(2,1)}) custom-call(bf16[2048,384]{1,0:T(8,128)(2,1)} %get-tuple-element.62.refs_0_, bf16[2048,384]{1,0:T(8,128)(2,1)} %bitcast.140, bf16[256,1536]{1,0:T(8,128)(2,1)} %refs_2_.1, bf16[256,1536]{1,0:T(8,128)(2,1)} %bitcast.128), custom_call_target="tpu_custom_call" | custom-call | tf_op jit(solution)/shard_map/fold/pallas_call | solution.py:245
  238.5 2.7 multiply_reduce_fusion.2
  241.2 1.2 multiply_convert_fusion.refs_0_
  242.4 56.4 %gather_rows.2 = (bf16[8,256,2048]{2,1,0:T(8,128)(2,1)}, bf16[4,512,512]{2,1,0:T(8,128)(2,1)}) custom-call(bf16[256,2048]{1,0:T(8,128)(2,1)} %multiply_convert_fusion.refs_0_, bf16[256,1536]{1,0:T(8,128)(2,1)} %refs_1_.1), custom_call_target="tpu_custom_call" | custom-call | tf_op jit(solution)/shard_map/gather_rows/pallas_call | solution.py:245
  298.8 52.7 %feed.1 = (bf16[2048,768]{1,0:T(8,128)(2,1)}, bf16[2048,768]{1,0:T(8,128)(2,1)}, bf16[2048,768]{1,0:T(8,128)(2,1)}, bf16[4,512,512]{2,1,0:T(8,128)(2,1)}) custom-call(bf16[2048,2048]{1,0:T(8,128)(2,1)} %bitcast.119, bf16[2048,2048]{1,0:T(8,128)(2,1)} %bitcast.117, bf16[2048,256]{1,0:T(8,128)(2,1)} %bitcast.130, bf16[2048,512]{1,0:T(8,128)(2,1)} %bitcast.122, ...), custom_call_target="tpu_custom_call" | custom-call | tf_op jit(solution)/shard_map/feed/pallas_call | solution.py:245
  351.5 11.8 %convolution_convert_fusion.3 = bf16[2048,768]{1,0:T(8,128)(2,1)} fusion(bf16[2048,2048]{1,0:T(8,128)(2,1)} %bitcast.118, bf16[2048,768]{1,0:T(8,128)(2,1)} %get-tuple-element.94.refs_0_), kind=kOutput, calls=%fused_computation.5 | convolution fusion | flops 6444023808 | bytes 14680064 | tf_op jit(solution)/shard_map/dot_general | solution.py:1346
  363.3 11.4 %convolution_convert_fusion.1 = bf16[2048,768]{1,0:T(8,128)(2,1)} fusion(bf16[2048,2048]{1,0:T(8,128)(2,1)} %bitcast.120, bf16[2048,768]{1,0:T(8,128)(2,1)} %get-tuple-element.79.refs_1_), kind=kOutput, calls=%fused_computation.3 | convolution fusion | flops 6444023808 | bytes 14680064 | tf_op jit(solution)/shard_map/dot_general | solution.py:1346
  374.7 11.4 %convolution_convert_fusion.2 = bf16[2048,768]{1,0:T(8,128)(2,1)} fusion(bf16[2048,2048]{1,0:T(8,128)(2,1)} %bitcast.121, bf16[2048,768]{1,0:T(8,128)(2,1)} %get-tuple-element.78.refs_0_), kind=kOutput, calls=%fused_computation.4 | convolution fusion | flops 6444023808 | bytes 14680064 | tf_op jit(solution)/shard_map/dot_general | solution.py:1346
  387.6 49.4 %fold.5 = f32[256,2048]{1,0:T(8,128)} custom-call(bf16[2048,768]{1,0:T(8,128)(2,1)} %get-tuple-element.78.refs_0_, bf16[2048,768]{1,0:T(8,128)(2,1)} %get-tuple-element.79.refs_1_, bf16[2048,256]{1,0:T(8,128)(2,1)} %bitcast.131, bf16[2048,512]{1,0:T(8,128)(2,1)} %bitcast.123, bf16[2048,256]{1,0:T(8,128)(2,1)} %bitcast.133, bf16[2048,512]{1,0:T(8,128)(2,1)} %bitcast.125), custom_call_target="tpu_custom_call" | custom-call | tf_op jit(solution)/shard_map/fold/pallas_call | solution.py:245
  437.0 2.3 multiply_reduce_fusion
  439.5 2.0 multiply_add_fusion
  441.5 3.8 reduce-scatter.7.cloned.1.call-done
  445.3 2.7 convert_element_type.133.rows
  448.0 40.1 %gather_rows.3 = bf16[8,256,2048]{2,1,0:T(8,128)(2,1)} custom-call(bf16[256,2048]{1,0:T(8,128)(2,1)} %convert_element_type.133.rows), custom_call_target="tpu_custom_call" | custom-call | tf_op jit(solution)/shard_map/gather_rows/pallas_call | solution.py:245
  488.0 9.6 %convolution_convert_fusion.4 = bf16[2048,384]{1,0:T(8,128)(2,1)} fusion(bf16[2048,2048]{1,0:T(8,128)(2,1)} %bitcast.126, bf16[2048,384]{1,0:T(8,128)(2,1)} %get-tuple-element.62.refs_0_), kind=kOutput, calls=%fused_computation.13 | convolution fusion | flops 3222011904 | bytes 11534336 | tf_op jit(solution)/shard_map/dot_general | solution.py:1346
  497.6 10.0 %fusion.69.grad_merged = f32[2048,384]{1,0:T(8,128)} fusion(bf16[2048,2048]{1,0:T(8,128)(2,1)} %bitcast.127, bf16[2048,384]{1,0:T(8,128)(2,1)} %bitcast.141), kind=kOutput, calls=%fused_computation.168 | convolution fusion | flops 3221225472 | bytes 13107200 | tf_op jit(solution)/shard_map/dot_general | solution.py:1500
  507.9 38.7 %scan_backward.1 = (bf16[2048,768]{1,0:T(8,128)(2,1)}, f32[384,768]{1,0:T(8,128)}, f32[8,384]{1,0:T(8,128)}) custom-call(f32[2048,768]{1,0:T(8,128)} %get-tuple-element.60.refs_0_.pre, f32[2048,384]{1,0:T(8,128)} %fusion.69.grad_merged, f32[2048,384]{1,0:T(8,128)} %get-tuple-element.84.conv, f32[2048,384]{1,0:T(8,128)} %get-tuple-element.85.recur_in, ...), custom_call_target="tpu_custom_call" | custom-call | tf_op jit(solution)/shard_map/scan_backward/pallas_call | solution.py:245
  548.3 1.3 convert.36
  553.1 2.7 slice_select_fusion
  556.5 3.3 slice.195
  560.4 4.0 fusion.1.refs_1_
  564.4 9.3 %convolution_convert_fusion = bf16[2048,768]{0,1:T(8,128)(2,1)S(1)} fusion(bf16[2048,2048]{1,0:T(8,128)(2,1)} %get-tuple-element.90, bf16[2048,768]{1,0:T(8,128)(2,1)S(1)} %copy-done.3), kind=kOutput, calls=%fused_computation.2 | convolution fusion | flops 6444023808 | bytes 14680064 | tf_op jit(solution)/shard_map/dot_general | solution.py:1346
  574.0 1.8 pad_maximum_fusion
  575.8 1.9 constant_dynamic-slice_fusion.1
  577.7 1.9 copy.153
  579.8 46.1 %fold.6 = f32[256,2048]{1,0:T(8,128)} custom-call(bf16[2048,768]{1,0:T(8,128)(2,1)} %get-tuple-element.91.refs_0_, bf16[2048,768]{1,0:T(8,128)(2,1)} %fusion.1.refs_1_), custom_call_target="tpu_custom_call" | custom-call | tf_op jit(solution)/shard_map/fold/pallas_call | solution.py:245
  625.9 2.0 constant_dynamic-slice_fusion.3
  628.0 1.9 copy.151
  629.9 1.2 collective-permute-start.4
  631.1 2.0 constant_dynamic-slice_fusion.5
  633.1 1.9 copy.149
  635.9 3.1 fusion.6
  639.6 1.3 pad_maximum_fusion.8.refs_3_
  640.9 50.2 %fold.7 = (f32[256,2048]{1,0:T(8,128)}, f32[16,256]{1,0:T(8,128)}) custom-call(bf16[2048,768]{1,0:T(8,128)(2,1)} %get-tuple-element.94.refs_0_, bf16[2048,256]{1,0:T(8,128)(2,1)} %bitcast.135, bf16[2048,512]{1,0:T(8,128)(2,1)} %bitcast.138, f32[16,256]{1,0:T(8,128)} %pad_maximum_fusion.8.refs_3_), custom_call_target="tpu_custom_call" | custom-call | tf_op jit(solution)/shard_map/fold/pallas_call | solution.py:245
  691.2 3.9 fusion.10
  695.1 1.3 add_convert_fusion
  696.9 1.3 constant_dynamic-slice_fusion.6
  700.4 1.8 bitcast_select_fusion.5
  702.2 1.3 convert_bitcast_fusion
  703.6 1.4 dynamic-slice_bitcast_fusion
  706.9 1.6 copy.157
  708.5 1.6 copy.156
  713.6 1.3 collective-permute-start.2
  717.0 2.0 reshape.343
  719.0 1.4 constant_dynamic-slice_fusion.10
  723.9 6.6 collective-permute-done
  (187 shorter events, 42.5 us)
Async XLA Ops:
  7.2 6.1 copy-start.8
  7.2 438.1 %reduce-scatter.7.cloned.1.call-start = ((), (), s32[]{:S(2)}) async-start(), calls=%async_computation.6 | async-start | bytes 3932160 | tf_op jit(solution)/shard_map/reduce_scatter | solution.py:1479
  15.5 94.0 %copy-start.16 = (s32[6]{0:T(128)S(1)}, s32[6]{0:T(128)}, u32[]{:S(2)}) copy-start(s32[6]{0:T(128)} %param.17) | copy-start | bytes 76
  108.4 3.5 copy-start.11
  110.6 1.4 copy-start.9
  111.8 2.0 copy-start.7
  112.0 3.1 slice-start
  180.4 58.1 %copy-start.1 = (bf16[256,2048]{1,0:T(8,128)(2,1)S(1)}, bf16[256,2048]{1,0:T(8,128)(2,1)}, u32[]{:S(2)}) copy-start(bf16[256,2048]{1,0:T(8,128)(2,1)} %refs_0_.1) | copy-start | bytes 3145732
  386.1 121.8 %reduce-scatter.9.cloned.1.call-start = ((), (), s32[]{:S(2)}) async-start(), calls=%async_computation.7 | async-start | bytes 3932160 | tf_op jit(solution)/shard_map/reduce_scatter | solution.py:1479
  386.9 239.1 %reduce-scatter.11.cloned.1.call-start = ((), (), s32[]{:S(2)}) async-start(), calls=%async_computation.8 | async-start | bytes 3932160 | tf_op jit(solution)/shard_map/reduce_scatter | solution.py:1479
  387.6 316.0 %reduce-scatter.15.cloned.1.call-start = ((), (), s32[]{:S(2)}) async-start(), calls=%async_computation.10 | async-start | bytes 286720 | tf_op jit(solution)/shard_map/reduce_scatter | solution.py:1479
  437.0 2.3 copy-start
  437.0 2.5 copy-start.2
  507.9 39.5 %copy-start.12 = (f32[5,384]{1,0:T(8,128)S(1)}, f32[5,384]{1,0:T(8,128)}, u32[]{:S(2)}) copy-start(f32[5,384]{1,0:T(8,128)} %copy-done.11) | copy-start | bytes 23044
  553.0 159.4 %reduce-scatter.17.cloned.1.call-start = ((), (), s32[]{:S(2)}) async-start(), calls=%async_computation.11 | async-start | bytes 1966080 | tf_op jit(solution)/shard_map/reduce_scatter | solution.py:1479
  553.1 2.8 copy-start.14
  555.8 161.2 %reduce-scatter.13.cloned.1.call-start = ((), (), s32[]{:S(2)}) async-start(), calls=%async_computation.9 | async-start | bytes 3276800 | tf_op jit(solution)/shard_map/reduce_scatter | solution.py:1479
  560.4 4.0 copy-start.3
  579.6 118.6 %collective-permute-start.5 = (bf16[256,768]{0,1:T(8,128)(2,1)}, bf16[256,768]{0,1:T(8,128)(2,1)}, u32[]{:S(2)}, u32[]{:S(2)}) collective-permute-start(bf16[256,768]{0,1:T(8,128)(2,1)} %bitcast.152), channel_id=1, source_target_pairs={{0,4},{4,0},{8,12},{12,8},{16,20},{20,16},{24,28},{28,24},{1,5},{5... | collective-permute-start | bytes 1179656 | tf_op jit(solution)/shard_map/ppermute | solution.py:1563
  629.9 69.4 %collective-permute-start.4 = (bf16[256,768]{0,1:T(8,128)(2,1)}, bf16[256,768]{0,1:T(8,128)(2,1)}, u32[]{:S(2)}, u32[]{:S(2)}) collective-permute-start(bf16[256,768]{0,1:T(8,128)(2,1)} %bitcast.153), channel_id=1, source_target_pairs={{0,4},{4,0},{8,12},{12,8},{16,20},{20,16},{24,28},{28,24},{1,5},{5... | collective-permute-start | bytes 1179656 | tf_op jit(solution)/shard_map/ppermute | solution.py:1563
  635.0 65.3 %collective-permute-start.3 = (bf16[256,768]{0,1:T(8,128)(2,1)}, bf16[256,768]{0,1:T(8,128)(2,1)}, u32[]{:S(2)}, u32[]{:S(2)}) collective-permute-start(bf16[256,768]{0,1:T(8,128)(2,1)} %bitcast.154), channel_id=1, source_target_pairs={{0,4},{4,0},{8,12},{12,8},{16,20},{20,16},{24,28},{28,24},{1,5},{5... | collective-permute-start | bytes 1179656 | tf_op jit(solution)/shard_map/ppermute | solution.py:1563
  640.9 50.2 %copy-start.15 = (f32[256]{0:T(256)S(1)}, f32[256]{0:T(256)}, u32[]{:S(2)}) copy-start(f32[256]{0:T(256)} %get-tuple-element.164) | copy-start | bytes 3076
  640.9 50.3 %copy-start.13 = (f32[256]{0:T(256)S(1)}, f32[256]{0:T(256)}, u32[]{:S(2)}) copy-start(f32[256]{0:T(256)} %add_rsqrt_fusion) | copy-start | bytes 3076
  691.2 3.9 copy-start.4
  695.1 1.4 copy-start.5
  695.1 1.6 copy-start.6
  704.9 5.2 collective-permute-start.1
  708.5 1.6 copy-start.10
  713.6 8.5 %collective-permute-start.2 = (bf16[256,384]{0,1:T(8,128)(2,1)S(1)}, bf16[256,384]{0,1:T(8,128)(2,1)S(1)}, u32[]{:S(2)}, u32[]{:S(2)}) collective-permute-start(bf16[256,384]{0,1:T(8,128)(2,1)S(1)} %bitcast.161), channel_id=1, source_target_pairs={{0,4},{4,0},{8,12},{12,8},{16,20},{20,16},{24,28},{28,24},{1,5},{5... | collective-permute-start | bytes 589832 | tf_op jit(solution)/shard_map/ppermute | solution.py:1563
  721.3 9.2 %collective-permute-start = (bf16[256,640]{1,0:T(8,128)(2,1)S(1)}, bf16[256,640]{1,0:T(8,128)(2,1)S(1)}, u32[]{:S(2)}, u32[]{:S(2)}) collective-permute-start(bf16[256,640]{1,0:T(8,128)(2,1)S(1)} %bitcast.156), channel_id=1, source_target_pairs={{0,4},{4,0},{8,12},{12,8},{16,20},{20,16},{24,28},{28,24},{1,5},{5... | collective-permute-start | bytes 983048 | tf_op jit(solution)/shard_map/ppermute | solution.py:1563
Sparse Core Ops, SparseCore 0:
  386.2 58.9 reduce-scatter.6
  447.6 60.2 reduce-scatter.8
  510.2 62.0 reduce-scatter.10
  574.4 19.5 reduce-scatter.14
  596.3 33.5 reduce-scatter.16
  632.1 52.1 reduce-scatter.12

commit v3 on v2

--- a/solution.py
+++ b/solution.py
@@ -202,6 +202,68 @@
 
         self.keep().wait()
         self.swap().wait_send()
+
+
+class Stream:
+    def __init__(self, source, target, sems, from_row=0, to_row=0, columns=None):
+        self.source, self.target, self.sems = source, target, sems
+        self.from_row, self.to_row, self.columns = from_row, to_row, columns
+        self.pieces = sems.shape[0]
+
+    def copy(self, r):
+        source = (pl.ds(r + self.from_row, CHUNK),)
+        if self.columns is not None:
+            source += (self.columns,)
+        return pltpu.make_async_copy(
+            self.source.at[source],
+            self.target.at[pl.ds(r + self.to_row, CHUNK)],
+            self.sems.at[r // CHUNK],
+        )
+
+    def start(self, r):
+        self.copy(r).start()
+
+    def wait(self, r):
+        self.copy(r).wait()
+
+    def start_all(self):
+        for k in range(self.pieces):
+            self.start(k * CHUNK)
+
+    def wait_all(self):
+        for k in range(self.pieces):
+            self.wait(k * CHUNK)
+
+
+class Swap:
+    def __init__(self, values, outs, send, receive, local):
+        line, side, deck, core = spot()
+        self.copies = []
+        for k, (value, out) in enumerate(zip(values, outs)):
+            self.copies.append(
+                remote(
+                    value.at[1 - side],
+                    out.at[side],
+                    send.at[k],
+                    receive.at[k],
+                    seat(line, 1 - side, deck, core),
+                )
+            )
+            self.copies.append(
+                pltpu.make_async_copy(value.at[side], out.at[side], local.at[k])
+            )
+
+    @staticmethod
+    def scratch(values):
+        return [pltpu.SemaphoreType.DMA((len(values),))] * 3 if values else []
+
+    def start(self):
+        for copy in self.copies:
+            copy.start()
+
+    def finish(self):
+        for copy in self.copies:
+            copy.wait()
 
 
 def cargo_peers(count):
@@ -317,10 +379,22 @@
 
     def start(self):
         self.make()
-        for copy in self.first:
-            copy.start()
+        self.first[1].start()
+        self.first[2].start()
         self.near.start()
         self.keep.start()
+
+    def start_across(self):
+        self.first[0].start()
+        self.first[3].start()
+
+    def landed(self):
+        self.near.wait_recv()
+        self.keep.wait()
+
+    def landed_relays(self):
+        for copy in self.last:
+            copy.wait_recv()
 
     def forward(self):
         for k in range(2):
@@ -341,19 +415,16 @@
     return out
 
 
-def group_finish(gather, send, receive):
+def group_finish(gather, send, receive, early=False):
     relays = corner_relay(gather, send, receive)
     for k in range(2):
         gather.second[k].wait_recv()
         relays[k].start()
-    gather.keep.wait()
-    gather.near.wait()
-    for copy in gather.first:
+    if not early:
+        gather.landed()
+        gather.landed_relays()
+    for copy in [gather.near] + gather.first + gather.second + gather.last:
         copy.wait_send()
-    for copy in gather.second:
-        copy.wait_send()
-    for copy in gather.last:
-        copy.wait()
     for copy in relays:
         copy.wait()
 
@@ -370,148 +441,145 @@
 
 def first_kernel(count, starts, small_top, *refs):
     loads = len(starts)
-    rows, small = refs[:2]
-    halves, refs = refs[2 : 2 + loads], refs[2 + loads :]
-    everything, everyone, normed, pre = refs[:4]
-    targets, refs = refs[4 : 4 + loads], refs[4 + loads :]
-    incoming, table, weights, incoming_sems, out_sems, weight_sems = refs[:6]
-    sems = refs[6:]
-    dp, tensor = lax.axis_index("dp"), lax.axis_index("tensor")
+    rows = refs[0]
+    halves, refs = refs[1 : 1 + loads], refs[1 + loads :]
+    everything, normed, pre = refs[:3]
+    targets, refs = refs[3 : 3 + loads], refs[3 + loads :]
+    incoming, table, weights, result, tails = refs[:5]
+    incoming_sems, out_sems, weight_sems, result_sems, tail_sem = refs[5:10]
+    sems = refs[10:]
     gather = GroupGather(rows, everything, *sems[:3])
-    corner = sems[3:5]
-    send, receive, local = sems[5:8]
-    freights = load(count, starts, halves, targets, sems[8:])
+    corner_sems = sems[3:5]
+    small, branch, *others = load(count, starts, halves, targets, sems[5:])
     shares = 2 * count
     line, side, deck, core = spot()
-    greet(
-        [((dp + k) % shares, tensor) for k in range(1, shares)]
-        + [seat(line, side, deck, 1 - core), seat(line, side, 1 - deck, core)]
-    )
-    copies = [
-        remote(
-            small.at[(dp + k) % 2],
-            everyone.at[dp],
-            send.at[k],
-            receive.at[k],
-            ((dp + k) % shares, tensor),
-        )
-        for k in range(1, shares)
-    ]
-    copies.append(pltpu.make_async_copy(small.at[side], everyone.at[dp], local))
-    freights[0].start()
+    greet(cargo_peers(count))
+    small.start()
+    branch.start()
     gather.start()
-    for copy in copies:
-        copy.start()
-    for freight in freights[1:]:
-        freight.start()
-    for freight in freights:
-        freight.second()
-    gather.forward()
-    freights[0].forward()
-    group_finish(gather, *corner)
-    for copy in copies:
-        copy.wait()
+    small.second()
+    gather.start_across()
+    small.forward()
+    branch.second()
+    small.finish()
+    tail = pltpu.make_async_copy(targets[0], tails, tail_sem)
+    tail.start()
+    tail.wait()
 
     block_rows, features = rows.shape
-
-    def fetch(g):
-        slot = g % 2
-        return pltpu.make_async_copy(
-            everything.at[g], incoming.at[slot], incoming_sems.at[slot]
-        )
-
     gain = jnp.concatenate(
         [
-            everyone[k, small_top : small_top + 16, : features // shares].astype(F32)[
-                SMALL_GAINS : SMALL_GAINS + 1
-            ]
+            tails[
+                k // 2,
+                (k % 2) * (small_top + 16) + small_top : (k % 2 + 1) * (small_top + 16),
+                : features // shares,
+            ].astype(F32)[SMALL_GAINS : SMALL_GAINS + 1]
             for k in range(shares)
         ],
         axis=1,
     )
-    fetch(0).start()
-    for g in range(8):
-        fetch(g).wait()
-        if g < 7:
-            fetch(g + 1).start()
-
-        def norm_rows(i, carry, g=g):
-            r = pl.multiple_of(i * 32, 32)
-            value = incoming[g % 2, pl.ds(r, 32), :].astype(F32)
-            mean = jnp.mean(value * value, axis=1, keepdims=True)
-            unit = value * lax.rsqrt(mean + EPSILON)
-            table[pl.ds(g * block_rows + r, 32), :] = (unit * gain).astype(BF16)
-            return carry
-
-        lax.fori_loop(0, block_rows // 32, norm_rows, 0)
-        pltpu.make_async_copy(
-            table.at[pl.ds(g * block_rows, block_rows)],
-            normed.at[pl.ds(g * block_rows, block_rows)],
-            out_sems.at[g],
-        ).start()
-    for freight in freights[1:]:
-        freight.forward()
-    freights[0].finish()
-    depth = targets[0].shape[1]
+
+    def block(ref, g):
+        return ref.at[pl.ds(pl.multiple_of(g * block_rows, block_rows), block_rows)]
+
+    def norm_blocks(pair):
+        fetches = [
+            pltpu.make_async_copy(everything.at[g], incoming.at[k], incoming_sems.at[k])
+            for k, g in enumerate(pair)
+        ]
+        for fetch in fetches:
+            fetch.start()
+        for k, g in enumerate(pair):
+            fetches[k].wait()
+
+            def norm_rows(i, carry, k=k, g=g):
+                r = pl.multiple_of(i * 32, 32)
+                value = incoming[k, pl.ds(r, 32), :].astype(F32)
+                mean = jnp.mean(value * value, axis=1, keepdims=True)
+                unit = value * lax.rsqrt(mean + EPSILON)
+                base = pl.multiple_of(g * block_rows + r, 32)
+                table[pl.ds(base, 32), :] = (unit * gain).astype(BF16)
+                return carry
+
+            lax.fori_loop(0, block_rows // 32, norm_rows, 0)
+            pltpu.make_async_copy(block(table, g), block(normed, g), out_sems.at[g]).start()
+
+    def both_cores(s, d):
+        return [rank(s, d, core), rank(s, d, 1 - core)]
+
+    gather.landed()
+    norm_blocks(both_cores(side, deck))
+    gather.forward()
+    branch.forward()
+    for freight in others:
+        freight.start()
+    gather.landed_relays()
+    norm_blocks(both_cores(1 - side, deck))
+    norm_blocks(both_cores(side, 1 - deck))
+    for freight in others:
+        freight.second()
+    group_finish(gather, *corner_sems, early=True)
+    norm_blocks(both_cores(1 - side, 1 - deck))
+    branch.finish()
+    depth = targets[1].shape[1]
     loading = [
         pltpu.make_async_copy(
-            targets[0].at[k], weights.at[pl.ds(k * depth, depth)], weight_sems.at[k]
+            targets[1].at[k], weights.at[pl.ds(k * depth, depth)], weight_sems.at[k]
         )
         for k in range(count)
     ]
     for copy in loading:
         copy.start()
+    for freight in others:
+        freight.forward()
     for copy in loading:
         copy.wait()
     lanes, width = weights.shape[1] // 2, pre.shape[1] // 2
-    shift = lanes - (2 * lanes - width)
+    shift = 2 * lanes - width
     inside = lax.broadcasted_iota(jnp.int32, (CHUNK, width), 1) < lanes
+    writes = Stream(result, pre, result_sems)
 
     def product(r):
         where = pl.ds(r, CHUNK)
         both = jnp.dot(table[where, :], weights[...], preferred_element_type=F32)
-        pre[where, :width] = jnp.where(inside, both[:, :width], 0.0)
-        later = pltpu.roll(both[:, 2 * lanes - width :], width - shift, 1)
-        pre[where, width:] = jnp.where(inside, later, 0.0)
+        result[where, :width] = jnp.where(inside, both[:, :width], 0.0)
+        later = pltpu.roll(both[:, shift:], lanes, 1)
+        result[where, width:] = jnp.where(inside, later, 0.0)
+        writes.start(r)
 
     chunks(pre.shape[0], product)
     for g in range(8):
-        pltpu.make_async_copy(
-            table.at[pl.ds(g * block_rows, block_rows)],
-            normed.at[pl.ds(g * block_rows, block_rows)],
-            out_sems.at[g],
-        ).wait()
-    for freight in freights[1:]:
+        pltpu.make_async_copy(block(table, g), block(normed, g), out_sems.at[g]).wait()
+    writes.wait_all()
+    for freight in others:
         freight.finish()
 
 
-def first(count, rows, small, cargo, width):
-    shares = 2 * count
+def first(count, rows, cargo, width):
     total = 8 * rows.shape[0]
+    small, branch = cargo[:2]
     out = call(
         functools.partial(first_kernel, count, cargo_starts(cargo), small.shape[1] - 16),
         [
             ((8,) + rows.shape, BF16, ANY),
-            ((shares,) + small.shape[1:], BF16, VMEM),
             ((total, rows.shape[1]), BF16, ANY),
-            ((total, 2 * width), F32, VMEM),
+            ((total, 2 * width), F32, ANY),
         ]
         + cargo_outs(count, cargo),
-        [(rows, ANY), (small, ANY)] + cargo_ins(cargo),
+        [(rows, ANY)] + cargo_ins(cargo),
         [
             pltpu.VMEM((2,) + rows.shape, BF16),
             pltpu.VMEM((total, rows.shape[1]), BF16),
-            pltpu.VMEM((rows.shape[1], cargo[0].shape[2]), BF16),
+            pltpu.VMEM((rows.shape[1], branch.shape[2]), BF16),
+            pltpu.VMEM((total, 2 * width), F32),
+            pltpu.VMEM(piece_shape(count, small), BF16),
             pltpu.SemaphoreType.DMA((2,)),
             pltpu.SemaphoreType.DMA((8,)),
             pltpu.SemaphoreType.DMA((count,)),
+            pltpu.SemaphoreType.DMA((total // CHUNK,)),
+            pltpu.SemaphoreType.DMA,
         ]
         + rows_scratch()
-        + [
-            pltpu.SemaphoreType.DMA((shares,)),
-            pltpu.SemaphoreType.DMA((shares,)),
-            pltpu.SemaphoreType.DMA,
-        ]
         + cargo_scratch(count, cargo),
         0,
         "first",
@@ -527,11 +595,12 @@
     gather = GroupGather(rows, everything, *sems[:3])
     freights = load(count, starts, halves, targets, sems[5:])
     greet(cargo_peers(count))
+    for freight in freights:
+        freight.start()
     gather.start()
     for freight in freights:
-        freight.start()
-    for freight in freights:
         freight.second()
+    gather.start_across()
     gather.forward()
     for freight in freights:
         freight.forward()
@@ -556,6 +625,7 @@
     gather = GroupGather(rows, everything, *sems[:3])
     greet(group_peers())
     gather.start()
+    gather.start_across()
     gather.forward()
     group_finish(gather, *sems[3:5])
 
@@ -629,7 +699,8 @@
         self.totals[...] = total
 
 
-def fold_kernel(count, plan, starts, gained, *refs):
+def fold_kernel(count, plan, starts, swaps, *refs):
+    gained = swaps > 0
     loads = len(starts)
     lefts = refs[: plan[-1][0] + 1]
     rights = refs[len(lefts) : len(lefts) + len(plan)]
@@ -637,12 +708,13 @@
     halves, refs = refs[:loads], refs[loads:]
     gains = None
     if gained:
-        gains, refs = refs[0], refs[1:]
+        gains, values, refs = refs[0], refs[1 : 1 + swaps], refs[1 + swaps :]
     out, refs = refs[0], refs[1:]
     targets, refs = refs[:loads], refs[loads:]
     if gained:
-        totals, refs = refs[0], refs[1:]
+        totals, swapped, refs = refs[0], refs[1 : 1 + swaps], refs[1 + swaps :]
         gain_sum = GainSum(count, gains, totals, *refs[-6:])
+        swap = Swap(values, swapped, *refs[-9:-6])
     mine, stage, near, leaving, arriving, refs = *refs[:5], refs[5:]
     send, receive, near_send, near_receive = refs[:4]
     line, side, deck, core = spot()
@@ -651,6 +723,7 @@
     if gained:
         greet(whole_group() + line_peers(count))
         gain_sum.start()
+        swap.start()
     else:
         greet(cargo_peers(count) if loads else group_peers())
     for freight in freights:
@@ -766,6 +839,7 @@
         freight.forward()
     if gained:
         gain_sum.finish()
+        swap.finish()
     for k in range(2, 6):
         ships[k].wait_recv()
 
@@ -785,7 +859,7 @@
         freight.finish()
 
 
-def fold(count, pairs, identity, cargo=(), gains=None):
+def fold(count, pairs, identity, cargo=(), gains=None, swaps=()):
     lefts, rights, plan = [], [], []
     for k, (left, parts) in enumerate(pairs):
         lefts.append(left)
@@ -814,9 +888,12 @@
     if gains is not None:
         outs.append((gains.shape, F32, VMEM))
         ins.append((gains, VMEM))
+        outs += [(value.shape, BF16, ANY) for value in swaps]
+        ins += [(value, ANY) for value in swaps]
+        scratch += Swap.scratch(swaps)
         scratch += GainSum.scratch(count, gains)
     out = call(
-        functools.partial(fold_kernel, count, plan, cargo_starts(cargo), gains is not None),
+        functools.partial(fold_kernel, count, plan, cargo_starts(cargo), len(swaps)),
         outs,
         ins,
         scratch,
@@ -940,14 +1017,30 @@
     loads = len(starts)
     pre, masks, table, gate_weights, cotangent = refs[:5]
     halves, refs = refs[5 : 5 + loads], refs[5 + loads :]
-    conv, recur_out, admit_out, state, merged, entry, everything = refs[:7]
-    targets, refs = refs[7 : 7 + loads], refs[7 + loads :]
-    prods, sums, halo, outgoing, slots, edge_sems, send, receive = refs[:8]
-    sems = refs[8:]
+    everything, targets, refs = refs[6], refs[7 : 7 + loads], refs[:6] + refs[7 + loads :]
+    saved, refs = refs[:6], refs[6:]
+    gate, entry, conv, recur_out, admit_out, state, merged = refs[:7]
+    prods, sums, halo, outgoing, slots, edge_sems, send, receive = refs[7:15]
+    in_sems, out_sems, head_sems = refs[15:18]
+    sems = refs[18:]
     line, side, deck, core = spot()
     rows, width = conv.shape
     gather = GroupGather(cotangent, everything, *sems[:3])
     freights = load(count, starts, halves, targets, sems[5:])
+    gate_reads = Stream(pre, gate, in_sems.at[0], columns=pl.ds(0, width))
+    entry_reads = Stream(pre, entry, in_sems.at[1], to_row=8, columns=pl.ds(width, width))
+    conv_writes = Stream(conv, saved[0], out_sems.at[0])
+    recur_writes = Stream(recur_out, saved[1], out_sems.at[1])
+    admit_writes = Stream(admit_out, saved[2], out_sems.at[2])
+    state_writes = Stream(state, saved[3], out_sems.at[3], 8, 8)
+    merged_writes = Stream(merged, saved[4], out_sems.at[4])
+    entry_writes = Stream(entry, saved[5], out_sems.at[5], 8, 8)
+    heads = [
+        pltpu.make_async_copy(local.at[pl.ds(0, 8)], away.at[pl.ds(0, 8)], head_sems.at[k])
+        for k, (local, away) in enumerate([(state, saved[3]), (entry, saved[5])])
+    ]
+    entry_reads.start_all()
+    gate_reads.start_all()
     greet(cargo_peers(count))
 
     def edge(place):
@@ -967,11 +1060,6 @@
         freight.start()
     gather.start()
 
-    def copy_entry(r):
-        entry[pl.ds(r + 8, CHUNK), :] = pre[pl.ds(r, CHUNK), width:]
-
-    chunks(rows, copy_entry)
-
     @pl.when(line > 0)
     def _():
         edge(line - 1).wait_recv()
@@ -985,7 +1073,10 @@
     def _():
         edge(line + 1).wait_send()
 
+    heads[1].start()
+
     def gate_chunk(r):
+        entry_reads.wait(r)
         wide = entry[pl.ds(r, CHUNK + 8), :]
         mask = masks[pl.ds(r, CHUNK), :]
         value = table[0:1, :] * wide[8:, :]
@@ -1005,26 +1096,45 @@
         norm = root * opened + (1.0 - opened)
         prods[where, :] = decay * opened
         sums[where, :] = norm * admit * value
-
-    spans(0, rows // CHUNK // 2, gate_chunk)
+        for stream in (entry_writes, conv_writes, recur_writes, admit_writes):
+            stream.start(r)
+
+    pieces = rows // CHUNK
+    spans(0, pieces // 4, gate_chunk)
     for freight in freights:
         freight.second()
-    spans(rows // CHUNK // 2, rows // CHUNK, gate_chunk)
+    gather.start_across()
+    spans(pieces // 4, pieces, gate_chunk)
+    prod, total = tile_scan(prods, sums, rows, width, False)
     gather.forward()
-    prod, total = tile_scan(prods, sums, rows, width, False)
     entering = pool(count, prod, total, outgoing, slots, send, receive, False)
     for freight in freights:
         freight.forward()
     state[0:8, :] = entering
+    heads[0].start()
 
     def state_chunk(r):
+        gate_reads.wait(r)
         where = pl.ds(r, CHUNK)
         value = sums[where, :] + prods[where, :] * entering[0:1, :]
         state[pl.ds(r + 8, CHUNK), :] = value
-        act, _ = gelu_both(pre[where, :width])
+        act, _ = gelu_both(gate[where, :])
         merged[where, :] = (value * act).astype(BF16)
+        state_writes.start(r)
+        merged_writes.start(r)
 
     chunks(rows, state_chunk)
+    for stream in (
+        entry_writes,
+        conv_writes,
+        recur_writes,
+        admit_writes,
+        state_writes,
+        merged_writes,
+    ):
+        stream.wait_all()
+    for copy in heads:
+        copy.wait()
     group_finish(gather, *sems[3:5])
     for freight in freights:
         freight.finish()
@@ -1032,21 +1142,31 @@
 
 def scan_forward(count, pre, masks, table, gate_weights, cotangent, cargo):
     rows, width = pre.shape[0], pre.shape[1] // 2
+    pieces = rows // CHUNK
+    tall = (rows + 8, width)
+    saved = [
+        ((rows, width), F32),
+        ((rows, width), F32),
+        ((rows, width), F32),
+        (tall, F32),
+        ((rows, width), BF16),
+        (tall, F32),
+    ]
     out = call(
         functools.partial(scan_kernel, count, cargo_starts(cargo)),
-        [
-            ((rows, width), F32, VMEM),
-            ((rows, width), F32, VMEM),
-            ((rows, width), F32, VMEM),
-            ((rows + 8, width), F32, VMEM),
-            ((rows, width), BF16, VMEM),
-            ((rows + 8, width), F32, VMEM),
-            ((8,) + cotangent.shape, BF16, ANY),
-        ]
+        [(shape, kind, ANY) for shape, kind in saved]
+        + [((8,) + cotangent.shape, BF16, ANY)]
         + cargo_outs(count, cargo),
-        [(pre, VMEM), (masks, VMEM), (table, VMEM), (gate_weights, VMEM), (cotangent, ANY)]
+        [(pre, ANY), (masks, VMEM), (table, VMEM), (gate_weights, VMEM), (cotangent, ANY)]
         + cargo_ins(cargo),
         [
+            pltpu.VMEM((rows, width), F32),
+            pltpu.VMEM(tall, F32),
+            pltpu.VMEM((rows, width), F32),
+            pltpu.VMEM((rows, width), F32),
+            pltpu.VMEM((rows, width), F32),
+            pltpu.VMEM(tall, F32),
+            pltpu.VMEM((rows, width), BF16),
             pltpu.VMEM((rows, width), F32),
             pltpu.VMEM((rows, width), F32),
             pltpu.VMEM((8, width), F32),
@@ -1055,6 +1175,9 @@
             pltpu.SemaphoreType.DMA((2,)),
             pltpu.SemaphoreType.DMA((count,)),
             pltpu.SemaphoreType.DMA((count,)),
+            pltpu.SemaphoreType.DMA((2, pieces)),
+            pltpu.SemaphoreType.DMA((6, pieces)),
+            pltpu.SemaphoreType.DMA((2,)),
         ]
         + rows_scratch()
         + cargo_scratch(count, cargo),
@@ -1064,50 +1187,77 @@
     return out[:6] + [out[6].reshape(-1, cotangent.shape[1])] + flat_rows(out[7:])
 
 
-def back_kernel(
-    count,
-    pre,
-    grad_merged,
-    conv,
-    recur_in,
-    admit_in,
-    state,
-    entry,
-    masks,
-    table,
-    gate_weights,
-    grad_pre,
-    grad_gates,
-    grad_table,
-    prods,
-    sums,
-    mixes,
-    outgoing,
-    slots,
-    edge_sems,
-    send,
-    receive,
-):
+def back_kernel(count, lanes, swaps, *refs):
+    pre, low, outlet = refs[:3]
+    saved, refs = refs[3:8], refs[8:]
+    masks, table, gate_weights = refs[:3]
+    values, refs = refs[3 : 3 + swaps], refs[3 + swaps :]
+    grad_pre, grad_gates, grad_table = refs[:3]
+    swapped, refs = refs[3 : 3 + swaps], refs[3 + swaps :]
+    gate, conv, recur_in, admit_in, state, entry, lows = refs[:7]
+    prods, sums, mixes, outgoing, slots, edge_sems, send, receive = refs[7:15]
+    in_sems, low_sems, head_sems = refs[15:18]
     line, side, deck, core = spot()
     rows, width = conv.shape
-    greet(line_peers(count))
-
-    def direct_chunk(r):
+    pieces = rows // CHUNK
+    swap = Swap(values, swapped, *refs[18:])
+    conv_reads = Stream(saved[0], conv, in_sems.at[0])
+    recur_reads = Stream(saved[1], recur_in, in_sems.at[1])
+    admit_reads = Stream(saved[2], admit_in, in_sems.at[2])
+    state_reads = Stream(saved[3], state, in_sems.at[3], 8, 8)
+    entry_reads = Stream(saved[4], entry, in_sems.at[4], 8, 8)
+    gate_reads = Stream(pre, gate, in_sems.at[5], columns=pl.ds(0, width))
+    heads = [
+        pltpu.make_async_copy(away.at[pl.ds(0, 8)], local.at[pl.ds(0, 8)], head_sems.at[k])
+        for k, (local, away) in enumerate([(state, saved[3]), (entry, saved[4])])
+    ]
+
+    def fetch(i):
+        slot = i % 2
+        start = pl.multiple_of(i * CHUNK, CHUNK)
+        return pltpu.make_async_copy(
+            low.at[pl.ds(start, CHUNK)], lows.at[slot], low_sems.at[slot]
+        )
+
+    fetch(0).start()
+    for k in range(pieces):
+        for stream in (gate_reads, recur_reads, state_reads):
+            stream.start(k * CHUNK)
+    for copy in heads:
+        copy.start()
+    for stream in (conv_reads, admit_reads, entry_reads):
+        stream.start_all()
+    greet(line_peers(count) + ([seat(line, 1 - side, deck, core)] if swaps else []))
+    swap.start()
+
+    def direct(i, carry):
+        r = pl.multiple_of(i * CHUNK, CHUNK)
+
+        @pl.when(i + 1 < pieces)
+        def _():
+            fetch(i + 1).start()
+
+        fetch(i).wait()
+        for stream in (gate_reads, recur_reads, state_reads):
+            stream.wait(r)
         where = pl.ds(r, CHUNK)
-        act, slope = gelu_both(pre[where, :width])
-        grad = grad_merged[where, :]
-        grad_pre[where, :width] = (grad * state[pl.ds(r + 8, CHUNK), :] * slope).astype(BF16)
-        direct = grad * act
-        carry = jnp.exp(-8.0 * recur_in[where, :] * table[4:5, :]) * masks[where, 3:4]
-        mixes[where, :] = direct
-        prods[where, :] = carry
-        sums[where, :] = carry * direct
-
-    chunks(rows, direct_chunk)
+        grad = jnp.dot(lows[i % 2], outlet[...], preferred_element_type=F32)
+        act, slope = gelu_both(gate[where, :])
+        gate[where, :] = grad * state[pl.ds(r + 8, CHUNK), :] * slope
+        straight = grad * act
+        carried = jnp.exp(-8.0 * recur_in[where, :] * table[4:5, :]) * masks[where, 3:4]
+        mixes[where, :] = straight
+        prods[where, :] = carried
+        sums[where, :] = carried * straight
+        return carry
+
+    lax.fori_loop(0, pieces, direct, 0)
     prods[rows : rows + 8, :] = jnp.ones((8, width), F32)
     sums[rows : rows + 8, :] = jnp.zeros((8, width), F32)
     prod, total = tile_scan(prods, sums, rows, width, True)
     entering = pool(count, prod, total, outgoing, slots, send, receive, True)
+    for copy in heads:
+        copy.wait()
     grad_gates[...] = jnp.zeros_like(grad_gates)
     grad_table[...] = jnp.zeros_like(grad_table)
 
@@ -1115,6 +1265,8 @@
         return jnp.sum(value, axis=0, keepdims=True)
 
     def gate_chunk(r):
+        conv_reads.wait(r)
+        admit_reads.wait(r)
         where = pl.ds(r, CHUNK)
         wide = pl.ds(r, CHUNK + 8)
         later = sums[wide, :] + prods[wide, :] * entering[0:1, :]
@@ -1153,11 +1305,7 @@
     def _():
         edge(line - 1).start()
 
-    def other(i, carry):
-        gate_chunk(pl.multiple_of(i * CHUNK, CHUNK))
-        return carry
-
-    lax.fori_loop(1, rows // CHUNK, other, 0)
+    spans(1, pieces, gate_chunk)
 
     @pl.when(line < count - 1)
     def _():
@@ -1167,7 +1315,11 @@
     def _():
         mixes[rows : rows + 8, :] = jnp.zeros((8, width), F32)
 
+    spare = width - lanes
+    shift = 2 * lanes - width
+
     def entry_chunk(r):
+        entry_reads.wait(r)
         where, wide = pl.ds(r, CHUNK), pl.ds(r, CHUNK + 8)
         ahead, mask = mixes[wide, :], masks[where, :]
         source = entry[wide, :]
@@ -1179,7 +1331,12 @@
             grad_table[k : k + 1, :] += fold_rows(
                 here * source[8 - k : 8 - k + CHUNK, :] * mask[:, k - 1 : k]
             )
-        grad_pre[where, width:] = total.astype(BF16)
+        total = pltpu.roll(total, spare, 1)
+        first = gate[where, :]
+        middle = first[:, shift:] + total[:, : width - shift]
+        grad_pre[where, :shift] = first[:, :shift].astype(BF16)
+        grad_pre[where, shift:width] = middle.astype(BF16)
+        grad_pre[where, width:] = total[:, width - shift :].astype(BF16)
 
     chunks(rows, entry_chunk)
 
@@ -1187,76 +1344,108 @@
     def _():
         edge(line - 1).wait_send()
 
-
-def scan_backward(count, pre, grad_merged, saved, masks, table, gate_weights):
-    rows, width = grad_merged.shape
-    values = [pre, grad_merged, *saved, masks, table, gate_weights]
+    swap.finish()
+
+
+def scan_backward(count, lanes, pre, low, outlet, saved, masks, table, gate_weights, swaps):
+    rows, width = pre.shape[0], pre.shape[1] // 2
+    pieces = rows // CHUNK
+    tall = (rows + 8, width)
     return call(
-        functools.partial(back_kernel, count),
+        functools.partial(back_kernel, count, lanes, len(swaps)),
         [
-            ((rows, 2 * width), BF16, VMEM),
+            ((rows, 2 * lanes), BF16, VMEM),
             ((width, 2 * width), F32, VMEM),
             ((8, width), F32, VMEM),
-        ],
-        [(value, VMEM) for value in values],
+        ]
+        + [(value.shape, BF16, ANY) for value in swaps],
+        [(pre, ANY), (low, ANY), (outlet, VMEM)]
+        + [(value, ANY) for value in saved]
+        + [(value, VMEM) for value in (masks, table, gate_weights)]
+        + [(value, ANY) for value in swaps],
         [
-            pltpu.VMEM((rows + 8, width), F32),
-            pltpu.VMEM((rows + 8, width), F32),
-            pltpu.VMEM((rows + 8, width), F32),
+            pltpu.VMEM((rows, width), F32),
+            pltpu.VMEM((rows, width), F32),
+            pltpu.VMEM((rows, width), F32),
+            pltpu.VMEM((rows, width), F32),
+            pltpu.VMEM(tall, F32),
+            pltpu.VMEM(tall, F32),
+            pltpu.VMEM((2, CHUNK, low.shape[1]), BF16),
+            pltpu.VMEM(tall, F32),
+            pltpu.VMEM(tall, F32),
+            pltpu.VMEM(tall, F32),
             pltpu.VMEM((16, width), F32),
             pltpu.VMEM((count, 16, width), F32),
             pltpu.SemaphoreType.DMA((2,)),
             pltpu.SemaphoreType.DMA((count,)),
             pltpu.SemaphoreType.DMA((count,)),
-        ],
+            pltpu.SemaphoreType.DMA((6, pieces)),
+            pltpu.SemaphoreType.DMA((2,)),
+            pltpu.SemaphoreType.DMA((2,)),
+        ]
+        + Swap.scratch(swaps),
         7,
         "scan_backward",
     )
 
 
-def feed_kernel(count, early, starts, normed, cotangent, *refs):
+def feed_kernel(count, early, starts, *refs):
     loads = len(starts)
-    gate_parts, refs = refs[:2], refs[2:]
-    up_parts, refs = refs[:2], refs[2:]
-    down_parts, refs = refs[:early], refs[early:]
+    normed, cotangent = refs[:2]
+    gate_parts, up_parts, down_parts = refs[2:4], refs[4:6], refs[6 : 6 + early]
+    refs = refs[6 + early :]
     halves, refs = refs[:loads], refs[loads:]
-    hidden, grad_gating, grad_lifting = refs[:3]
-    targets, refs = refs[3 : 3 + loads], refs[3 + loads :]
-    table, acts, slopes, down, sems = *refs[:4], refs[4:]
-    table_sem, down_sems = sems[:2]
-    freights = load(count, starts, halves, targets, sems[2:])
+    results, targets, refs = refs[:3], refs[3 : 3 + loads], refs[3 + loads :]
+    table, gate_up, acts, slopes, down, hidden, grad_gating, grad_lifting = refs[:8]
+    table_sems, back_sems, write_sems, weight_sems, down_sems = refs[8:13]
+    freights = load(count, starts, halves, targets, refs[13:])
+    rows, width = hidden.shape
+    pieces = rows // CHUNK
+    reads = Stream(normed, table, table_sems)
+    again = Stream(cotangent, table, back_sems)
+    writes = [
+        Stream(local, away, write_sems.at[k])
+        for k, (local, away) in enumerate(zip((hidden, grad_gating, grad_lifting), results))
+    ]
+    weights = []
+    for which, parts in enumerate((gate_parts, up_parts)):
+        start = 0
+        for part in parts:
+            weights.append(
+                pltpu.make_async_copy(
+                    part,
+                    gate_up.at[which, :, pl.ds(start, part.shape[1])],
+                    weight_sems.at[len(weights)],
+                )
+            )
+            start += part.shape[1]
+    for copy in weights:
+        copy.start()
+    reads.start_all()
     greet(cargo_peers(count))
     for freight in freights:
         freight.start()
-    rows, width = hidden.shape
-    pieces = rows // CHUNK
-    first = pltpu.make_async_copy(normed, table, table_sem)
-    first.start()
-    first.wait()
+    for copy in weights:
+        copy.wait()
 
     def forward_chunk(r):
+        reads.wait(r)
         where = pl.ds(r, CHUNK)
-        start = 0
-        for gate_part, up_part in zip(gate_parts, up_parts):
-            columns = slice(start, start + gate_part.shape[1])
-            gating = jnp.dot(table[where, :], gate_part[...], preferred_element_type=F32)
-            lifting = jnp.dot(table[where, :], up_part[...], preferred_element_type=F32)
-            act, slope = gelu_both(gating)
-            hidden[where, columns] = (act * lifting).astype(BF16)
-            acts[where, columns] = act
-            slopes[where, columns] = lifting * slope
-            start += gate_part.shape[1]
+        gating = jnp.dot(table[where, :], gate_up[0], preferred_element_type=F32)
+        lifting = jnp.dot(table[where, :], gate_up[1], preferred_element_type=F32)
+        act, slope = gelu_both(gating)
+        hidden[where, :] = (act * lifting).astype(BF16)
+        acts[where, :] = act
+        slopes[where, :] = lifting * slope
+        writes[0].start(r)
+        again.start(r)
 
     spans(0, pieces // 4, forward_chunk)
     for freight in freights:
         freight.second()
     spans(pieces // 4, pieces, forward_chunk)
-    second = pltpu.make_async_copy(cotangent, table, table_sem)
-    second.start()
     for freight in freights:
         freight.forward()
-    for freight in freights:
-        freight.finish()
     rows_in = down.shape[0] // count
     copies, start = [], 0
     for k, part in enumerate(down_parts):
@@ -1276,39 +1465,61 @@
                 )
             )
         start += target.shape[2]
-    for copy in copies:
-        copy.start()
-    second.wait()
-    for copy in copies:
-        copy.wait()
-
-    def back_chunk(r):
-        where = pl.ds(r, CHUNK)
-        for start in range(0, width, width // 3):
-            columns = slice(start, start + width // 3)
+
+    def back(low, high):
+        def chunk(r):
+            where = pl.ds(r, CHUNK)
+            columns = slice(low, high)
             grad = jnp.dot(table[where, :], down[:, columns], preferred_element_type=F32)
             grad_gating[where, columns] = (grad * slopes[where, columns]).astype(BF16)
             grad_lifting[where, columns] = (grad * acts[where, columns]).astype(BF16)
-
-    chunks(rows, back_chunk)
+            if high == width:
+                writes[1].start(r)
+                writes[2].start(r)
+
+        chunks(rows, chunk)
+
+    for copy in copies[:early]:
+        copy.start()
+    again.wait_all()
+    for copy in copies[:early]:
+        copy.wait()
+    ready = sum(part.shape[1] for part in down_parts)
+    back(0, ready)
+    for freight in freights:
+        freight.finish()
+    for copy in copies[early:]:
+        copy.start()
+    for copy in copies[early:]:
+        copy.wait()
+    back(ready, width)
+    for stream in writes:
+        stream.wait_all()
 
 
 def feed(count, normed, cotangent, gate_parts, up_parts, down_parts, cargo):
     rows = normed.shape[0]
     width = sum(part.shape[1] for part in gate_parts)
+    pieces = rows // CHUNK
     out = call(
         functools.partial(feed_kernel, count, len(down_parts), cargo_starts(cargo)),
-        [((rows, width), BF16, VMEM)] * 3 + cargo_outs(count, cargo),
+        [((rows, width), BF16, ANY)] * 3 + cargo_outs(count, cargo),
         [(normed, ANY), (cotangent, ANY)]
-        + [(part, VMEM) for part in list(gate_parts) + list(up_parts)]
-        + [(part, ANY) for part in down_parts]
+        + [(part, ANY) for part in list(gate_parts) + list(up_parts) + list(down_parts)]
         + cargo_ins(cargo),
         [
             pltpu.VMEM(normed.shape, BF16),
+            pltpu.VMEM((2, normed.shape[1], width), BF16),
             pltpu.VMEM((rows, width), F32),
             pltpu.VMEM((rows, width), F32),
             pltpu.VMEM((normed.shape[1], width), BF16),
-            pltpu.SemaphoreType.DMA,
+            pltpu.VMEM((rows, width), BF16),
+            pltpu.VMEM((rows, width), BF16),
+            pltpu.VMEM((rows, width), BF16),
+            pltpu.SemaphoreType.DMA((pieces,)),
+            pltpu.SemaphoreType.DMA((pieces,)),
+            pltpu.SemaphoreType.DMA((3, pieces)),
+            pltpu.SemaphoreType.DMA((4,)),
             pltpu.SemaphoreType.DMA((len(down_parts) + count * len(cargo),)),
         ]
         + cargo_scratch(count, cargo),
@@ -1384,49 +1595,32 @@
     broad = 2 * narrow
 
     mine = lax.axis_index("dp")
-    blocks = jnp.concatenate(
-        [
-            jnp.stack(
-                [
-                    jnp.pad(
-                        jnp.concatenate(
-                            [
-                                widen(jnp.pad(rate_gate[h], ((0, 0), (p, 0))), width),
-                                widen(jnp.pad(input_gate[h], ((0, 0), (p, 0))), width),
-                            ],
-                            axis=1,
-                        ),
-                        ((0, 0), (0, 0)),
-                    )
-                    for h, p in [(s * half_heads + k, k * head_width) for k in range(half_heads)]
-                ]
-            ).reshape(1, half_heads * piece, 2 * width)
-            for s in range(2)
-        ]
-    )
+    blocks = jnp.concatenate([rate_gate, input_gate], axis=2)
+    blocks = widen(blocks.reshape(2, half_heads * piece, 2 * head_width), width)
     own = jnp.concatenate([conv_taps, decay_param[None]], axis=0)
     own = jnp.pad(own, ((0, 0), (0, 0), (0, head_width - piece)))
     own = jnp.roll(own, mine * piece, axis=2)
     own = own.reshape(TAPS + 1, 2, lanes).transpose(1, 0, 2)
     gains_own = jnp.pad(
-        jnp.stack([mixer_gain, feed_gain]), ((0, 16 - TAPS - 3), (0, 2 * width - slim))
+        jnp.stack([mixer_gain, feed_gain]), ((0, 16 - TAPS - 3), (0, width - slim))
     )
     tail = jnp.concatenate(
-        [widen(own, 2 * width), jnp.broadcast_to(gains_own, (2,) + gains_own.shape)], axis=1
+        [widen(own, width), jnp.broadcast_to(gains_own, (2,) + gains_own.shape)], axis=1
     )
     small_top = -(-half_heads * piece // 16) * 16
     small = jnp.concatenate(
         [jnp.pad(blocks, ((0, 0), (0, small_top - half_heads * piece), (0, 0))), tail], axis=1
     )
 
-    small_all, normed_one, pre, branch_all, gate_first = first(
-        count, layer_input, small, [branch_halves, (feed_gate, 0, narrow)], width
-    )
-
+    normed_one, pre, small_all, branch_all, gate_first = first(
+        count, layer_input, [small, branch_halves, (feed_gate, 0, narrow)], width
+    )
+
+    small_all = small_all.reshape(shares, -1, width)
     tails = small_all[:, small_top:].astype(F32)
     gain_first = tails[:, SMALL_GAINS, :slim].reshape(feature_count)
     gain_second = tails[:, SMALL_GAINS + 1, :slim].reshape(feature_count)
-    sums = jnp.sum(tails[:, : TAPS + 1, :width], axis=0)
+    sums = jnp.sum(tails[:, : TAPS + 1], axis=0)
     decay_flat = sums[TAPS, :lanes]
     inside = (jnp.arange(width) < lanes)[None]
     table = jnp.concatenate(
@@ -1436,11 +1630,21 @@
             jnp.zeros((3, width), F32),
         ]
     )
-    gate_weights = (
-        small_all[:, : half_heads * piece]
-        .reshape(shares, half_heads, piece, 2 * width)
+    blocks = (
+        small_all[:, : half_heads * piece, : 2 * head_width]
+        .reshape(shares, half_heads, piece, 2 * head_width)
         .transpose(1, 0, 2, 3)
-        .reshape(lanes, 2 * width)
+        .reshape(lanes, 2 * head_width)
+    )
+    head_of = jnp.arange(width) // head_width
+    same = (head_of[:lanes, None] == head_of[None, :]) & (jnp.arange(width) < lanes)[None]
+
+    def diagonal(part):
+        wide = widen(jnp.concatenate([part] * half_heads, axis=1), width)
+        return jnp.where(same, wide, 0)
+
+    gate_weights = jnp.concatenate(
+        [diagonal(blocks[:, :head_width]), diagonal(blocks[:, head_width:])], axis=1
     )
     gate_weights = jnp.pad(gate_weights, ((0, width - lanes), (0, 0)))
 
@@ -1455,9 +1659,6 @@
 
     residual = layer_input.astype(F32)
     unit_one, scale_one = unit_norm(residual)
-    branch_wide = jnp.concatenate(
-        [widen(branch_all[:, :lanes], width), widen(branch_all[:, lanes:], width)], axis=1
-    )
     conv, recur, admit, state, merged, entry, cot_all, mixer_all, up_first = scan_forward(
         count, pre, masks, table, gate_weights, out_grad, [mixer_halves, (feed_up, 0, narrow)]
     )
@@ -1497,37 +1698,26 @@
     grad_hidden_one, down_sum = lax.optimization_barrier((grad_hidden_one, down_sum))
     back_low = gather_plain(grad_hidden_one.astype(BF16), 8)
     outlet_grads = by_rows(back_low, merged)
-    grad_merged = jnp.dot(back_low, mixer_all, preferred_element_type=F32)
-    grad_merged, outlet_grads, gate_sum = lax.optimization_barrier(
-        (grad_merged, outlet_grads, gate_sum)
-    )
-    outlet_sum = line_sum(outlet_grads)
-    grad_pre, grad_gates, grad_table = scan_backward(
-        count, pre, grad_merged, [conv, recur, admit, state, entry], masks, table, gate_weights
+
+    def by_side(value):
+        return value.reshape(2, -1, value.shape[1])
+
+    back_low, outlet_grads, gate_sum = lax.optimization_barrier(
+        (back_low, outlet_grads, gate_sum)
+    )
+    grad_pre, grad_gates, grad_table, down_both, gate_both = scan_backward(
+        count,
+        lanes,
+        pre,
+        back_low,
+        mixer_all,
+        [conv, recur, admit, state, entry],
+        masks,
+        table,
+        gate_weights,
+        [by_side(down_sum), by_side(gate_sum)],
     )
     branch_grads = by_rows(normed_one, grad_pre)
-    branch_grads = jnp.concatenate(
-        [branch_grads[:, :lanes], branch_grads[:, width : width + lanes]], axis=1
-    )
-    grad_pre, branch_grads = lax.optimization_barrier((grad_pre, branch_grads))
-    branch_sum = line_sum(branch_grads)
-    grad_normed_one = fold(count, [(grad_pre, [branch_wide])], 10)[0]
-    hidden, grad_normed_one, up_sum = lax.optimization_barrier(
-        (hidden, grad_normed_one, up_sum)
-    )
-    gains = jnp.concatenate(
-        [
-            jnp.sum(grad_normed_one * unit_one, axis=0).reshape(shares, slim),
-            jnp.sum(grad_normed_two * unit_two, axis=0).reshape(shares, slim),
-        ]
-    )
-    feed_own, gains = fold(count, [(hidden, down_parts)], 9, gains=gains)
-    first_gain_grad = lax.dynamic_index_in_dim(gains, mine, 0, False)
-    second_gain_grad = lax.dynamic_index_in_dim(gains, shares + mine, 0, False)
-    layer_output = (hidden_one + feed_own).astype(BF16)
-    input_grad = (
-        grad_hidden_one + norm_back(grad_normed_one * gain_first, unit_one, scale_one)
-    ).astype(BF16)
 
     def spots(value):
         blocks = [
@@ -1552,29 +1742,47 @@
         axis=1,
     )
     flat_size = grad_small.shape[1]
-    small_rows = -(-flat_size // (128 * 16)) * 16
-    grad_small = widen(grad_small, small_rows * 128).reshape(shares * small_rows, 128)
-    small_sum = line_sum(grad_small.astype(BF16)).astype(F32)
-
-    def swap(value):
-        pair = value.reshape(2, -1, value.shape[1])
-        kept = lax.dynamic_index_in_dim(pair, side, 0, False)
-        given = lax.dynamic_index_in_dim(pair, 1 - side, 0, False)
-        other = lax.ppermute(given, "dp", [(k, k ^ 1) for k in range(shares)])
-        first = jnp.where(side == 0, kept, other).astype(F32)
-        second = jnp.where(side == 0, other, kept).astype(F32)
-        return first, second
-
-    def joined(value):
-        return jnp.concatenate(swap(value), axis=1)
-
-    branch_first, branch_second = swap(branch_sum)
-    branch_gate_grad = jnp.concatenate([branch_first[:, :lanes], branch_second[:, :lanes]], axis=1)
-    branch_input_grad = jnp.concatenate([branch_first[:, lanes:], branch_second[:, lanes:]], axis=1)
-    outlet_first, outlet_second = swap(outlet_sum)
-    mixer_out_grad = jnp.concatenate([outlet_first[:, :lanes], outlet_second[:, :lanes]], axis=1).T
-
-    smalls = [value.reshape(-1)[:flat_size] for value in swap(small_sum.astype(BF16))]
+    spare = width - lanes
+    grad_small = widen(grad_small, slim * spare).reshape(feature_count, spare).astype(BF16)
+    last_grads = jnp.concatenate([outlet_grads[:, :lanes], grad_small, branch_grads], axis=1)
+    grad_pre, last_grads = lax.optimization_barrier((grad_pre, last_grads))
+    last_sum = line_sum(last_grads)
+    grad_normed_one = fold(count, [(grad_pre, [branch_all])], 10)[0]
+    hidden, grad_normed_one, up_sum = lax.optimization_barrier(
+        (hidden, grad_normed_one, up_sum)
+    )
+    gains = jnp.concatenate(
+        [
+            jnp.sum(grad_normed_one * unit_one, axis=0).reshape(shares, slim),
+            jnp.sum(grad_normed_two * unit_two, axis=0).reshape(shares, slim),
+        ]
+    )
+    feed_own, gains, up_both = fold(
+        count, [(hidden, down_parts)], 9, gains=gains, swaps=[by_side(up_sum)]
+    )
+    first_gain_grad = lax.dynamic_index_in_dim(gains, mine, 0, False)
+    second_gain_grad = lax.dynamic_index_in_dim(gains, shares + mine, 0, False)
+    layer_output = (hidden_one + feed_own).astype(BF16)
+    input_grad = (
+        grad_hidden_one + norm_back(grad_normed_one * gain_first, unit_one, scale_one)
+    ).astype(BF16)
+
+    pair = by_side(last_sum)
+    kept = lax.dynamic_index_in_dim(pair, side, 0, False)
+    given = lax.dynamic_index_in_dim(pair, 1 - side, 0, False)
+    other = lax.ppermute(given, "dp", [(k, k ^ 1) for k in range(shares)])
+    lasts = [
+        jnp.where(side == 0, kept, other).astype(F32),
+        jnp.where(side == 0, other, kept).astype(F32),
+    ]
+
+    def columns(start, stop):
+        return jnp.concatenate([value[:, start:stop] for value in lasts], axis=1)
+
+    mixer_out_grad = columns(0, lanes).T
+    branch_gate_grad = columns(width, width + lanes)
+    branch_input_grad = columns(width + lanes, width + 2 * lanes)
+    smalls = [value[:, lanes:width].reshape(-1)[:flat_size] for value in lasts]
     one = half_heads * piece * head_width
     tap_size = TAPS * half_heads * piece
     rate_grad = jnp.concatenate([v[:one].reshape(half_heads, piece, head_width) for v in smalls])
@@ -1587,6 +1795,10 @@
     decay_grad = jnp.concatenate(
         [v[2 * one + tap_size :].reshape(half_heads, piece) for v in smalls]
     )
+
+    def joined(value):
+        return jnp.concatenate([value[0], value[1]], axis=1).astype(F32)
+
     return (
         layer_output,
         input_grad,
@@ -1599,9 +1811,9 @@
         decay_grad,
         mixer_out_grad,
         second_gain_grad,
-        joined(gate_sum),
-        joined(up_sum),
-        joined(down_sum).T,
+        joined(gate_both),
+        joined(up_both),
+        joined(down_both).T,
     )
 
 

time: 747 us -> 695 us (0.930)
  Pallas kernels: 548 us -> 529 us
  local copies, waits for them, and re-layouts: 46.6 us -> 29.2 us
  waiting for transfers between devices: 12.1 us -> 24.4 us
  other arithmetic: 49 us -> 37 us
  matrix products: 63.5 us -> 52.9 us
    pallas_call x10, Pallas kernels: 548 us -> 529 us  [call(): pl.pallas_call(kernel, out_shape=[jax.ShapeDtypeStruct(shape, kind) for s...]
    dynamic_slice x15 -> x0, local copies, waits for them, and re-layouts: 16.7 us -> none  [the longest x10 9.93 us: swap(): kept = lax.dynamic_index_in_dim(pair, side, 0, False)]
    dot_general x1 -> x0, matrix products: 10 us -> none  [shards(): grad_merged = jnp.dot(back_low, mixer_all, preferred_element_type=F32)]
    reduce_scatter x6 -> x4, waiting for transfers between devices: 4.11 us -> 13.6 us  [line_sum(): lax.psum_scatter(value, 'dp', scatter_dimension=0, axis_index_groups=line...]
  transfers between devices with their start and end apart: 12 -> 5, of which waited for: 3 -> 3; matrix products, arithmetic and copies ran while one was open for 14% -> 8% of each run, Pallas kernels for 30% -> 34%
where the time goes in v3:
time: 695 us; the launch traced here: 689 us
  Pallas kernels  529 us (76%)
  matrix products  52.9 us (8%)
  other arithmetic  37 us (5%)
  local copies, waits for them, and re-layouts  29.2 us (4%)
  waiting for transfers between devices  24.4 us (4%)
  between operations  14.7 us (2%)
    pallas_call x10, Pallas kernels, call(): pl.pallas_call(kernel, out_shape=[jax.ShapeDtypeStruct(shape, kind) for s...  529 us
    dot_general x5, matrix products, by_rows(): lax.dot_general(left, right, TN, preferred_element_type=F32).astype(BF16)  52.9 us
  transfers between devices with their start and end apart: 5, of which 3 were waited for; matrix products, arithmetic and copies ran while one was open for 8% of the time, Pallas kernels for 34%

profile of v3, /device:TPU:0, one launch (start us, length us, event | category | flops | bytes accessed | tf_op | source)
XLA Modules:
  0.0 689.0 jit_solution(14123684148419433482)
XLA Ops:
  10.6 1.1 copy.86
  12.3 1.0 pad_maximum_fusion.1.refs_2_
  14.1 87.4 %first.1 = (bf16[8,256,2048]{2,1,0:T(8,128)(2,1)}, bf16[2048,2048]{1,0:T(8,128)(2,1)}, f32[2048,768]{1,0:T(8,128)}, bf16[4,128,384]{2,1,0:T(8,128)(2,1)}, bf16[4...) custom-call(bf16[256,2048]{1,0:T(8,128)(2,1)} %refs_0_.1, bf16[2,64,384]{2,1,0:T(8,128)(2,1)} %fusion.27.refs_1_, ...), custom_call_target="tpu_custom_call" | custom-call | tf_op jit(solution)/shard_map/first/pallas_call | solution.py:307
  101.5 1.0 slice.195
  104.9 1.0 convert_element_type.107.refs_1_.refs_8_
  106.1 1.2 copy.94
  110.0 56.9 %scan_forward.1 = (f32[2048,384]{1,0:T(8,128)}, f32[2048,384]{1,0:T(8,128)}, f32[2048,384]{1,0:T(8,128)}, f32[2056,384]{1,0:T(8,128)}, bf16[2048,384]{1,0:T(8,12...) custom-call(f32[2048,768]{1,0:T(8,128)} %get-tuple-element.63.refs_0, ...), custom_call_target="tpu_custom_call" | custom-call | tf_op jit(solution)/shard_map/scan_forward/pallas_call | solution.py:307
  166.9 57.6 %fold.4 = (f32[256,2048]{1,0:T(8,128)}, bf16[4,512,512]{2,1,0:T(8,128)(2,1)}, bf16[4,512,256]{2,1,0:T(8,128)(2,1)}) custom-call(bf16[2048,384]{1,0:T(8,128)(2,1)} %get-tuple-element.65.refs_0_, bf16[2048,384]{1,0:T(8,128)(2,1)} %bitcast.92, bf16[256,1536]{1,0:T(8,128)(2,1)} %refs_2_.1, bf16[256,1536]{1,0:T(8,128)(2,1)} %bitcast.90), custom_call_target="tpu_custom_call" | custom-call | tf_op jit(solution)/shard_map/fold/pallas_call | solution.py:307
  224.5 2.1 multiply_reduce_fusion.2
  226.6 1.2 multiply_convert_fusion.refs_0_
  227.8 47.2 %gather_rows.2 = (bf16[8,256,2048]{2,1,0:T(8,128)(2,1)}, bf16[4,512,512]{2,1,0:T(8,128)(2,1)}) custom-call(bf16[256,2048]{1,0:T(8,128)(2,1)} %multiply_convert_fusion.refs_0_, bf16[256,1536]{1,0:T(8,128)(2,1)} %refs_1_.1), custom_call_target="tpu_custom_call" | custom-call | tf_op jit(solution)/shard_map/gather_rows/pallas_call | solution.py:307
  275.1 46.7 %feed.1 = (bf16[2048,768]{1,0:T(8,128)(2,1)}, bf16[2048,768]{1,0:T(8,128)(2,1)}, bf16[2048,768]{1,0:T(8,128)(2,1)}, bf16[4,512,512]{2,1,0:T(8,128)(2,1)}) custom-call(bf16[2048,2048]{1,0:T(8,128)(2,1)} %bitcast.83, bf16[2048,2048]{1,0:T(8,128)(2,1)} %bitcast.81, bf16[2048,256]{1,0:T(8,128)(2,1)} %bitcast.94, bf16[2048,512]{1,0:T(8,128)(2,1)} %bitcast.86, ...), custom_call_target="tpu_custom_call" | custom-call | tf_op jit(solution)/shard_map/feed/pallas_call | solution.py:307
  321.8 11.5 %convolution_convert_fusion.2 = bf16[2048,768]{1,0:T(8,128)(2,1)} fusion(bf16[2048,2048]{1,0:T(8,128)(2,1)} %bitcast.82, bf16[2048,768]{1,0:T(8,128)(2,1)} %get-tuple-element.102.refs_0_), kind=kOutput, calls=%fused_computation.3 | convolution fusion | flops 6444023808 | bytes 14680064 | tf_op jit(solution)/shard_map/dot_general | solution.py:1557
  333.4 11.4 %convolution_convert_fusion = bf16[2048,768]{1,0:T(8,128)(2,1)} fusion(bf16[2048,2048]{1,0:T(8,128)(2,1)} %bitcast.84, bf16[2048,768]{1,0:T(8,128)(2,1)} %get-tuple-element.82.refs_1_), kind=kOutput, calls=%fused_computation.1 | convolution fusion | flops 6444023808 | bytes 14680064 | tf_op jit(solution)/shard_map/dot_general | solution.py:1557
  344.7 11.4 %convolution_convert_fusion.1 = bf16[2048,768]{1,0:T(8,128)(2,1)} fusion(bf16[2048,2048]{1,0:T(8,128)(2,1)} %bitcast.85, bf16[2048,768]{1,0:T(8,128)(2,1)} %get-tuple-element.81.refs_0_), kind=kOutput, calls=%fused_computation.2 | convolution fusion | flops 6444023808 | bytes 14680064 | tf_op jit(solution)/shard_map/dot_general | solution.py:1557
  357.7 49.5 %fold.5 = f32[256,2048]{1,0:T(8,128)} custom-call(bf16[2048,768]{1,0:T(8,128)(2,1)} %get-tuple-element.81.refs_0_, bf16[2048,768]{1,0:T(8,128)(2,1)} %get-tuple-element.82.refs_1_, bf16[2048,256]{1,0:T(8,128)(2,1)} %bitcast.95, bf16[2048,512]{1,0:T(8,128)(2,1)} %bitcast.87, bf16[2048,256]{1,0:T(8,128)(2,1)} %bitcast.97, bf16[2048,512]{1,0:T(8,128)(2,1)} %bitcast.89), custom_call_target="tpu_custom_call" | custom-call | tf_op jit(solution)/shard_map/fold/pallas_call | solution.py:307
  407.2 2.3 multiply_reduce_fusion
  409.6 1.9 multiply_add_fusion
  411.6 3.3 reduce-scatter.5.cloned.1.call-done
  414.8 2.7 convert_element_type.114.rows
  417.5 40.1 %gather_rows.3 = bf16[8,256,2048]{2,1,0:T(8,128)(2,1)} custom-call(bf16[256,2048]{1,0:T(8,128)(2,1)} %convert_element_type.114.rows), custom_call_target="tpu_custom_call" | custom-call | tf_op jit(solution)/shard_map/gather_rows/pallas_call | solution.py:307
  457.6 9.5 %convolution_convert_fusion.4 = bf16[2048,384]{1,0:T(8,128)(2,1)} fusion(bf16[2048,2048]{1,0:T(8,128)(2,1)} %bitcast.79, bf16[2048,384]{1,0:T(8,128)(2,1)} %get-tuple-element.65.refs_0_), kind=kOutput, calls=%fused_computation.11 | convolution fusion | flops 3222011904 | bytes 11534336 | tf_op jit(solution)/shard_map/dot_general | solution.py:1557
  467.1 10.3 %reduce-scatter.7.cloned.1.call-done = bf16[512,768]{1,0:T(8,128)(2,1)} async-done(((bf16[2048,768]{1,0:T(8,128)(2,1)}), bf16[512,768]{1,0:T(8,128)(2,1)}) %reduce-scatter.7.cloned.1.call-update) | async-done | bytes 786448 | tf_op jit(solution)/shard_map/reduce_scatter | solution.py:1680
  477.4 44.2 %scan_backward.1 = (bf16[2048,640]{1,0:T(8,128)(2,1)}, f32[384,768]{1,0:T(8,128)}, f32[8,384]{1,0:T(8,128)}, bf16[2,256,768]{2,1,0:T(8,128)(2,1)}, bf16[2,256,768]{2,1,0:T(8,128)(2,1)}) custom-call(f32[2048,768]{1,0:T(8,128)} %get-tuple-element.63.refs_0_, bf16[2048,2048]{1,0:T(8,128)(2,1)} %bitcast.80, bf16[2048,384]{1,0:T(8,128)(2,1)} %bitcast.93, ...), custom_call_target="tpu_custom_call" | custom-call | tf_op jit(solution)/shard_map/scan_backward/pallas_call | solution.py:307
  523.3 1.3 convert.29
  527.2 1.3 convert_element_type.116
  528.6 1.2 copy.98
  529.8 2.5 copy.97
  532.3 9.0 %convolution_convert_fusion.3 = bf16[2048,640]{0,1:T(8,128)(2,1)S(1)} fusion(bf16[2048,2048]{1,0:T(8,128)(2,1)} %get-tuple-element.98, bf16[2048,640]{1,0:T(8,128)(2,1)} %get-tuple-element.99.refs_0_), kind=kOutput, calls=%fused_computation.4 | convolution fusion | flops 5370019840 | bytes 13631488 | tf_op jit(solution)/shard_map/dot_general | solution.py:1557
  541.4 2.2 pad_maximum_fusion
  543.7 1.2 slice_bitcast_fusion.1
  544.9 1.3 convert_bitcast_fusion
  546.2 3.0 copy.104
  549.2 47.3 %fold.6 = f32[256,2048]{1,0:T(8,128)} custom-call(bf16[2048,640]{1,0:T(8,128)(2,1)} %get-tuple-element.99.refs_0_, bf16[2048,640]{1,0:T(8,128)(2,1)} %bitcast.102), custom_call_target="tpu_custom_call" | custom-call | tf_op jit(solution)/shard_map/fold/pallas_call | solution.py:307
  596.5 2.2 fusion.4
  599.4 52.5 %fold.7 = (f32[256,2048]{1,0:T(8,128)}, f32[16,256]{1,0:T(8,128)}, bf16[2,256,768]{2,1,0:T(8,128)(2,1)}) custom-call(bf16[2048,768]{1,0:T(8,128)(2,1)} %get-tuple-element.102.refs_0_, bf16[2048,256]{1,0:T(8,128)(2,1)} %bitcast.99, bf16[2048,512]{1,0:T(8,128)(2,1)} %bitcast.103, f32[16,256]{1,0:T(8,128)} %pad_maximum_fusion.7.refs_3_, ...), custom_call_target="tpu_custom_call" | custom-call | tf_op jit(solution)/shard_map/fold/pallas_call | solution.py:307
  652.0 1.4 constant_dynamic-slice_fusion
  653.3 1.2 slice_bitcast_fusion.3
  654.6 1.3 maximum_convert_fusion.1
  655.9 1.3 maximum_convert_fusion
  657.9 1.6 fusion.8
  659.6 1.5 copy.105
  661.1 1.2 collective-permute-start
  662.3 2.8 add_convert_fusion
  665.1 9.4 %collective-permute-done = bf16[256,1024]{1,0:T(8,128)(2,1)S(1)} collective-permute-done((bf16[256,1024]{1,0:T(8,128)(2,1)S(1)}, bf16[256,1024]{1,0:T(8,128)(2,1)S(1)}, u32[]{:S(2)}, u32[]{:S(2)}) %collective-permute-start) | collective-permute-done | bytes 524320 | tf_op jit(solution)/shard_map/ppermute | solution.py:1773
  676.0 1.1 copy.103
  680.3 1.0 pad_maximum_fusion.3
  681.3 1.0 pad_maximum_fusion.2
  (139 shorter events, 21.6 us)
Async XLA Ops:
  7.2 4.7 copy-start.8
  7.2 407.6 %reduce-scatter.5.cloned.1.call-start = ((), (), s32[]{:S(2)}) async-start(), calls=%async_computation.4 | async-start | bytes 3932160 | tf_op jit(solution)/shard_map/reduce_scatter | solution.py:1680
  101.5 2.3 copy-start.12
  103.4 2.5 copy-start.10
  103.5 2.5 copy-start.9
  103.5 2.6 copy-start.6
  106.1 3.2 slice-start
  166.9 57.6 %copy-start.3 = (bf16[256,2048]{1,0:T(8,128)(2,1)S(1)}, bf16[256,2048]{1,0:T(8,128)(2,1)}, u32[]{:S(2)}) copy-start(bf16[256,2048]{1,0:T(8,128)(2,1)} %refs_0_.1) | copy-start | bytes 3145732
  356.1 121.3 %reduce-scatter.7.cloned.1.call-start = ((), (), s32[]{:S(2)}) async-start(), calls=%async_computation.5 | async-start | bytes 3932160 | tf_op jit(solution)/shard_map/reduce_scatter | solution.py:1680
  356.9 239.7 %reduce-scatter.9.cloned.1.call-start = ((), (), s32[]{:S(2)}) async-start(), calls=%async_computation.6 | async-start | bytes 3932160 | tf_op jit(solution)/shard_map/reduce_scatter | solution.py:1680
  357.6 301.9 %reduce-scatter.11.cloned.1.call-start = ((), (), s32[]{:S(2)}) async-start(), calls=%async_computation.7 | async-start | bytes 5242880 | tf_op jit(solution)/shard_map/reduce_scatter | solution.py:1680
  407.1 2.3 copy-start.2
  407.2 2.5 copy-start.5
  477.4 44.9 %copy-start.11 = (f32[5,384]{1,0:T(8,128)S(1)}, f32[5,384]{1,0:T(8,128)}, u32[]{:S(2)}) copy-start(f32[5,384]{1,0:T(8,128)} %copy-done.10) | copy-start | bytes 23044
  532.3 9.1 %copy-start.4 = (bf16[2048,320]{0,1:T(8,128)(2,1)S(1)}, bf16[2048,320]{0,1:T(8,128)(2,1)}, u32[]{:S(2)}) copy-start(bf16[2048,320]{0,1:T(8,128)(2,1)} %copy.97) | copy-start | bytes 3932164
  651.9 2.5 copy-start.7
  654.6 2.7 copy-start
  654.6 3.4 copy-start.1
  661.1 13.5 %collective-permute-start = (bf16[256,1024]{1,0:T(8,128)(2,1)S(1)}, bf16[256,1024]{1,0:T(8,128)(2,1)S(1)}, u32[]{:S(2)}, u32[]{:S(2)}) collective-permute-start(bf16[256,1024]{1,0:T(8,128)(2,1)S(1)} %dynamic-slice_bitcast_fusion), channel_id=1, source_target_pairs={{0,4},{4,0},{8,12},{12,8},{16,20},{20,16},{24,28},{28,24},{1,5},{5... | collective-permute-start | bytes 1572872 | tf_op jit(solution)/shard_map/ppermute | solution.py:1773
Sparse Core Ops, SparseCore 0:
  356.2 58.5 reduce-scatter.4
  417.1 60.2 reduce-scatter.6
  479.7 62.0 reduce-scatter.8
  544.0 77.8 reduce-scatter.10

commit v4 on v3

--- a/solution.py
+++ b/solution.py
@@ -456,11 +456,15 @@
     greet(cargo_peers(count))
     small.start()
     branch.start()
+    small.second()
+    branch.second()
+    for freight in others:
+        freight.start()
     gather.start()
-    small.second()
     gather.start_across()
     small.forward()
-    branch.second()
+    for freight in others:
+        freight.second()
     small.finish()
     tail = pltpu.make_async_copy(targets[0], tails, tail_sem)
     tail.start()
@@ -508,16 +512,14 @@
         return [rank(s, d, core), rank(s, d, 1 - core)]
 
     gather.landed()
+    branch.forward()
+    gather.forward()
+    for freight in others:
+        freight.forward()
     norm_blocks(both_cores(side, deck))
-    gather.forward()
-    branch.forward()
-    for freight in others:
-        freight.start()
     gather.landed_relays()
     norm_blocks(both_cores(1 - side, deck))
     norm_blocks(both_cores(side, 1 - deck))
-    for freight in others:
-        freight.second()
     group_finish(gather, *corner_sems, early=True)
     norm_blocks(both_cores(1 - side, 1 - deck))
     branch.finish()
@@ -530,8 +532,6 @@
     ]
     for copy in loading:
         copy.start()
-    for freight in others:
-        freight.forward()
     for copy in loading:
         copy.wait()
     lanes, width = weights.shape[1] // 2, pre.shape[1] // 2
@@ -621,25 +621,51 @@
     return [out[0].reshape(-1, rows.shape[1])] + flat_rows(out[1:])
 
 
-def plain_rows_kernel(rows, everything, *sems):
-    gather = GroupGather(rows, everything, *sems[:3])
+def turned(left, right, out, tiles, low, high):
+    size = left.shape[1] // tiles
+
+    def body(i, carry):
+        place = pl.ds(pl.multiple_of(i * size, size), size)
+        total = lax.dot_general(left[:, place], right[...], TN, preferred_element_type=F32)
+        out[place, :] = total.astype(BF16)
+        return carry
+
+    lax.fori_loop(low, high, body, 0)
+
+
+def plain_rows_kernel(rows, left, right, everything, product, left_here, right_here, *sems):
+    gather = GroupGather(rows, everything, *sems[1:4])
+    loading = [
+        pltpu.make_async_copy(left, left_here, sems[0].at[0]),
+        pltpu.make_async_copy(right, right_here, sems[0].at[1]),
+    ]
     greet(group_peers())
     gather.start()
     gather.start_across()
+    for copy in loading:
+        copy.start()
+    for copy in loading:
+        copy.wait()
+    turned(left_here, right_here, product, 4, 0, 4)
     gather.forward()
-    group_finish(gather, *sems[3:5])
-
-
-def gather_plain(rows, identity):
+    group_finish(gather, *sems[4:6])
+
+
+def gather_plain(rows, left, right, identity):
     out = call(
         plain_rows_kernel,
-        [((8,) + rows.shape, BF16, ANY)],
-        [(rows, ANY)],
-        rows_scratch(),
+        [((8,) + rows.shape, BF16, ANY), ((left.shape[1], right.shape[1]), BF16, VMEM)],
+        [(rows, ANY), (left, ANY), (right, ANY)],
+        [
+            pltpu.VMEM(left.shape, BF16),
+            pltpu.VMEM(right.shape, BF16),
+            pltpu.SemaphoreType.DMA((2,)),
+        ]
+        + rows_scratch(),
         identity,
         "gather_rows",
     )
-    return out[0].reshape(-1, rows.shape[1])
+    return out[0].reshape(-1, rows.shape[1]), out[1]
 
 
 def flip(value, bit):
@@ -699,49 +725,53 @@
         self.totals[...] = total
 
 
-def fold_kernel(count, plan, starts, swaps, *refs):
-    gained = swaps > 0
-    loads = len(starts)
-    lefts = refs[: plan[-1][0] + 1]
-    rights = refs[len(lefts) : len(lefts) + len(plan)]
-    refs = refs[len(lefts) + len(rights) :]
-    halves, refs = refs[:loads], refs[loads:]
-    gains = None
-    if gained:
-        gains, values, refs = refs[0], refs[1 : 1 + swaps], refs[1 + swaps :]
-    out, refs = refs[0], refs[1:]
-    targets, refs = refs[:loads], refs[loads:]
-    if gained:
-        totals, swapped, refs = refs[0], refs[1 : 1 + swaps], refs[1 + swaps :]
-        gain_sum = GainSum(count, gains, totals, *refs[-6:])
-        swap = Swap(values, swapped, *refs[-9:-6])
-    mine, stage, near, leaving, arriving, refs = *refs[:5], refs[5:]
-    send, receive, near_send, near_receive = refs[:4]
-    line, side, deck, core = spot()
-    sibling, across, above = group_peers()
-    freights = load(count, starts, halves, targets, refs[4:])
-    if gained:
-        greet(whole_group() + line_peers(count))
-        gain_sum.start()
-        swap.start()
-    else:
-        greet(cargo_peers(count) if loads else group_peers())
-    for freight in freights:
-        freight.start()
-    rows = out.shape[0]
-    half = rows // 2
-    width = out.shape[1]
-    step = 512
-
-    def product(which, store):
-        base = pl.multiple_of(which * rows, rows)
+class Fold:
+    OWN, ACROSS, ABOVE, CORNER = 0, 1, 2, 3
+
+    def __init__(self, plan, lefts, rights, out, refs):
+        self.plan, self.lefts, self.rights, self.out = plan, lefts, rights, out
+        self.mine, self.stage, self.near = refs[:3]
+        self.across_sum, self.above_sum, self.leaving, self.arriving = refs[3:7]
+        send, receive, self.near_send, self.near_receive = refs[7:11]
+        self.line, self.side, self.deck, self.core = spot()
+        sibling, across, above = group_peers()
+        self.sibling = sibling
+        self.rows, self.width = out.shape
+        self.half = self.rows // 2
+        self.ships = [
+            remote(
+                self.leaving.at[k], self.arriving.at[k], send.at[k], receive.at[k], peer
+            )
+            for k, peer in enumerate((above, across, above, across, across, above))
+        ]
+
+    @staticmethod
+    def scratch(rows, width):
+        half = rows // 2
+        return [
+            pltpu.VMEM((rows, width), F32),
+            pltpu.VMEM((2, rows, width), BF16),
+            pltpu.VMEM((4, rows, width), BF16),
+            pltpu.VMEM((half, width), F32),
+            pltpu.VMEM((half, width), F32),
+            pltpu.VMEM((6, half, width), BF16),
+            pltpu.VMEM((6, half, width), BF16),
+            pltpu.SemaphoreType.DMA((6,)),
+            pltpu.SemaphoreType.DMA((6,)),
+            pltpu.SemaphoreType.DMA((4,)),
+            pltpu.SemaphoreType.DMA((4,)),
+        ]
+
+    def product(self, which, store):
+        base = pl.multiple_of(which * self.rows, self.rows)
+        step = 512
 
         def body(j, carry):
             columns = pl.ds(pl.multiple_of(j * step, step), step)
             total = None
-            for (which_left, start), right in zip(plan, rights):
+            for (which_left, start), right in zip(self.plan, self.rights):
                 part = lax.dot_general(
-                    lefts[which_left][pl.ds(base, rows), start : start + right.shape[1]],
+                    self.lefts[which_left][pl.ds(base, self.rows), start : start + right.shape[1]],
                     right[columns, :],
                     NT,
                     preferred_element_type=F32,
@@ -750,159 +780,303 @@
             store(columns, total)
             return carry
 
-        lax.fori_loop(0, width // step, body, 0)
-
-    def sweep(action):
+        lax.fori_loop(0, self.width // step, body, 0)
+
+    def sweep(self, action):
         def body(i, carry):
             action(pl.multiple_of(i * 16, 16))
             return carry
 
-        lax.fori_loop(0, half // 16, body, 0)
-
-    def chip_sum(q, h, r):
-        place = pl.ds(h * half + r, 16)
-        return mine[q, place, :] + near[q, place, :].astype(F32)
-
-    def ship(index, peer):
+        lax.fori_loop(0, self.half // 16, body, 0)
+
+    def near_copy(self, q):
         return remote(
-            leaving.at[index], arriving.at[index], send.at[index], receive.at[index], peer
+            self.stage.at[q % 2],
+            self.near.at[q],
+            self.near_send.at[q],
+            self.near_receive.at[q],
+            self.sibling,
         )
 
-    ships = [ship(k, peer) for k, peer in enumerate((above, across, above, across, across, above))]
-    OWN, ACROSS, ABOVE, CORNER = 0, 1, 2, 3
-    seats = {
-        CORNER: (1 - side, 1 - deck),
-        ABOVE: (side, 1 - deck),
-        ACROSS: (1 - side, deck),
-        OWN: (side, deck),
-    }
-    nears = []
-    for q in (CORNER, ABOVE, ACROSS, OWN):
-        s, d = seats[q]
-
-        def put_stage(columns, total, q=q):
-            stage[q, :, columns] = total.astype(BF16)
-
-        def put_mine(columns, total, q=q):
-            mine[q, :, columns] = total
-
-        product(rank(s, d, 1 - core), put_stage)
-        copy = remote(stage.at[q], near.at[q], near_send.at[q], near_receive.at[q], sibling)
-        copy.start()
-        nears.append(copy)
-        product(rank(s, d, core), put_mine)
-        copy.wait_recv()
-        if q == CORNER:
-
-            def corner_sum(r):
-                for h in range(2):
-                    leaving[h, pl.ds(r, 16), :] = chip_sum(CORNER, h, r).astype(BF16)
-
-            sweep(corner_sum)
-            ships[0].start()
-            ships[1].start()
-        if q == ABOVE:
-
-            def above_sum(r):
-                leaving[2, pl.ds(r, 16), :] = chip_sum(ABOVE, 0, r).astype(BF16)
-
-            sweep(above_sum)
-            ships[2].start()
-            for freight in freights:
-                freight.second()
-            if gained:
-                gain_sum.second()
-        if q == ACROSS:
-
-            def across_sum(r):
-                leaving[3, pl.ds(r, 16), :] = chip_sum(ACROSS, 1, r).astype(BF16)
-
-            sweep(across_sum)
-            ships[3].start()
-    ships[0].wait_recv()
-
-    def pass_across(r):
-        total = chip_sum(ACROSS, 0, r) + arriving[0, pl.ds(r, 16), :].astype(F32)
-        leaving[4, pl.ds(r, 16), :] = total.astype(BF16)
-
-    sweep(pass_across)
-    ships[4].start()
-    ships[1].wait_recv()
-
-    def pass_above(r):
-        total = chip_sum(ABOVE, 1, r) + arriving[1, pl.ds(r, 16), :].astype(F32)
-        leaving[5, pl.ds(r, 16), :] = total.astype(BF16)
-
-    sweep(pass_above)
-    ships[5].start()
+    def chip_sum(self, q, h, r):
+        place = pl.ds(h * self.half + r, 16)
+        return self.mine[place, :] + self.near[q, place, :].astype(F32)
+
+    def block(self, q):
+        s, d = [
+            (self.side, self.deck),
+            (1 - self.side, self.deck),
+            (self.side, 1 - self.deck),
+            (1 - self.side, 1 - self.deck),
+        ][q]
+        if q < 2:
+            self.near_copy(q + 2).wait_send()
+
+        def put_stage(columns, total):
+            self.stage[q % 2, :, columns] = total.astype(BF16)
+
+        def put_mine(columns, total):
+            target = self.out if q == self.OWN else self.mine
+            target[:, columns] = total
+
+        self.product(rank(s, d, 1 - self.core), put_stage)
+        self.near_copy(q).start()
+        self.product(rank(s, d, self.core), put_mine)
+        self.near_copy(q).wait_recv()
+
+    def send(self, k):
+        self.ships[k].start()
+
+    def begin(self, freights=()):
+        self.block(self.CORNER)
+
+        def corner(r):
+            for h in range(2):
+                self.leaving[h, pl.ds(r, 16), :] = self.chip_sum(self.CORNER, h, r).astype(BF16)
+
+        self.sweep(corner)
+        self.send(0)
+        self.send(1)
+        self.block(self.ABOVE)
+
+        def above(r):
+            place = pl.ds(r, 16)
+            self.leaving[2, place, :] = self.chip_sum(self.ABOVE, 0, r).astype(BF16)
+            self.above_sum[place, :] = self.chip_sum(self.ABOVE, 1, r)
+
+        self.sweep(above)
+        self.send(2)
+        for freight in freights:
+            freight.second()
+        self.block(self.ACROSS)
+
+        def across(r):
+            place = pl.ds(r, 16)
+            self.leaving[3, place, :] = self.chip_sum(self.ACROSS, 1, r).astype(BF16)
+            self.across_sum[place, :] = self.chip_sum(self.ACROSS, 0, r)
+
+        self.sweep(across)
+        self.send(3)
+        self.block(self.OWN)
+
+    def middle(self):
+        self.ships[0].wait_recv()
+
+        def across(r):
+            place = pl.ds(r, 16)
+            total = self.across_sum[place, :] + self.arriving[0, place, :].astype(F32)
+            self.leaving[4, place, :] = total.astype(BF16)
+
+        self.sweep(across)
+        self.send(4)
+        self.ships[1].wait_recv()
+
+        def above(r):
+            place = pl.ds(r, 16)
+            total = self.above_sum[place, :] + self.arriving[1, place, :].astype(F32)
+            self.leaving[5, place, :] = total.astype(BF16)
+
+        self.sweep(above)
+        self.send(5)
+
+    def finish(self, store):
+        for k in range(2, 6):
+            self.ships[k].wait_recv()
+
+        def total(r):
+            for h, pair in enumerate(((2, 4), (3, 5))):
+                place, here = pl.ds(r, 16), pl.ds(h * self.half + r, 16)
+                value = self.out[here, :] + self.near[self.OWN, here, :].astype(F32)
+                for k in pair:
+                    value = value + self.arriving[k, place, :].astype(F32)
+                store(here, value)
+
+        self.sweep(total)
+        for k in range(6):
+            self.ships[k].wait_send()
+        for q in range(2):
+            self.near_copy(q).wait_send()
+
+
+def unit_rows(value):
+    scale = lax.rsqrt(jnp.mean(value * value, axis=1, keepdims=True) + EPSILON)
+    return value * scale, scale
+
+
+def norm_back_rows(grad, unit, scale, gain):
+    grad_unit = grad * gain
+    inner = jnp.mean(grad_unit * unit, axis=1, keepdims=True)
+    return scale * (grad_unit - unit * inner), jnp.sum(grad * unit, axis=0, keepdims=True)
+
+
+def mixer_fold_kernel(count, jobs, starts, left, right, *refs):
+    loads = len(starts)
+    inputs, gain, refs = refs[0], refs[1], refs[2:]
+    halves, refs = refs[:loads], refs[loads:]
+    out, normed, refs = refs[0], refs[1], refs[2:]
+    targets, refs = refs[:loads], refs[loads:]
+    fold = Fold(jobs[0], [left], [right], out, refs[:11])
+    freights = load(count, starts, halves, targets, refs[11:])
+    greet(cargo_peers(count))
+    for freight in freights:
+        freight.start()
+    fold.begin(freights)
+    fold.middle()
     for freight in freights:
         freight.forward()
-    if gained:
-        gain_sum.finish()
-        swap.finish()
-    for k in range(2, 6):
-        ships[k].wait_recv()
-
-    def finish(r):
-        place = pl.ds(r, 16)
-        first = arriving[2, place, :].astype(F32) + arriving[4, place, :].astype(F32)
-        out[place, :] = chip_sum(OWN, 0, r) + first
-        second = arriving[3, place, :].astype(F32) + arriving[5, place, :].astype(F32)
-        out[pl.ds(half + r, 16), :] = chip_sum(OWN, 1, r) + second
-
-    sweep(finish)
-    for k in range(6):
-        ships[k].wait_send()
-    for copy in nears:
-        copy.wait_send()
+
+    def store(here, value):
+        value = value + inputs[here, :].astype(F32)
+        out[here, :] = value
+        normed[here, :] = (unit_rows(value)[0] * gain[...]).astype(BF16)
+
+    fold.finish(store)
     for freight in freights:
         freight.finish()
 
 
-def fold(count, pairs, identity, cargo=(), gains=None, swaps=()):
+def plan_of(lefts_rights):
     lefts, rights, plan = [], [], []
-    for k, (left, parts) in enumerate(pairs):
-        lefts.append(left)
+    for k, (left, parts) in enumerate(lefts_rights):
+        lefts.append((left, VMEM))
         start = 0
         for part in parts:
-            rights.append(part)
+            rights.append((part, VMEM))
             plan.append((k, start))
             start += part.shape[1]
-    rows, width = lefts[0].shape[0] // 8, rights[0].shape[0]
-    outs = [((rows, width), F32, VMEM)]
-    ins = [(value, VMEM) for value in list(lefts) + list(rights)]
-    scratch = [
-        pltpu.VMEM((4, rows, width), F32),
-        pltpu.VMEM((4, rows, width), BF16),
-        pltpu.VMEM((4, rows, width), BF16),
-        pltpu.VMEM((6, rows // 2, width), BF16),
-        pltpu.VMEM((6, rows // 2, width), BF16),
-        pltpu.SemaphoreType.DMA((6,)),
-        pltpu.SemaphoreType.DMA((6,)),
-        pltpu.SemaphoreType.DMA((4,)),
-        pltpu.SemaphoreType.DMA((4,)),
-    ]
-    outs += cargo_outs(count, cargo)
-    ins += cargo_ins(cargo)
-    scratch += cargo_scratch(count, cargo)
-    if gains is not None:
-        outs.append((gains.shape, F32, VMEM))
-        ins.append((gains, VMEM))
-        outs += [(value.shape, BF16, ANY) for value in swaps]
-        ins += [(value, ANY) for value in swaps]
-        scratch += Swap.scratch(swaps)
-        scratch += GainSum.scratch(count, gains)
+    return plan, lefts + rights
+
+
+def mixer_fold(count, merged, mixer, inputs, gain, cargo):
+    plan, ins = plan_of([(merged, [mixer])])
+    rows, width = inputs.shape
     out = call(
-        functools.partial(fold_kernel, count, plan, cargo_starts(cargo), len(swaps)),
-        outs,
-        ins,
-        scratch,
-        identity,
-        "fold",
-    )
-    if gains is not None:
-        return out
-    return out[:1] + flat_rows(out[1:])
+        functools.partial(mixer_fold_kernel, count, [plan], cargo_starts(cargo)),
+        [((rows, width), F32, VMEM), ((rows, width), BF16, VMEM)] + cargo_outs(count, cargo),
+        ins + [(inputs, VMEM), (gain, VMEM)] + cargo_ins(cargo),
+        Fold.scratch(rows, width) + cargo_scratch(count, cargo),
+        3,
+        "mixer_fold",
+    )
+    return out[:2] + flat_rows(out[2:])
+
+
+def feed_fold_kernel(plan, parts, left, other, *refs):
+    rights, refs = refs[:parts], refs[parts:]
+    normed, hidden, cotangent, gain, refs = *refs[:4], refs[4:]
+    out, low, gain_sum, grads = refs[:4]
+    fold = Fold(plan, [left, other], rights, out, refs[4:15])
+    normed_here, load_sem = refs[15:]
+    greet(group_peers())
+    loading = pltpu.make_async_copy(normed, normed_here, load_sem)
+    loading.start()
+    fold.begin()
+    fold.middle()
+    loading.wait()
+    turned(normed_here, left, grads, 4, 0, 4)
+    gain_sum[...] = jnp.zeros_like(gain_sum)
+
+    def store(here, value):
+        unit, scale = unit_rows(hidden[here, :])
+        back, terms = norm_back_rows(value, unit, scale, gain[...])
+        gain_sum[0:1, :] += terms
+        back = cotangent[here, :].astype(F32) + back
+        out[here, :] = back
+        low[here, :] = back.astype(BF16)
+
+    fold.finish(store)
+
+
+def feed_fold(grad_gating, grad_lifting, gates, ups, normed, hidden, cotangent, gain):
+    plan, ins = plan_of([(grad_gating, gates), (grad_lifting, ups)])
+    rows, width = hidden.shape
+    return call(
+        functools.partial(feed_fold_kernel, plan, len(gates) + len(ups)),
+        [
+            ((rows, width), F32, VMEM),
+            ((rows, width), BF16, VMEM),
+            ((8, width), F32, VMEM),
+            ((normed.shape[1], grad_gating.shape[1]), BF16, VMEM),
+        ],
+        ins + [(normed, ANY), (hidden, VMEM), (cotangent, VMEM), (gain, VMEM)],
+        Fold.scratch(rows, width)
+        + [pltpu.VMEM(normed.shape, BF16), pltpu.SemaphoreType.DMA],
+        6,
+        "feed_fold",
+    )
+
+
+def last_fold_kernel(count, plans, parts, swaps, left, right, feed_left, *refs):
+    rights, refs = refs[:parts], refs[parts:]
+    inputs, gain, grad_hidden, hidden, second, refs = *refs[:5], refs[5:]
+    values, refs = refs[:swaps], refs[swaps:]
+    input_grad, output, totals = refs[:3]
+    swapped, refs = refs[3 : 3 + swaps], refs[3 + swaps :]
+    out, feed_out, sums, terms_here, refs = *refs[:4], refs[4:]
+    fold = Fold(plans[0], [left], [right], out, refs[:11])
+    feed = Fold(plans[1], [feed_left], rights, feed_out, refs[11:22])
+    swap = Swap(values, swapped, *refs[22:25])
+    gain_sum = GainSum(count, sums, totals, *refs[25:])
+    greet(whole_group() + line_peers(count))
+    swap.start()
+    fold.begin()
+    feed.begin()
+    fold.middle()
+    feed.middle()
+    terms_here[...] = jnp.zeros_like(terms_here)
+
+    def store(here, value):
+        unit, scale = unit_rows(inputs[here, :].astype(F32))
+        back, terms = norm_back_rows(value, unit, scale, gain[...])
+        terms_here[0:1, :] += terms
+        input_grad[here, :] = (grad_hidden[here, :] + back).astype(BF16)
+
+    fold.finish(store)
+    shares, slim = sums.shape[0] // 2, sums.shape[1]
+    for k in range(shares):
+        columns = slice(k * slim, (k + 1) * slim)
+        sums[k : k + 1, :] = terms_here[0:1, columns]
+        sums[shares + k : shares + k + 1, :] = second[0:1, columns]
+    gain_sum.start()
+    gain_sum.second()
+
+    def store_output(here, value):
+        output[here, :] = (hidden[here, :] + value).astype(BF16)
+
+    feed.finish(store_output)
+    gain_sum.finish()
+    swap.finish()
+
+
+def last_fold(count, grads, branch, feed_left, downs, inputs, gain, grad_hidden, hidden, second, swaps):
+    plan, ins = plan_of([(grads, [branch])])
+    feed_plan, feed_ins = plan_of([(feed_left, downs)])
+    rows, width = hidden.shape
+    both = jax.ShapeDtypeStruct((4 * count, width // (2 * count)), F32)
+    return call(
+        functools.partial(last_fold_kernel, count, (plan, feed_plan), len(downs), len(swaps)),
+        [
+            ((rows, width), BF16, VMEM),
+            ((rows, width), BF16, VMEM),
+            (both.shape, F32, VMEM),
+        ]
+        + [(value.shape, BF16, ANY) for value in swaps],
+        ins
+        + feed_ins
+        + [(value, VMEM) for value in (inputs, gain, grad_hidden, hidden, second)]
+        + [(value, ANY) for value in swaps],
+        [
+            pltpu.VMEM((rows, width), F32),
+            pltpu.VMEM((rows, width), F32),
+            pltpu.VMEM(both.shape, F32),
+            pltpu.VMEM((8, width), F32),
+        ]
+        + Fold.scratch(rows, width) * 2
+        + Swap.scratch(swaps)
+        + GainSum.scratch(count, both),
+        9,
+        "last_fold",
+    )
 
 
 def gelu_both(value):
@@ -1395,7 +1569,8 @@
     gate_parts, up_parts, down_parts = refs[2:4], refs[4:6], refs[6 : 6 + early]
     refs = refs[6 + early :]
     halves, refs = refs[:loads], refs[loads:]
-    results, targets, refs = refs[:3], refs[3 : 3 + loads], refs[3 + loads :]
+    results, down_grads = refs[:3], refs[3]
+    targets, refs = refs[4 : 4 + loads], refs[4 + loads :]
     table, gate_up, acts, slopes, down, hidden, grad_gating, grad_lifting = refs[:8]
     table_sems, back_sems, write_sems, weight_sems, down_sems = refs[8:13]
     freights = load(count, starts, halves, targets, refs[13:])
@@ -1484,6 +1659,7 @@
     again.wait_all()
     for copy in copies[:early]:
         copy.wait()
+    turned(table, hidden, down_grads, 4, 0, 4)
     ready = sum(part.shape[1] for part in down_parts)
     back(0, ready)
     for freight in freights:
@@ -1503,7 +1679,9 @@
     pieces = rows // CHUNK
     out = call(
         functools.partial(feed_kernel, count, len(down_parts), cargo_starts(cargo)),
-        [((rows, width), BF16, ANY)] * 3 + cargo_outs(count, cargo),
+        [((rows, width), BF16, ANY)] * 3
+        + [((normed.shape[1], width), BF16, VMEM)]
+        + cargo_outs(count, cargo),
         [(normed, ANY), (cotangent, ANY)]
         + [(part, ANY) for part in list(gate_parts) + list(up_parts) + list(down_parts)]
         + cargo_ins(cargo),
@@ -1526,22 +1704,11 @@
         5,
         "feed",
     )
-    return out[:3] + flat_rows(out[3:])
+    return out[:4] + flat_rows(out[4:])
 
 
 def doc_index(places, doc_starts):
     return jnp.sum((doc_starts[None, :] <= places[:, None]).astype(jnp.int32), axis=1)
-
-
-def norm_back(grad_unit, unit_rows, scale_rows):
-    return scale_rows * (
-        grad_unit - unit_rows * jnp.mean(grad_unit * unit_rows, axis=1, keepdims=True)
-    )
-
-
-def unit_norm(values):
-    scale = lax.rsqrt(jnp.mean(values * values, axis=1, keepdims=True) + EPSILON)
-    return values * scale, scale
 
 
 def split_columns(value):
@@ -1657,22 +1824,27 @@
     columns.append(columns[0])
     masks = jnp.stack(columns, axis=1).astype(F32)
 
-    residual = layer_input.astype(F32)
-    unit_one, scale_one = unit_norm(residual)
     conv, recur, admit, state, merged, entry, cot_all, mixer_all, up_first = scan_forward(
         count, pre, masks, table, gate_weights, out_grad, [mixer_halves, (feed_up, 0, narrow)]
     )
-    mixer_own, gate_second, down_first = fold(
-        count, [(merged, [mixer_all])], 3, [(feed_gate, narrow, broad), (down_rows, 0, narrow)]
-    )
-    hidden_one = residual + mixer_own
-    unit_two, scale_two = unit_norm(hidden_one)
-    normed_two, up_second = gather_rows(
-        count, (unit_two * gain_second).astype(BF16), [(feed_up, narrow, broad)], 4
-    )
+    hidden_one, normed_own, gate_second, down_first = mixer_fold(
+        count,
+        merged,
+        mixer_all,
+        layer_input,
+        gain_second[None],
+        [(feed_gate, narrow, broad), (down_rows, 0, narrow)],
+    )
+    normed_two, up_second = gather_rows(count, normed_own, [(feed_up, narrow, broad)], 4)
     gate_parts, up_parts = [gate_first, gate_second], [up_first, up_second]
-    hidden, grad_gating, grad_lifting, down_second = feed(
-        count, normed_two, cot_all, gate_parts, up_parts, [down_first], [(down_rows, narrow, broad)]
+    hidden, grad_gating, grad_lifting, down_grads, down_second = feed(
+        count,
+        normed_two,
+        cot_all,
+        gate_parts,
+        up_parts,
+        [down_first],
+        [(down_rows, narrow, broad)],
     )
     down_parts = [down_first, down_second]
 
@@ -1681,22 +1853,21 @@
             value, "dp", scatter_dimension=0, axis_index_groups=line_groups, tiled=True
         )
 
-    down_grads = by_rows(cot_all, hidden)
-    grad_gating, grad_lifting, down_grads = lax.optimization_barrier(
-        (grad_gating, grad_lifting, down_grads)
-    )
-    gate_grads = by_rows(normed_two, grad_gating)
-    up_grads = by_rows(normed_two, grad_lifting)
-    grad_gating, grad_lifting, down_grads, gate_grads, up_grads = lax.optimization_barrier(
-        (grad_gating, grad_lifting, down_grads, gate_grads, up_grads)
-    )
-    down_sum, gate_sum, up_sum = line_sum(down_grads), line_sum(gate_grads), line_sum(up_grads)
-    grad_normed_two = fold(count, [(grad_gating, gate_parts), (grad_lifting, up_parts)], 6)[0]
-    grad_hidden_one = out_grad.astype(F32) + norm_back(
-        grad_normed_two * gain_second, unit_two, scale_two
-    )
-    grad_hidden_one, down_sum = lax.optimization_barrier((grad_hidden_one, down_sum))
-    back_low = gather_plain(grad_hidden_one.astype(BF16), 8)
+    down_sum = line_sum(down_grads)
+    grad_hidden_one, low_own, second_terms, gate_grads = feed_fold(
+        grad_gating,
+        grad_lifting,
+        gate_parts,
+        up_parts,
+        normed_two,
+        hidden_one,
+        out_grad,
+        gain_second[None],
+    )
+    low_own, down_sum = lax.optimization_barrier((low_own, down_sum))
+    gate_sum = line_sum(gate_grads)
+    back_low, up_grads = gather_plain(low_own, normed_two, grad_lifting, 8)
+    up_sum = line_sum(up_grads)
     outlet_grads = by_rows(back_low, merged)
 
     def by_side(value):
@@ -1747,34 +1918,33 @@
     last_grads = jnp.concatenate([outlet_grads[:, :lanes], grad_small, branch_grads], axis=1)
     grad_pre, last_grads = lax.optimization_barrier((grad_pre, last_grads))
     last_sum = line_sum(last_grads)
-    grad_normed_one = fold(count, [(grad_pre, [branch_all])], 10)[0]
-    hidden, grad_normed_one, up_sum = lax.optimization_barrier(
-        (hidden, grad_normed_one, up_sum)
-    )
-    gains = jnp.concatenate(
-        [
-            jnp.sum(grad_normed_one * unit_one, axis=0).reshape(shares, slim),
-            jnp.sum(grad_normed_two * unit_two, axis=0).reshape(shares, slim),
-        ]
-    )
-    feed_own, gains, up_both = fold(
-        count, [(hidden, down_parts)], 9, gains=gains, swaps=[by_side(up_sum)]
+    input_grad, layer_output, gains, up_both = last_fold(
+        count,
+        grad_pre,
+        branch_all,
+        hidden,
+        down_parts,
+        layer_input,
+        gain_first[None],
+        grad_hidden_one,
+        hidden_one,
+        second_terms,
+        [by_side(up_sum)],
     )
     first_gain_grad = lax.dynamic_index_in_dim(gains, mine, 0, False)
     second_gain_grad = lax.dynamic_index_in_dim(gains, shares + mine, 0, False)
-    layer_output = (hidden_one + feed_own).astype(BF16)
-    input_grad = (
-        grad_hidden_one + norm_back(grad_normed_one * gain_first, unit_one, scale_one)
-    ).astype(BF16)
-
-    pair = by_side(last_sum)
-    kept = lax.dynamic_index_in_dim(pair, side, 0, False)
-    given = lax.dynamic_index_in_dim(pair, 1 - side, 0, False)
-    other = lax.ppermute(given, "dp", [(k, k ^ 1) for k in range(shares)])
-    lasts = [
-        jnp.where(side == 0, kept, other).astype(F32),
-        jnp.where(side == 0, other, kept).astype(F32),
-    ]
+
+    def swap(value):
+        pair = by_side(value)
+        kept = lax.dynamic_index_in_dim(pair, side, 0, False)
+        given = lax.dynamic_index_in_dim(pair, 1 - side, 0, False)
+        other = lax.ppermute(given, "dp", [(k, k ^ 1) for k in range(shares)])
+        return [
+            jnp.where(side == 0, kept, other).astype(F32),
+            jnp.where(side == 0, other, kept).astype(F32),
+        ]
+
+    lasts = swap(last_sum)
 
     def columns(start, stop):
         return jnp.concatenate([value[:, start:stop] for value in lasts], axis=1)

time: 695 us -> 639 us (0.919)
  matrix products: 52.9 us -> 16.9 us
  other arithmetic: 37 us -> 17.5 us
    dot_general x5 -> x2, matrix products: 52.9 us -> 16.9 us  [by_rows(): lax.dot_general(left, right, TN, preferred_element_type=F32).astype(BF16)]
    convert_element_type x5 -> x1, other arithmetic: 8.5 us -> 0.14 us  [swap(): jnp.where(side == 0, kept, other).astype(F32)]
    pallas_call x10 -> x9, Pallas kernels: 529 us -> 530 us  [call(): pl.pallas_call(kernel, out_shape=[jax.ShapeDtypeStruct(shape, kind) for s...]
  transfers between devices with their start and end apart: 5 -> 5, of which waited for: 3 -> 3; matrix products, arithmetic and copies ran while one was open for 8% -> 5% of each run, Pallas kernels for 34% -> 37%
where the time goes in v4:
time: 639 us; the launch traced here: 633 us
  Pallas kernels  530 us (83%)
  waiting for transfers between devices  26.8 us (4%)
  local copies, waits for them, and re-layouts  26.4 us (4%)
  other arithmetic  17.5 us (3%)
  matrix products  16.9 us (3%)
  between operations  14.6 us (2%)
    pallas_call x9, Pallas kernels, call(): pl.pallas_call(kernel, out_shape=[jax.ShapeDtypeStruct(shape, kind) for s...  530 us
    dot_general x2, matrix products, by_rows(): lax.dot_general(left, right, TN, preferred_element_type=F32).astype(BF16)  16.9 us
    reduce_scatter x4, waiting for transfers between devices, line_sum(): lax.psum_scatter(value, 'dp', scatter_dimension=0, axis_index_groups=line...  15.6 us
  transfers between devices with their start and end apart: 5, of which 3 were waited for; matrix products, arithmetic and copies ran while one was open for 5% of the time, Pallas kernels for 37%

profile of v4, /device:TPU:0, one launch (start us, length us, event | category | flops | bytes accessed | tf_op | source)
XLA Modules:
  0.0 633.3 jit_solution(9764254704079511532)
XLA Ops:
  7.3 0.7 fusion.27
  8.3 0.9 pad_maximum_fusion.6
  9.2 0.7 stack.8
  9.9 0.7 stack.9
  10.5 1.1 copy.89
  11.9 1.1 copy.91
  13.3 1.0 pad_maximum_fusion.1.refs_2_
  14.3 0.7 fusion.17.refs_1_
  15.0 85.2 %first.1 = (bf16[8,256,2048]{2,1,0:T(8,128)(2,1)}, bf16[2048,2048]{1,0:T(8,128)(2,1)}, f32[2048,768]{1,0:T(8,128)}, bf16[4,128,384]{2,1,0:T(8,128)(2,1)}, bf16[4...) custom-call(bf16[256,2048]{1,0:T(8,128)(2,1)} %refs_2_.3, bf16[2,64,384]{2,1,0:T(8,128)(2,1)} %fusion.17.refs_1_, ...), custom_call_target="tpu_custom_call" | custom-call | tf_op jit(solution)/shard_map/first/pallas_call | solution.py:307
  100.2 1.0 slice.195
  101.2 0.9 slice.191
  103.6 1.0 convert_element_type.79.refs_1_.refs_8_
  105.5 1.2 copy.98
  107.0 0.9 fusion.2.refs_3_.refs_10_
  107.9 0.8 pad.48.refs_5_
  108.7 0.7 maximum_maximum_fusion.refs_2_.refs_9_
  109.4 56.9 %scan_forward.1 = (f32[2048,384]{1,0:T(8,128)}, f32[2048,384]{1,0:T(8,128)}, f32[2048,384]{1,0:T(8,128)}, f32[2056,384]{1,0:T(8,128)}, bf16[2048,384]{1,0:T(8,12...) custom-call(f32[2048,768]{1,0:T(8,128)} %get-tuple-element.61.refs_0, ...), custom_call_target="tpu_custom_call" | custom-call | tf_op jit(solution)/shard_map/scan_forward/pallas_call | solution.py:307
  166.3 58.1 %mixer_fold.1 = (f32[256,2048]{1,0:T(8,128)}, bf16[256,2048]{1,0:T(8,128)(2,1)}, bf16[4,512,512]{2,1,0:T(8,128)(2,1)}, bf16[4,512,256]{2,1,0:T(8,128)(2,1)}) custom-call(bf16[2048,384]{1,0:T(8,128)(2,1)} %get-tuple-element.63.left, bf16[2048,384]{1,0:T(8,128)(2,1)} %bitcast.91, bf16[256,2048]{1,0:T(8,128)(2,1)} %refs_2_.3, f32[1,2048]{1,0:T(1,128)} %bitcast.116, ...), custom_call_target="tpu_custom_call" | custom-call | tf_op jit(solution)/shard_map/mixer_fold/pallas_call | solution.py:307
  224.4 47.3 %gather_rows.2 = (bf16[8,256,2048]{2,1,0:T(8,128)(2,1)}, bf16[4,512,512]{2,1,0:T(8,128)(2,1)}) custom-call(bf16[256,2048]{1,0:T(8,128)(2,1)} %get-tuple-element.65.refs_0_, bf16[256,1536]{1,0:T(8,128)(2,1)} %refs_1_.1), custom_call_target="tpu_custom_call" | custom-call | tf_op jit(solution)/shard_map/gather_rows/pallas_call | solution.py:307
  271.7 48.3 %feed.1 = (bf16[2048,768]{1,0:T(8,128)(2,1)}, bf16[2048,768]{1,0:T(8,128)(2,1)}, bf16[2048,768]{1,0:T(8,128)(2,1)}, bf16[2048,768]{1,0:T(8,128)(2,1)}, bf16[4,512,512]{2,1,0:T(8,128)(2,1)}) custom-call(bf16[2048,2048]{1,0:T(8,128)(2,1)} %bitcast.79, bf16[2048,2048]{1,0:T(8,128)(2,1)} %bitcast.82, bf16[2048,256]{1,0:T(8,128)(2,1)} %bitcast.93, ...), custom_call_target="tpu_custom_call" | custom-call | tf_op jit(solution)/shard_map/feed/pallas_call | solution.py:307
  320.5 53.9 %feed_fold.1 = (f32[256,2048]{1,0:T(8,128)}, bf16[256,2048]{1,0:T(8,128)(2,1)}, f32[8,2048]{1,0:T(8,128)}, bf16[2048,768]{1,0:T(8,128)(2,1)}) custom-call(bf16[2048,768]{1,0:T(8,128)(2,1)} %get-tuple-element.73.left, bf16[2048,768]{1,0:T(8,128)(2,1)} %get-tuple-element.74.other.right, bf16[2048,256]{1,0:T(8,128)(2,1)} %bitcast.94, ...), custom_call_target="tpu_custom_call" | custom-call | tf_op jit(solution)/shard_map/feed_fold/pallas_call | solution.py:307
  374.5 4.0 reduce-scatter.5.cloned.1.call-done
  378.6 41.7 %gather_rows.3 = (bf16[8,256,2048]{2,1,0:T(8,128)(2,1)}, bf16[2048,768]{1,0:T(8,128)(2,1)}) custom-call(bf16[256,2048]{1,0:T(8,128)(2,1)} %get-tuple-element.78.rows, bf16[2048,2048]{1,0:T(8,128)(2,1)} %bitcast.81, bf16[2048,768]{1,0:T(8,128)(2,1)} %get-tuple-element.74.other.right), custom_call_target="tpu_custom_call" | custom-call | tf_op jit(solution)/shard_map/gather_rows/pallas_call | solution.py:307
  420.4 1.3 copy-done
  421.7 7.9 %convolution_convert_fusion.1 = bf16[2048,384]{1,0:T(8,128)(2,1)S(1)} fusion(bf16[2048,2048]{1,0:T(8,128)(2,1)} %bitcast.83, bf16[2048,384]{1,0:T(8,128)(2,1)S(1)} %copy-done), kind=kOutput, calls=%fused_computation.2 | convolution fusion | flops 3222011904 | bytes 11534336 | tf_op jit(solution)/shard_map/dot_general | solution.py:1724
  429.7 11.6 %reduce-scatter.7.cloned.1.call-done = bf16[512,768]{1,0:T(8,128)(2,1)} async-done(((bf16[2048,768]{1,0:T(8,128)(2,1)}), bf16[512,768]{1,0:T(8,128)(2,1)}) %reduce-scatter.7.cloned.1.call-update) | async-done | bytes 786448 | tf_op jit(solution)/shard_map/reduce_scatter | solution.py:1852
  441.2 44.0 %scan_backward.1 = (bf16[2048,640]{1,0:T(8,128)(2,1)}, f32[384,768]{1,0:T(8,128)}, f32[8,384]{1,0:T(8,128)}, bf16[2,256,768]{2,1,0:T(8,128)(2,1)}, bf16[2,256,768]{2,1,0:T(8,128)(2,1)}) custom-call(f32[2048,768]{1,0:T(8,128)} %get-tuple-element.61.refs_0_, bf16[2048,2048]{1,0:T(8,128)(2,1)} %bitcast.84, bf16[2048,384]{1,0:T(8,128)(2,1)} %bitcast.92, ...), custom_call_target="tpu_custom_call" | custom-call | tf_op jit(solution)/shard_map/scan_backward/pallas_call | solution.py:307
  485.3 0.7 slice.249
  486.0 0.7 convert_reduce_fusion.7
  486.9 1.3 convert.29
  490.0 0.7 copy.101
  490.7 9.0 %convolution_convert_fusion = bf16[2048,640]{0,1:T(8,128)(2,1)S(1)} fusion(bf16[2048,2048]{1,0:T(8,128)(2,1)} %get-tuple-element.93, bf16[2048,640]{1,0:T(8,128)(2,1)} %get-tuple-element.94.left), kind=kOutput, calls=%fused_computation.1 | convolution fusion | flops 5370019840 | bytes 13631488 | tf_op jit(solution)/shard_map/dot_general | solution.py:1724
  499.7 2.3 pad_maximum_fusion
  503.4 1.6 copy.108
  505.1 1.3 maximum_convert_fusion
  506.4 94.4 %last_fold.1 = (bf16[256,2048]{1,0:T(8,128)(2,1)}, bf16[256,2048]{1,0:T(8,128)(2,1)}, f32[16,256]{1,0:T(8,128)}, bf16[2,256,768]{2,1,0:T(8,128)(2,1)}) custom-call(bf16[2048,640]{1,0:T(8,128)(2,1)} %get-tuple-element.94.left, bf16[2048,640]{1,0:T(8,128)(2,1)} %bitcast.101, bf16[2048,768]{1,0:T(8,128)(2,1)} %get-tuple-element.96.feed_left, ...), custom_call_target="tpu_custom_call" | custom-call | tf_op jit(solution)/shard_map/last_fold/pallas_call | solution.py:307
  600.8 1.4 constant_dynamic-slice_fusion
  602.2 1.5 copy.109
  603.7 0.6 collective-permute-start
  604.4 1.3 maximum_convert_fusion.1
  605.7 11.2 %collective-permute-done = bf16[256,1024]{1,0:T(8,128)(2,1)S(1)} collective-permute-done((bf16[256,1024]{1,0:T(8,128)(2,1)S(1)}, bf16[256,1024]{1,0:T(8,128)(2,1)S(1)}, u32[]{:S(2)}, u32[]{:S(2)}) %collective-permute-start) | collective-permute-done | bytes 524320 | tf_op jit(solution)/shard_map/ppermute | solution.py:1941
  618.3 1.1 copy.107
  619.7 0.7 copy.106
  620.6 0.7 copy.105
  622.6 1.0 pad_maximum_fusion.3
  623.6 1.0 pad_maximum_fusion.2
  624.6 1.0 copy.123
  625.6 1.0 copy.124
  (121 shorter events, 10.5 us)
Async XLA Ops:
  7.2 371.4 %reduce-scatter.5.cloned.1.call-start = ((), (), s32[]{:S(2)}) async-start(), calls=%async_computation.4 | async-start | bytes 3932160 | tf_op jit(solution)/shard_map/reduce_scatter | solution.py:1852
  15.0 87.5 %copy-start.10 = (s32[6]{0:T(128)S(1)}, s32[6]{0:T(128)}, u32[]{:S(2)}) copy-start(s32[6]{0:T(128)} %param.17) | copy-start | bytes 76
  100.2 4.5 copy-start.7
  102.1 3.4 copy-start.3
  102.2 4.5 copy-start.8
  106.7 2.0 slice-start
  320.1 121.1 %reduce-scatter.7.cloned.1.call-start = ((), (), s32[]{:S(2)}) async-start(), calls=%async_computation.5 | async-start | bytes 3932160 | tf_op jit(solution)/shard_map/reduce_scatter | solution.py:1852
  374.5 131.9 %reduce-scatter.9.cloned.1.call-start = ((), (), s32[]{:S(2)}) async-start(), calls=%async_computation.6 | async-start | bytes 3932160 | tf_op jit(solution)/shard_map/reduce_scatter | solution.py:1852
  420.3 1.4 copy-start
  420.3 181.8 %reduce-scatter.11.cloned.1.call-start = ((), (), s32[]{:S(2)}) async-start(), calls=%async_computation.7 | async-start | bytes 5242880 | tf_op jit(solution)/shard_map/reduce_scatter | solution.py:1852
  441.2 44.8 %copy-start.9 = (f32[5,384]{1,0:T(8,128)S(1)}, f32[5,384]{1,0:T(8,128)}, u32[]{:S(2)}) copy-start(f32[5,384]{1,0:T(8,128)} %copy-done.8) | copy-start | bytes 23044
  502.0 1.1 copy-start.5
  503.2 1.8 copy-start.4
  600.8 3.5 copy-start.6
  603.7 13.2 %collective-permute-start = (bf16[256,1024]{1,0:T(8,128)(2,1)S(1)}, bf16[256,1024]{1,0:T(8,128)(2,1)S(1)}, u32[]{:S(2)}, u32[]{:S(2)}) collective-permute-start(bf16[256,1024]{1,0:T(8,128)(2,1)S(1)} %dynamic-slice_bitcast_fusion), channel_id=1, source_target_pairs={{0,4},{4,0},{8,12},{12,8},{16,20},{20,16},{24,28},{28,24},{1,5},{5... | collective-permute-start | bytes 1572872 | tf_op jit(solution)/shard_map/ppermute | solution.py:1941
  620.6 5.0 copy-start.1
  621.4 3.2 copy-start.2
Sparse Core Ops, SparseCore 0:
  320.2 58.3 reduce-scatter.4
  380.9 60.2 reduce-scatter.6
  443.5 62.0 reduce-scatter.8
  507.7 76.7 reduce-scatter.10

commit v5 on v4

--- a/solution.py
+++ b/solution.py
@@ -16,6 +16,7 @@
 F32, BF16 = jnp.float32, jnp.bfloat16
 ANY = pl.BlockSpec(memory_space=pl.ANY)
 VMEM = pl.BlockSpec(memory_space=pltpu.VMEM)
+LATE = pl.BlockSpec(memory_space=pl.ANY)
 GRANT = 60 * 1024 * 1024
 NT = (((1,), (1,)), ((), ()))
 TN = (((0,), (0,)), ((), ()))
@@ -304,8 +305,24 @@
 
 
 def call(kernel, outs, ins, scratch, identity, name):
+    late = [k for k, (_, space) in enumerate(ins) if space is LATE]
+    body = kernel
+    if late:
+        held = [pltpu.VMEM(ins[k][0].shape, ins[k][0].dtype) for k in late]
+        scratch = scratch + held + [pltpu.SemaphoreType.DMA((len(late),))]
+
+        def body(*refs):
+            inputs, rest = list(refs[: len(ins)]), refs[len(ins) : -len(late) - 1]
+            fetches = []
+            for i, (k, buffer) in enumerate(zip(late, refs[-len(late) - 1 : -1])):
+                fetches.append(pltpu.make_async_copy(inputs[k], buffer, refs[-1].at[i]))
+                inputs[k] = buffer
+            for fetch in fetches:
+                fetch.start()
+            kernel(*inputs, *rest, fetches=fetches)
+
     results = pl.pallas_call(
-        kernel,
+        body,
         out_shape=[jax.ShapeDtypeStruct(shape, kind) for shape, kind, _ in outs],
         in_specs=[space for _, space in ins],
         out_specs=[space for _, _, space in outs],
@@ -436,155 +453,148 @@
     ]
 
 
-SMALL_GAINS = 5
-
-
-def first_kernel(count, starts, small_top, *refs):
+def first_kernel(count, starts, *refs):
     loads = len(starts)
-    rows = refs[0]
-    halves, refs = refs[1 : 1 + loads], refs[1 + loads :]
-    everything, normed, pre = refs[:3]
+    rows, gains = refs[:2]
+    halves, refs = refs[2 : 2 + loads], refs[2 + loads :]
+    normed, pre, gains_all = refs[:3]
     targets, refs = refs[3 : 3 + loads], refs[3 + loads :]
-    incoming, table, weights, result, tails = refs[:5]
-    incoming_sems, out_sems, weight_sems, result_sems, tail_sem = refs[5:10]
+    own, table, weights, result = refs[:4]
+    gain_send, gain_receive, gain_local, out_sems, weight_sems, result_sems = refs[4:10]
     sems = refs[10:]
-    gather = GroupGather(rows, everything, *sems[:3])
+    dp, tensor = lax.axis_index("dp"), lax.axis_index("tensor")
+    gather = GroupGather(own, table, *sems[:3])
     corner_sems = sems[3:5]
-    small, branch, *others = load(count, starts, halves, targets, sems[5:])
+    branch, small, *others = load(count, starts, halves, targets, sems[5:])
     shares = 2 * count
     line, side, deck, core = spot()
-    greet(cargo_peers(count))
+    greet(
+        [((dp + k) % shares, tensor) for k in range(1, shares)]
+        + [seat(line, side, deck, 1 - core), seat(line, side, 1 - deck, core)]
+    )
+    gain_copies = [
+        remote(
+            gains,
+            gains_all.at[dp],
+            gain_send.at[k],
+            gain_receive.at[k],
+            ((dp + k) % shares, tensor),
+        )
+        for k in range(1, shares)
+    ]
+    gain_copies.append(pltpu.make_async_copy(gains, gains_all.at[dp], gain_local))
+    for copy in gain_copies:
+        copy.start()
+    branch.start()
     small.start()
-    branch.start()
+    for copy in gain_copies:
+        copy.wait()
+
+    block_rows, features = rows.shape
+    slim = features // shares
+    gain = jnp.concatenate(
+        [gains_all[k].astype(F32)[0:1] for k in range(shares)], axis=1
+    )
+
+    def norm_rows(i, carry):
+        where = pl.ds(pl.multiple_of(i * 32, 32), 32)
+        value = rows[where, :].astype(F32)
+        mean = jnp.mean(value * value, axis=1, keepdims=True)
+        own[where, :] = (value * lax.rsqrt(mean + EPSILON) * gain).astype(BF16)
+        return carry
+
+    lax.fori_loop(0, block_rows // 32, norm_rows, 0)
+    branch.second()
     small.second()
-    branch.second()
-    for freight in others:
-        freight.start()
     gather.start()
     gather.start_across()
     small.forward()
+    gather.forward()
+    branch.forward()
+    for freight in others:
+        freight.start()
     for freight in others:
         freight.second()
     small.finish()
-    tail = pltpu.make_async_copy(targets[0], tails, tail_sem)
-    tail.start()
-    tail.wait()
-
-    block_rows, features = rows.shape
-    gain = jnp.concatenate(
-        [
-            tails[
-                k // 2,
-                (k % 2) * (small_top + 16) + small_top : (k % 2 + 1) * (small_top + 16),
-                : features // shares,
-            ].astype(F32)[SMALL_GAINS : SMALL_GAINS + 1]
-            for k in range(shares)
-        ],
-        axis=1,
-    )
-
-    def block(ref, g):
-        return ref.at[pl.ds(pl.multiple_of(g * block_rows, block_rows), block_rows)]
-
-    def norm_blocks(pair):
-        fetches = [
-            pltpu.make_async_copy(everything.at[g], incoming.at[k], incoming_sems.at[k])
-            for k, g in enumerate(pair)
-        ]
-        for fetch in fetches:
-            fetch.start()
-        for k, g in enumerate(pair):
-            fetches[k].wait()
-
-            def norm_rows(i, carry, k=k, g=g):
-                r = pl.multiple_of(i * 32, 32)
-                value = incoming[k, pl.ds(r, 32), :].astype(F32)
-                mean = jnp.mean(value * value, axis=1, keepdims=True)
-                unit = value * lax.rsqrt(mean + EPSILON)
-                base = pl.multiple_of(g * block_rows + r, 32)
-                table[pl.ds(base, 32), :] = (unit * gain).astype(BF16)
-                return carry
-
-            lax.fori_loop(0, block_rows // 32, norm_rows, 0)
-            pltpu.make_async_copy(block(table, g), block(normed, g), out_sems.at[g]).start()
-
-    def both_cores(s, d):
-        return [rank(s, d, core), rank(s, d, 1 - core)]
-
-    gather.landed()
-    branch.forward()
-    gather.forward()
-    for freight in others:
-        freight.forward()
-    norm_blocks(both_cores(side, deck))
-    gather.landed_relays()
-    norm_blocks(both_cores(1 - side, deck))
-    norm_blocks(both_cores(side, 1 - deck))
-    group_finish(gather, *corner_sems, early=True)
-    norm_blocks(both_cores(1 - side, 1 - deck))
+    group_finish(gather, *corner_sems)
+    copies = [
+        pltpu.make_async_copy(
+            table.at[g], normed.at[pl.ds(g * block_rows, block_rows)], out_sems.at[g]
+        )
+        for g in range(8)
+    ]
+    for copy in copies:
+        copy.start()
     branch.finish()
-    depth = targets[1].shape[1]
+    depth = targets[0].shape[1]
     loading = [
         pltpu.make_async_copy(
-            targets[1].at[k], weights.at[pl.ds(k * depth, depth)], weight_sems.at[k]
+            targets[0].at[k], weights.at[pl.ds(k * depth, depth)], weight_sems.at[k]
         )
         for k in range(count)
     ]
     for copy in loading:
         copy.start()
+    for freight in others:
+        freight.forward()
     for copy in loading:
         copy.wait()
     lanes, width = weights.shape[1] // 2, pre.shape[1] // 2
     shift = 2 * lanes - width
-    inside = lax.broadcasted_iota(jnp.int32, (CHUNK, width), 1) < lanes
-    writes = Stream(result, pre, result_sems)
-
-    def product(r):
-        where = pl.ds(r, CHUNK)
-        both = jnp.dot(table[where, :], weights[...], preferred_element_type=F32)
+    inside = lax.broadcasted_iota(jnp.int32, (block_rows, width), 1) < lanes
+
+    def write(g):
+        where = pl.ds(pl.multiple_of(g * block_rows, block_rows), block_rows)
+        return pltpu.make_async_copy(result.at[where], pre.at[where], result_sems.at[g])
+
+    def product(g, carry):
+        where = pl.ds(pl.multiple_of(g * block_rows, block_rows), block_rows)
+        both = jnp.dot(table[g], weights[...], preferred_element_type=F32)
         result[where, :width] = jnp.where(inside, both[:, :width], 0.0)
         later = pltpu.roll(both[:, shift:], lanes, 1)
         result[where, width:] = jnp.where(inside, later, 0.0)
-        writes.start(r)
-
-    chunks(pre.shape[0], product)
+        write(g).start()
+        return carry
+
+    lax.fori_loop(0, 8, product, 0)
     for g in range(8):
-        pltpu.make_async_copy(block(table, g), block(normed, g), out_sems.at[g]).wait()
-    writes.wait_all()
+        copies[g].wait()
+        write(g).wait()
     for freight in others:
         freight.finish()
 
 
-def first(count, rows, cargo, width):
+def first(count, rows, gains, cargo, width):
     total = 8 * rows.shape[0]
-    small, branch = cargo[:2]
+    shares = 2 * count
+    branch = cargo[0]
     out = call(
-        functools.partial(first_kernel, count, cargo_starts(cargo), small.shape[1] - 16),
+        functools.partial(first_kernel, count, cargo_starts(cargo)),
         [
-            ((8,) + rows.shape, BF16, ANY),
             ((total, rows.shape[1]), BF16, ANY),
             ((total, 2 * width), F32, ANY),
+            ((shares,) + gains.shape, BF16, VMEM),
         ]
         + cargo_outs(count, cargo),
-        [(rows, ANY)] + cargo_ins(cargo),
+        [(rows, VMEM), (gains, VMEM)] + cargo_ins(cargo),
         [
-            pltpu.VMEM((2,) + rows.shape, BF16),
-            pltpu.VMEM((total, rows.shape[1]), BF16),
+            pltpu.VMEM(rows.shape, BF16),
+            pltpu.VMEM((8,) + rows.shape, BF16),
             pltpu.VMEM((rows.shape[1], branch.shape[2]), BF16),
             pltpu.VMEM((total, 2 * width), F32),
-            pltpu.VMEM(piece_shape(count, small), BF16),
-            pltpu.SemaphoreType.DMA((2,)),
+            pltpu.SemaphoreType.DMA((shares,)),
+            pltpu.SemaphoreType.DMA((shares,)),
+            pltpu.SemaphoreType.DMA,
             pltpu.SemaphoreType.DMA((8,)),
             pltpu.SemaphoreType.DMA((count,)),
-            pltpu.SemaphoreType.DMA((total // CHUNK,)),
-            pltpu.SemaphoreType.DMA,
+            pltpu.SemaphoreType.DMA((8,)),
         ]
         + rows_scratch()
         + cargo_scratch(count, cargo),
         0,
         "first",
     )
-    return out[1:4] + flat_rows(out[4:])
+    return out[:3] + flat_rows(out[3:])
 
 
 def rows_kernel(count, starts, *refs):
@@ -598,12 +608,12 @@
     for freight in freights:
         freight.start()
     gather.start()
+    gather.start_across()
     for freight in freights:
         freight.second()
-    gather.start_across()
-    gather.forward()
     for freight in freights:
         freight.forward()
+    gather.forward()
     group_finish(gather, *sems[3:5])
     for freight in freights:
         freight.finish()
@@ -633,34 +643,27 @@
     lax.fori_loop(low, high, body, 0)
 
 
-def plain_rows_kernel(rows, left, right, everything, product, left_here, right_here, *sems):
+def plain_rows_kernel(rows, left, right, everything, product_out, product, *sems, fetches):
     gather = GroupGather(rows, everything, *sems[1:4])
-    loading = [
-        pltpu.make_async_copy(left, left_here, sems[0].at[0]),
-        pltpu.make_async_copy(right, right_here, sems[0].at[1]),
-    ]
     greet(group_peers())
     gather.start()
     gather.start_across()
-    for copy in loading:
-        copy.start()
-    for copy in loading:
-        copy.wait()
-    turned(left_here, right_here, product, 4, 0, 4)
+    for fetch in fetches:
+        fetch.wait()
+    turned(left, right, product, 4, 0, 4)
+    writing = pltpu.make_async_copy(product, product_out, sems[0])
+    writing.start()
     gather.forward()
     group_finish(gather, *sems[4:6])
+    writing.wait()
 
 
 def gather_plain(rows, left, right, identity):
     out = call(
         plain_rows_kernel,
-        [((8,) + rows.shape, BF16, ANY), ((left.shape[1], right.shape[1]), BF16, VMEM)],
-        [(rows, ANY), (left, ANY), (right, ANY)],
-        [
-            pltpu.VMEM(left.shape, BF16),
-            pltpu.VMEM(right.shape, BF16),
-            pltpu.SemaphoreType.DMA((2,)),
-        ]
+        [((8,) + rows.shape, BF16, ANY), ((left.shape[1], right.shape[1]), BF16, ANY)],
+        [(rows, ANY), (left, LATE), (right, LATE)],
+        [pltpu.VMEM((left.shape[1], right.shape[1]), BF16), pltpu.SemaphoreType.DMA]
         + rows_scratch(),
         identity,
         "gather_rows",
@@ -909,7 +912,7 @@
     return scale * (grad_unit - unit * inner), jnp.sum(grad * unit, axis=0, keepdims=True)
 
 
-def mixer_fold_kernel(count, jobs, starts, left, right, *refs):
+def mixer_fold_kernel(count, jobs, starts, left, right, *refs, fetches):
     loads = len(starts)
     inputs, gain, refs = refs[0], refs[1], refs[2:]
     halves, refs = refs[:loads], refs[loads:]
@@ -920,11 +923,15 @@
     greet(cargo_peers(count))
     for freight in freights:
         freight.start()
+    for fetch in fetches[:2]:
+        fetch.wait()
     fold.begin(freights)
     fold.middle()
     for freight in freights:
         freight.forward()
 
+    fetches[2].wait()
+
     def store(here, value):
         value = value + inputs[here, :].astype(F32)
         out[here, :] = value
@@ -938,10 +945,10 @@
 def plan_of(lefts_rights):
     lefts, rights, plan = [], [], []
     for k, (left, parts) in enumerate(lefts_rights):
-        lefts.append((left, VMEM))
+        lefts.append((left, LATE))
         start = 0
         for part in parts:
-            rights.append((part, VMEM))
+            rights.append((part, LATE))
             plan.append((k, start))
             start += part.shape[1]
     return plan, lefts + rights
@@ -953,7 +960,7 @@
     out = call(
         functools.partial(mixer_fold_kernel, count, [plan], cargo_starts(cargo)),
         [((rows, width), F32, VMEM), ((rows, width), BF16, VMEM)] + cargo_outs(count, cargo),
-        ins + [(inputs, VMEM), (gain, VMEM)] + cargo_ins(cargo),
+        ins + [(inputs, LATE), (gain, VMEM)] + cargo_ins(cargo),
         Fold.scratch(rows, width) + cargo_scratch(count, cargo),
         3,
         "mixer_fold",
@@ -961,19 +968,22 @@
     return out[:2] + flat_rows(out[2:])
 
 
-def feed_fold_kernel(plan, parts, left, other, *refs):
+def feed_fold_kernel(plan, parts, left, other, *refs, fetches):
     rights, refs = refs[:parts], refs[parts:]
     normed, hidden, cotangent, gain, refs = *refs[:4], refs[4:]
-    out, low, gain_sum, grads = refs[:4]
+    out, low, gain_sum, grads_out = refs[:4]
     fold = Fold(plan, [left, other], rights, out, refs[4:15])
-    normed_here, load_sem = refs[15:]
+    grads, write_sem = refs[15:]
     greet(group_peers())
-    loading = pltpu.make_async_copy(normed, normed_here, load_sem)
-    loading.start()
+    for fetch in fetches[: 2 + parts]:
+        fetch.wait()
     fold.begin()
     fold.middle()
-    loading.wait()
-    turned(normed_here, left, grads, 4, 0, 4)
+    for fetch in fetches[2 + parts :]:
+        fetch.wait()
+    turned(normed, left, grads, 4, 0, 4)
+    writing = pltpu.make_async_copy(grads, grads_out, write_sem)
+    writing.start()
     gain_sum[...] = jnp.zeros_like(gain_sum)
 
     def store(here, value):
@@ -985,6 +995,7 @@
         low[here, :] = back.astype(BF16)
 
     fold.finish(store)
+    writing.wait()
 
 
 def feed_fold(grad_gating, grad_lifting, gates, ups, normed, hidden, cotangent, gain):
@@ -996,17 +1007,20 @@
             ((rows, width), F32, VMEM),
             ((rows, width), BF16, VMEM),
             ((8, width), F32, VMEM),
-            ((normed.shape[1], grad_gating.shape[1]), BF16, VMEM),
+            ((normed.shape[1], grad_gating.shape[1]), BF16, ANY),
         ],
-        ins + [(normed, ANY), (hidden, VMEM), (cotangent, VMEM), (gain, VMEM)],
+        ins + [(normed, LATE), (hidden, LATE), (cotangent, LATE), (gain, VMEM)],
         Fold.scratch(rows, width)
-        + [pltpu.VMEM(normed.shape, BF16), pltpu.SemaphoreType.DMA],
+        + [
+            pltpu.VMEM((normed.shape[1], grad_gating.shape[1]), BF16),
+            pltpu.SemaphoreType.DMA,
+        ],
         6,
         "feed_fold",
     )
 
 
-def last_fold_kernel(count, plans, parts, swaps, left, right, feed_left, *refs):
+def last_fold_kernel(count, plans, parts, swaps, left, right, feed_left, *refs, fetches):
     rights, refs = refs[:parts], refs[parts:]
     inputs, gain, grad_hidden, hidden, second, refs = *refs[:5], refs[5:]
     values, refs = refs[:swaps], refs[swaps:]
@@ -1019,7 +1033,11 @@
     gain_sum = GainSum(count, sums, totals, *refs[25:])
     greet(whole_group() + line_peers(count))
     swap.start()
+    for fetch in fetches[:2]:
+        fetch.wait()
     fold.begin()
+    for fetch in fetches[2:]:
+        fetch.wait()
     feed.begin()
     fold.middle()
     feed.middle()
@@ -1063,7 +1081,13 @@
         + [(value.shape, BF16, ANY) for value in swaps],
         ins
         + feed_ins
-        + [(value, VMEM) for value in (inputs, gain, grad_hidden, hidden, second)]
+        + [
+            (inputs, LATE),
+            (gain, VMEM),
+            (grad_hidden, LATE),
+            (hidden, LATE),
+            (second, VMEM),
+        ]
         + [(value, ANY) for value in swaps],
         [
             pltpu.VMEM((rows, width), F32),
@@ -1274,16 +1298,16 @@
             stream.start(r)
 
     pieces = rows // CHUNK
-    spans(0, pieces // 4, gate_chunk)
+    spans(0, 1, gate_chunk)
     for freight in freights:
         freight.second()
     gather.start_across()
-    spans(pieces // 4, pieces, gate_chunk)
+    spans(1, pieces, gate_chunk)
     prod, total = tile_scan(prods, sums, rows, width, False)
-    gather.forward()
     entering = pool(count, prod, total, outgoing, slots, send, receive, False)
     for freight in freights:
         freight.forward()
+    gather.forward()
     state[0:8, :] = entering
     heads[0].start()
 
@@ -1361,7 +1385,7 @@
     return out[:6] + [out[6].reshape(-1, cotangent.shape[1])] + flat_rows(out[7:])
 
 
-def back_kernel(count, lanes, swaps, *refs):
+def back_kernel(count, lanes, swaps, *refs, fetches):
     pre, low, outlet = refs[:3]
     saved, refs = refs[3:8], refs[8:]
     masks, table, gate_weights = refs[:3]
@@ -1403,6 +1427,8 @@
         stream.start_all()
     greet(line_peers(count) + ([seat(line, 1 - side, deck, core)] if swaps else []))
     swap.start()
+    for copy in fetches:
+        copy.wait()
 
     def direct(i, carry):
         r = pl.multiple_of(i * CHUNK, CHUNK)
@@ -1533,9 +1559,9 @@
             ((8, width), F32, VMEM),
         ]
         + [(value.shape, BF16, ANY) for value in swaps],
-        [(pre, ANY), (low, ANY), (outlet, VMEM)]
+        [(pre, ANY), (low, ANY), (outlet, LATE)]
         + [(value, ANY) for value in saved]
-        + [(value, VMEM) for value in (masks, table, gate_weights)]
+        + [(masks, LATE), (table, VMEM), (gate_weights, LATE)]
         + [(value, ANY) for value in swaps],
         [
             pltpu.VMEM((rows, width), F32),
@@ -1768,25 +1794,21 @@
     own = jnp.pad(own, ((0, 0), (0, 0), (0, head_width - piece)))
     own = jnp.roll(own, mine * piece, axis=2)
     own = own.reshape(TAPS + 1, 2, lanes).transpose(1, 0, 2)
-    gains_own = jnp.pad(
-        jnp.stack([mixer_gain, feed_gain]), ((0, 16 - TAPS - 3), (0, width - slim))
-    )
-    tail = jnp.concatenate(
-        [widen(own, width), jnp.broadcast_to(gains_own, (2,) + gains_own.shape)], axis=1
-    )
+    gains_own = jnp.pad(jnp.stack([mixer_gain, feed_gain]), ((0, 14), (0, 0)))
+    tail = jnp.pad(widen(own, width), ((0, 0), (0, 15 - TAPS), (0, 0)))
     small_top = -(-half_heads * piece // 16) * 16
     small = jnp.concatenate(
         [jnp.pad(blocks, ((0, 0), (0, small_top - half_heads * piece), (0, 0))), tail], axis=1
     )
 
-    normed_one, pre, small_all, branch_all, gate_first = first(
-        count, layer_input, [small, branch_halves, (feed_gate, 0, narrow)], width
+    normed_one, pre, gains_all, branch_all, small_all, gate_first = first(
+        count, layer_input, gains_own, [branch_halves, small, (feed_gate, 0, narrow)], width
     )
 
     small_all = small_all.reshape(shares, -1, width)
     tails = small_all[:, small_top:].astype(F32)
-    gain_first = tails[:, SMALL_GAINS, :slim].reshape(feature_count)
-    gain_second = tails[:, SMALL_GAINS + 1, :slim].reshape(feature_count)
+    gain_first = gains_all[:, 0].reshape(feature_count).astype(F32)
+    gain_second = gains_all[:, 1].reshape(feature_count).astype(F32)
     sums = jnp.sum(tails[:, : TAPS + 1], axis=0)
     decay_flat = sums[TAPS, :lanes]
     inside = (jnp.arange(width) < lanes)[None]

time: 639 us -> 624 us (0.977)
  Pallas kernels: 530 us -> 512 us
    pallas_call x9, Pallas kernels: 530 us -> 512 us  [call(): pl.pallas_call(body, out_shape=[jax.ShapeDtypeStruct(shape, kind) for sha...]
where the time goes in v5:
time: 624 us; the launch traced here: 618 us
  Pallas kernels  512 us (82%)
  waiting for transfers between devices  30.1 us (5%)
  local copies, waits for them, and re-layouts  23.8 us (4%)
  other arithmetic  20.1 us (3%)
  matrix products  16.9 us (3%)
  between operations  14.7 us (2%)
    pallas_call x9, Pallas kernels, call(): pl.pallas_call(body, out_shape=[jax.ShapeDtypeStruct(shape, kind) for sha...  512 us
    reduce_scatter x4, waiting for transfers between devices, line_sum(): lax.psum_scatter(value, 'dp', scatter_dimension=0, axis_index_groups=line...  18.9 us
    dot_general x2, matrix products, by_rows(): lax.dot_general(left, right, TN, preferred_element_type=F32).astype(BF16)  16.9 us
  transfers between devices with their start and end apart: 5, of which 3 were waited for; matrix products, arithmetic and copies ran while one was open for 5% of the time, Pallas kernels for 37%

profile of v5, /device:TPU:0, one launch (start us, length us, event | category | flops | bytes accessed | tf_op | source)
XLA Modules:
  0.0 618.5 jit_solution(14381824640413645899)
XLA Ops:
  7.4 0.7 fusion.21
  8.3 0.9 pad_maximum_fusion.6
  9.2 1.1 copy.84
  10.6 1.1 copy.86
  12.0 0.7 fusion.15.refs_3_
  12.7 1.0 pad_maximum_fusion.1.refs_2_
  14.3 76.5 %first.1 = (bf16[2048,2048]{1,0:T(8,128)(2,1)}, f32[2048,768]{1,0:T(8,128)}, bf16[8,16,256]{2,1,0:T(8,128)(2,1)}, bf16[4,512,640]{2,1,0:T(8,128)(2,1)}, bf16[4,1...) custom-call(bf16[256,2048]{1,0:T(8,128)(2,1)} %refs_5_.1, bf16[16,256]{1,0:T(8,128)(2,1)} %fusion.22.refs_1_, ...), custom_call_target="tpu_custom_call" | custom-call | tf_op jit(solution)/shard_map/first/pallas_call | solution.py:324
  90.8 1.0 slice.196
  91.8 0.9 convert_reduce_fusion
  94.1 1.0 convert_element_type.105.refs_1_.refs_8_
  95.4 0.9 fusion.42
  96.3 0.6 convert.36.refs_3_.refs_9_
  96.9 1.2 copy.94
  98.3 0.9 fusion.2.refs_3_.refs_10_
  99.3 0.8 pad.53.refs_5_
  100.1 0.7 maximum_maximum_fusion.refs_2_.refs_9_
  100.7 55.6 %scan_forward.1 = (f32[2048,384]{1,0:T(8,128)}, f32[2048,384]{1,0:T(8,128)}, f32[2048,384]{1,0:T(8,128)}, f32[2056,384]{1,0:T(8,128)}, bf16[2048,384]{1,0:T(8,12...) custom-call(f32[2048,768]{1,0:T(8,128)} %get-tuple-element.62.refs_0, ...), custom_call_target="tpu_custom_call" | custom-call | tf_op jit(solution)/shard_map/scan_forward/pallas_call | solution.py:324
  156.3 59.1 %mixer_fold.1 = (f32[256,2048]{1,0:T(8,128)}, bf16[256,2048]{1,0:T(8,128)(2,1)}, bf16[4,512,512]{2,1,0:T(8,128)(2,1)}, bf16[4,512,256]{2,1,0:T(8,128)(2,1)}) custom-call(bf16[2048,384]{1,0:T(8,128)(2,1)} %get-tuple-element.64.refs_0_, bf16[2048,384]{1,0:T(8,128)(2,1)} %bitcast.87, bf16[256,2048]{1,0:T(8,128)(2,1)} %refs_5_.1, ...), custom_call_target="tpu_custom_call" | custom-call | tf_op jit(solution)/shard_map/mixer_fold/pallas_call | solution.py:324
  215.5 46.3 %gather_rows.2 = (bf16[8,256,2048]{2,1,0:T(8,128)(2,1)}, bf16[4,512,512]{2,1,0:T(8,128)(2,1)}) custom-call(bf16[256,2048]{1,0:T(8,128)(2,1)} %get-tuple-element.67.refs_0_, bf16[256,1536]{1,0:T(8,128)(2,1)} %refs_1_.1), custom_call_target="tpu_custom_call" | custom-call | tf_op jit(solution)/shard_map/gather_rows/pallas_call | solution.py:324
  261.8 48.3 %feed.1 = (bf16[2048,768]{1,0:T(8,128)(2,1)}, bf16[2048,768]{1,0:T(8,128)(2,1)}, bf16[2048,768]{1,0:T(8,128)(2,1)}, bf16[2048,768]{1,0:T(8,128)(2,1)}, bf16[4,512,512]{2,1,0:T(8,128)(2,1)}) custom-call(bf16[2048,2048]{1,0:T(8,128)(2,1)} %bitcast.75, bf16[2048,2048]{1,0:T(8,128)(2,1)} %bitcast.78, bf16[2048,256]{1,0:T(8,128)(2,1)} %bitcast.89, ...), custom_call_target="tpu_custom_call" | custom-call | tf_op jit(solution)/shard_map/feed/pallas_call | solution.py:324
  310.7 52.2 %feed_fold.1 = (f32[256,2048]{1,0:T(8,128)}, bf16[256,2048]{1,0:T(8,128)(2,1)}, f32[8,2048]{1,0:T(8,128)}, bf16[2048,768]{1,0:T(8,128)(2,1)}) custom-call(bf16[2048,768]{1,0:T(8,128)(2,1)} %get-tuple-element.75.refs_0_, bf16[2048,768]{1,0:T(8,128)(2,1)} %get-tuple-element.76.refs_1_.refs_2_, bf16[2048,256]{1,0:T(8,128)(2,1)} %bitcast.90, ...), custom_call_target="tpu_custom_call" | custom-call | tf_op jit(solution)/shard_map/feed_fold/pallas_call | solution.py:324
  363.0 5.8 reduce-scatter.5.cloned.1.call-done
  368.7 40.1 %gather_rows.3 = (bf16[8,256,2048]{2,1,0:T(8,128)(2,1)}, bf16[2048,768]{1,0:T(8,128)(2,1)}) custom-call(bf16[256,2048]{1,0:T(8,128)(2,1)} %get-tuple-element.80.refs_0_, bf16[2048,2048]{1,0:T(8,128)(2,1)} %bitcast.77, bf16[2048,768]{1,0:T(8,128)(2,1)} %get-tuple-element.76.refs_1_.refs_2_), custom_call_target="tpu_custom_call" | custom-call | tf_op jit(solution)/shard_map/gather_rows/pallas_call | solution.py:324
  408.9 1.3 copy-done
  410.3 8.0 %convolution_convert_fusion.1 = bf16[2048,384]{1,0:T(8,128)(2,1)S(1)} fusion(bf16[2048,2048]{1,0:T(8,128)(2,1)} %bitcast.79, bf16[2048,384]{1,0:T(8,128)(2,1)S(1)} %copy-done), kind=kOutput, calls=%fused_computation.2 | convolution fusion | flops 3222011904 | bytes 11534336 | tf_op jit(solution)/shard_map/dot_general | solution.py:1750
  418.3 13.1 %reduce-scatter.7.cloned.1.call-done = bf16[512,768]{1,0:T(8,128)(2,1)} async-done(((bf16[2048,768]{1,0:T(8,128)(2,1)}), bf16[512,768]{1,0:T(8,128)(2,1)}) %reduce-scatter.7.cloned.1.call-update) | async-done | bytes 786448 | tf_op jit(solution)/shard_map/reduce_scatter | solution.py:1874
  431.4 43.4 %scan_backward.1 = (bf16[2048,640]{1,0:T(8,128)(2,1)}, f32[384,768]{1,0:T(8,128)}, f32[8,384]{1,0:T(8,128)}, bf16[2,256,768]{2,1,0:T(8,128)(2,1)}, bf16[2,256,768]{2,1,0:T(8,128)(2,1)}) custom-call(f32[2048,768]{1,0:T(8,128)} %get-tuple-element.62.refs_0_, bf16[2048,2048]{1,0:T(8,128)(2,1)} %bitcast.80, bf16[2048,384]{1,0:T(8,128)(2,1)} %bitcast.88, ...), custom_call_target="tpu_custom_call" | custom-call | tf_op jit(solution)/shard_map/scan_backward/pallas_call | solution.py:324
  474.8 0.7 slice.247
  475.5 0.7 convert_reduce_fusion.8
  476.4 1.3 convert.32
  479.5 0.7 copy.97
  480.3 8.9 %convolution_convert_fusion = bf16[2048,640]{0,1:T(8,128)(2,1)S(1)} fusion(bf16[2048,2048]{1,0:T(8,128)(2,1)} %get-tuple-element.95, bf16[2048,640]{1,0:T(8,128)(2,1)} %get-tuple-element.96.refs_0_), kind=kOutput, calls=%fused_computation.1 | convolution fusion | flops 5370019840 | bytes 13631488 | tf_op jit(solution)/shard_map/dot_general | solution.py:1750
  489.2 2.2 pad_maximum_fusion
  492.8 1.6 copy.104
  494.5 1.3 maximum_convert_fusion
  495.8 90.2 %last_fold.1 = (bf16[256,2048]{1,0:T(8,128)(2,1)}, bf16[256,2048]{1,0:T(8,128)(2,1)}, f32[16,256]{1,0:T(8,128)}, bf16[2,256,768]{2,1,0:T(8,128)(2,1)}) custom-call(bf16[2048,640]{1,0:T(8,128)(2,1)} %get-tuple-element.96.refs_0_, bf16[2048,640]{1,0:T(8,128)(2,1)} %bitcast.97, bf16[2048,768]{1,0:T(8,128)(2,1)} %get-tuple-element.98.refs_2_, ...), custom_call_target="tpu_custom_call" | custom-call | tf_op jit(solution)/shard_map/last_fold/pallas_call | solution.py:324
  586.0 1.4 constant_dynamic-slice_fusion
  587.4 1.5 copy.105
  588.9 0.6 collective-permute-start
  589.6 1.3 maximum_convert_fusion.1
  590.9 11.2 %collective-permute-done = bf16[256,1024]{1,0:T(8,128)(2,1)S(1)} collective-permute-done((bf16[256,1024]{1,0:T(8,128)(2,1)S(1)}, bf16[256,1024]{1,0:T(8,128)(2,1)S(1)}, u32[]{:S(2)}, u32[]{:S(2)}) %collective-permute-start) | collective-permute-done | bytes 524320 | tf_op jit(solution)/shard_map/ppermute | solution.py:1963
  603.5 1.1 copy.103
  604.9 0.7 copy.102
  605.8 0.7 copy.101
  607.8 1.0 pad_maximum_fusion.3
  608.8 1.0 pad_maximum_fusion.2
  609.8 1.0 copy.115
  610.8 1.0 copy.116
  (122 shorter events, 10.5 us)
Async XLA Ops:
  7.2 4.8 copy-start.11
  7.2 4.8 copy-start.12
  7.2 361.5 %reduce-scatter.5.cloned.1.call-start = ((), (), s32[]{:S(2)}) async-start(), calls=%async_computation.4 | async-start | bytes 3932160 | tf_op jit(solution)/shard_map/reduce_scatter | solution.py:1874
  14.3 78.7 %copy-start.10 = (s32[6]{0:T(128)S(1)}, s32[6]{0:T(128)}, u32[]{:S(2)}) copy-start(s32[6]{0:T(128)} %param.17) | copy-start | bytes 76
  90.8 4.4 copy-start.7
  91.8 5.0 copy-start.3
  92.7 5.3 copy-start.8
  98.0 2.0 slice-start
  310.2 121.2 %reduce-scatter.7.cloned.1.call-start = ((), (), s32[]{:S(2)}) async-start(), calls=%async_computation.5 | async-start | bytes 3932160 | tf_op jit(solution)/shard_map/reduce_scatter | solution.py:1874
  362.9 132.9 %reduce-scatter.9.cloned.1.call-start = ((), (), s32[]{:S(2)}) async-start(), calls=%async_computation.6 | async-start | bytes 3932160 | tf_op jit(solution)/shard_map/reduce_scatter | solution.py:1874
  408.8 1.4 copy-start
  408.9 178.5 %reduce-scatter.11.cloned.1.call-start = ((), (), s32[]{:S(2)}) async-start(), calls=%async_computation.7 | async-start | bytes 5242880 | tf_op jit(solution)/shard_map/reduce_scatter | solution.py:1874
  431.4 44.1 %copy-start.9 = (f32[5,384]{1,0:T(8,128)S(1)}, f32[5,384]{1,0:T(8,128)}, u32[]{:S(2)}) copy-start(f32[5,384]{1,0:T(8,128)} %copy-done.8) | copy-start | bytes 23044
  491.4 1.1 copy-start.5
  492.6 1.8 copy-start.4
  586.0 3.5 copy-start.6
  588.9 13.2 %collective-permute-start = (bf16[256,1024]{1,0:T(8,128)(2,1)S(1)}, bf16[256,1024]{1,0:T(8,128)(2,1)S(1)}, u32[]{:S(2)}, u32[]{:S(2)}) collective-permute-start(bf16[256,1024]{1,0:T(8,128)(2,1)S(1)} %dynamic-slice_bitcast_fusion), channel_id=1, source_target_pairs={{0,4},{4,0},{8,12},{12,8},{16,20},{20,16},{24,28},{28,24},{1,5},{5... | collective-permute-start | bytes 1572872 | tf_op jit(solution)/shard_map/ppermute | solution.py:1963
  605.8 5.0 copy-start.1
  606.6 3.2 copy-start.2
Sparse Core Ops, SparseCore 0:
  310.3 58.3 reduce-scatter.4
  371.0 60.2 reduce-scatter.6
  433.7 62.0 reduce-scatter.8
  497.9 76.7 reduce-scatter.10

commit v6 on v5

--- a/solution.py
+++ b/solution.py
@@ -4,6 +4,7 @@
 import jax.numpy as jnp
 from jax import lax
 from jax.experimental import pallas as pl
+from jax.experimental.layout import Layout, with_layout_constraint
 from jax.experimental.pallas import tpu as pltpu
 from jax.sharding import PartitionSpec as P
 
@@ -20,7 +21,7 @@
 GRANT = 60 * 1024 * 1024
 NT = (((1,), (1,)), ((), ()))
 TN = (((0,), (0,)), ((), ()))
-CHUNK = 256
+CHUNK = 512
 
 
 def spot():
@@ -731,7 +732,7 @@
 class Fold:
     OWN, ACROSS, ABOVE, CORNER = 0, 1, 2, 3
 
-    def __init__(self, plan, lefts, rights, out, refs):
+    def __init__(self, plan, lefts, rights, out, refs, uneven=0):
         self.plan, self.lefts, self.rights, self.out = plan, lefts, rights, out
         self.mine, self.stage, self.near = refs[:3]
         self.across_sum, self.above_sum, self.leaving, self.arriving = refs[3:7]
@@ -740,17 +741,21 @@
         sibling, across, above = group_peers()
         self.sibling = sibling
         self.rows, self.width = out.shape
-        self.half = self.rows // 2
+        self.cut = (self.rows // 2 + uneven, self.rows // 2 - uneven)
         self.ships = [
             remote(
-                self.leaving.at[k], self.arriving.at[k], send.at[k], receive.at[k], peer
+                self.leaving.at[k, pl.ds(0, self.cut[k % 2])],
+                self.arriving.at[k, pl.ds(0, self.cut[k % 2])],
+                send.at[k],
+                receive.at[k],
+                peer,
             )
             for k, peer in enumerate((above, across, above, across, across, above))
         ]
 
     @staticmethod
-    def scratch(rows, width):
-        half = rows // 2
+    def scratch(rows, width, uneven=0):
+        half = rows // 2 + uneven
         return [
             pltpu.VMEM((rows, width), F32),
             pltpu.VMEM((2, rows, width), BF16),
@@ -785,12 +790,12 @@
 
         lax.fori_loop(0, self.width // step, body, 0)
 
-    def sweep(self, action):
+    def sweep(self, part, action):
         def body(i, carry):
             action(pl.multiple_of(i * 16, 16))
             return carry
 
-        lax.fori_loop(0, self.half // 16, body, 0)
+        lax.fori_loop(0, self.cut[part] // 16, body, 0)
 
     def near_copy(self, q):
         return remote(
@@ -802,7 +807,7 @@
         )
 
     def chip_sum(self, q, h, r):
-        place = pl.ds(h * self.half + r, 16)
+        place = pl.ds(h * self.cut[0] + r, 16)
         return self.mine[place, :] + self.near[q, place, :].astype(F32)
 
     def block(self, q):
@@ -833,68 +838,59 @@
     def begin(self, freights=()):
         self.block(self.CORNER)
 
-        def corner(r):
-            for h in range(2):
-                self.leaving[h, pl.ds(r, 16), :] = self.chip_sum(self.CORNER, h, r).astype(BF16)
-
-        self.sweep(corner)
-        self.send(0)
-        self.send(1)
+        def depart(k, q, part):
+            def action(r):
+                self.leaving[k, pl.ds(r, 16), :] = self.chip_sum(q, part, r).astype(BF16)
+
+            self.sweep(part, action)
+            self.send(k)
+
+        def stay(sums, q, part):
+            def action(r):
+                sums[pl.ds(r, 16), :] = self.chip_sum(q, part, r)
+
+            self.sweep(part, action)
+
+        depart(0, self.CORNER, 0)
+        depart(1, self.CORNER, 1)
         self.block(self.ABOVE)
-
-        def above(r):
-            place = pl.ds(r, 16)
-            self.leaving[2, place, :] = self.chip_sum(self.ABOVE, 0, r).astype(BF16)
-            self.above_sum[place, :] = self.chip_sum(self.ABOVE, 1, r)
-
-        self.sweep(above)
-        self.send(2)
+        depart(2, self.ABOVE, 0)
+        stay(self.above_sum, self.ABOVE, 1)
         for freight in freights:
             freight.second()
         self.block(self.ACROSS)
-
-        def across(r):
-            place = pl.ds(r, 16)
-            self.leaving[3, place, :] = self.chip_sum(self.ACROSS, 1, r).astype(BF16)
-            self.across_sum[place, :] = self.chip_sum(self.ACROSS, 0, r)
-
-        self.sweep(across)
-        self.send(3)
+        depart(3, self.ACROSS, 1)
+        stay(self.across_sum, self.ACROSS, 0)
         self.block(self.OWN)
 
     def middle(self):
-        self.ships[0].wait_recv()
-
-        def across(r):
-            place = pl.ds(r, 16)
-            total = self.across_sum[place, :] + self.arriving[0, place, :].astype(F32)
-            self.leaving[4, place, :] = total.astype(BF16)
-
-        self.sweep(across)
-        self.send(4)
-        self.ships[1].wait_recv()
-
-        def above(r):
-            place = pl.ds(r, 16)
-            total = self.above_sum[place, :] + self.arriving[1, place, :].astype(F32)
-            self.leaving[5, place, :] = total.astype(BF16)
-
-        self.sweep(above)
-        self.send(5)
+        for k, sums in enumerate((self.across_sum, self.above_sum)):
+            self.ships[k].wait_recv()
+
+            def action(r, k=k, sums=sums):
+                place = pl.ds(r, 16)
+                total = sums[place, :] + self.arriving[k, place, :].astype(F32)
+                self.leaving[4 + k, place, :] = total.astype(BF16)
+
+            self.sweep(k, action)
+            self.send(4 + k)
 
     def finish(self, store):
         for k in range(2, 6):
             self.ships[k].wait_recv()
 
-        def total(r):
-            for h, pair in enumerate(((2, 4), (3, 5))):
-                place, here = pl.ds(r, 16), pl.ds(h * self.half + r, 16)
+        for part in range(2):
+
+            def total(r, part=part):
+                place = pl.ds(r, 16)
+                here = pl.ds(pl.multiple_of(part * self.cut[0] + r, 16), 16)
                 value = self.out[here, :] + self.near[self.OWN, here, :].astype(F32)
-                for k in pair:
+                for k in (2 + part, 4 + part):
                     value = value + self.arriving[k, place, :].astype(F32)
                 store(here, value)
 
-        self.sweep(total)
+            self.sweep(part, total)
+
         for k in range(6):
             self.ships[k].wait_send()
         for q in range(2):
@@ -1020,6 +1016,9 @@
     )
 
 
+UNEVEN = 16
+
+
 def last_fold_kernel(count, plans, parts, swaps, left, right, feed_left, *refs, fetches):
     rights, refs = refs[:parts], refs[parts:]
     inputs, gain, grad_hidden, hidden, second, refs = *refs[:5], refs[5:]
@@ -1027,8 +1026,8 @@
     input_grad, output, totals = refs[:3]
     swapped, refs = refs[3 : 3 + swaps], refs[3 + swaps :]
     out, feed_out, sums, terms_here, refs = *refs[:4], refs[4:]
-    fold = Fold(plans[0], [left], [right], out, refs[:11])
-    feed = Fold(plans[1], [feed_left], rights, feed_out, refs[11:22])
+    fold = Fold(plans[0], [left], [right], out, refs[:11], UNEVEN)
+    feed = Fold(plans[1], [feed_left], rights, feed_out, refs[11:22], UNEVEN)
     swap = Swap(values, swapped, *refs[22:25])
     gain_sum = GainSum(count, sums, totals, *refs[25:])
     greet(whole_group() + line_peers(count))
@@ -1036,11 +1035,10 @@
     for fetch in fetches[:2]:
         fetch.wait()
     fold.begin()
+    fold.middle()
     for fetch in fetches[2:]:
         fetch.wait()
     feed.begin()
-    fold.middle()
-    feed.middle()
     terms_here[...] = jnp.zeros_like(terms_here)
 
     def store(here, value):
@@ -1056,6 +1054,7 @@
         sums[k : k + 1, :] = terms_here[0:1, columns]
         sums[shares + k : shares + k + 1, :] = second[0:1, columns]
     gain_sum.start()
+    feed.middle()
     gain_sum.second()
 
     def store_output(here, value):
@@ -1095,7 +1094,7 @@
             pltpu.VMEM(both.shape, F32),
             pltpu.VMEM((8, width), F32),
         ]
-        + Fold.scratch(rows, width) * 2
+        + Fold.scratch(rows, width, UNEVEN) * 2
         + Swap.scratch(swaps)
         + GainSum.scratch(count, both),
         9,
@@ -1641,12 +1640,12 @@
         writes[0].start(r)
         again.start(r)
 
-    spans(0, pieces // 4, forward_chunk)
     for freight in freights:
         freight.second()
-    spans(pieces // 4, pieces, forward_chunk)
+    spans(0, 3 * pieces // 4, forward_chunk)
     for freight in freights:
         freight.forward()
+    spans(3 * pieces // 4, pieces, forward_chunk)
     rows_in = down.shape[0] // count
     copies, start = [], 0
     for k, part in enumerate(down_parts):
@@ -1795,21 +1794,21 @@
     own = jnp.roll(own, mine * piece, axis=2)
     own = own.reshape(TAPS + 1, 2, lanes).transpose(1, 0, 2)
     gains_own = jnp.pad(jnp.stack([mixer_gain, feed_gain]), ((0, 14), (0, 0)))
-    tail = jnp.pad(widen(own, width), ((0, 0), (0, 15 - TAPS), (0, 0)))
-    small_top = -(-half_heads * piece // 16) * 16
-    small = jnp.concatenate(
-        [jnp.pad(blocks, ((0, 0), (0, small_top - half_heads * piece), (0, 0))), tail], axis=1
-    )
+    tail = widen(own, width)
+    small_top = half_heads * piece
+    small_rows = -(-(small_top + TAPS + 1) // 16) * 16
+    small = jnp.concatenate([blocks, tail], axis=1)
+    small = jnp.pad(small, ((0, 0), (0, small_rows - small.shape[1]), (0, 0)))
 
     normed_one, pre, gains_all, branch_all, small_all, gate_first = first(
         count, layer_input, gains_own, [branch_halves, small, (feed_gate, 0, narrow)], width
     )
 
     small_all = small_all.reshape(shares, -1, width)
-    tails = small_all[:, small_top:].astype(F32)
+    tails = small_all[:, small_top : small_top + TAPS + 1].astype(F32)
     gain_first = gains_all[:, 0].reshape(feature_count).astype(F32)
     gain_second = gains_all[:, 1].reshape(feature_count).astype(F32)
-    sums = jnp.sum(tails[:, : TAPS + 1], axis=0)
+    sums = jnp.sum(tails, axis=0)
     decay_flat = sums[TAPS, :lanes]
     inside = (jnp.arange(width) < lanes)[None]
     table = jnp.concatenate(
@@ -1939,7 +1938,8 @@
     grad_small = widen(grad_small, slim * spare).reshape(feature_count, spare).astype(BF16)
     last_grads = jnp.concatenate([outlet_grads[:, :lanes], grad_small, branch_grads], axis=1)
     grad_pre, last_grads = lax.optimization_barrier((grad_pre, last_grads))
-    last_sum = line_sum(last_grads)
+    last_sum = line_sum(with_layout_constraint(last_grads, Layout(major_to_minor=(0, 1))))
+    last_sum = with_layout_constraint(last_sum, Layout(major_to_minor=(0, 1)))
     input_grad, layer_output, gains, up_both = last_fold(
         count,
         grad_pre,

time: 624 us -> 618 us (level)
  Pallas kernels: 512 us -> 501 us
    pallas_call x9, Pallas kernels: 512 us -> 501 us  [call(): pl.pallas_call(body, out_shape=[jax.ShapeDtypeStruct(shape, kind) for sha...]
  transfers between devices with their start and end apart: 5 -> 5, of which waited for: 3 -> 4; matrix products, arithmetic and copies ran while one was open for 5% -> 5% of each run, Pallas kernels for 37% -> 35%
where the time goes in v6:
time: 618 us; the launch traced here: 612 us
  Pallas kernels  501 us (81%)
  waiting for transfers between devices  31.3 us (5%)
  local copies, waits for them, and re-layouts  24.8 us (4%)
  other arithmetic  18.9 us (3%)
  matrix products  18.5 us (3%)
  between operations  15 us (2%)
    pallas_call x9, Pallas kernels, call(): pl.pallas_call(body, out_shape=[jax.ShapeDtypeStruct(shape, kind) for sha...  501 us
    reduce_scatter x4, waiting for transfers between devices, line_sum(): lax.psum_scatter(value, 'dp', scatter_dimension=0, axis_index_groups=line...  20.3 us
    dot_general x2, matrix products, by_rows(): lax.dot_general(left, right, TN, preferred_element_type=F32).astype(BF16)  18.5 us
  transfers between devices with their start and end apart: 5, of which 4 were waited for; matrix products, arithmetic and copies ran while one was open for 5% of the time, Pallas kernels for 35%

profile of v6, /device:TPU:0, one launch (start us, length us, event | category | flops | bytes accessed | tf_op | source)
XLA Modules:
  0.0 611.7 jit_solution(2542737281879805395)
XLA Ops:
  7.4 0.7 fusion.21
  8.3 0.9 pad_maximum_fusion.6
  9.2 1.1 copy.100
  10.6 1.1 copy.102
  12.0 0.6 pad.44.refs_3_
  12.7 1.0 pad_maximum_fusion.1.refs_2_
  14.3 75.3 %first.1 = (bf16[2048,2048]{1,0:T(8,128)(2,1)}, f32[2048,768]{1,0:T(8,128)}, bf16[8,16,256]{2,1,0:T(8,128)(2,1)}, bf16[4,512,640]{2,1,0:T(8,128)(2,1)}, bf16[4,9...) custom-call(bf16[256,2048]{1,0:T(8,128)(2,1)} %refs_5_.1, bf16[16,256]{1,0:T(8,128)(2,1)} %fusion.22.refs_1_, ...), custom_call_target="tpu_custom_call" | custom-call | tf_op jit(solution)/shard_map/first/pallas_call | solution.py:325
  89.6 1.0 slice.190
  90.7 0.8 convert_reduce_fusion
  92.9 1.0 convert_element_type.105.refs_1_.refs_8_
  94.2 0.8 pad.48.refs_5_
  95.0 0.8 fusion.42
  95.8 0.6 convert.35.refs_3_.refs_9_
  96.4 1.2 copy.110
  97.9 0.9 fusion.2.refs_3_.refs_10_
  98.8 0.7 maximum_maximum_fusion.refs_2_.refs_9_
  99.5 56.7 %scan_forward.1 = (f32[2048,384]{1,0:T(8,128)}, f32[2048,384]{1,0:T(8,128)}, f32[2048,384]{1,0:T(8,128)}, f32[2056,384]{1,0:T(8,128)}, bf16[2048,384]{1,0:T(8,12...) custom-call(f32[2048,768]{1,0:T(8,128)} %get-tuple-element.62.refs_0, ...), custom_call_target="tpu_custom_call" | custom-call | tf_op jit(solution)/shard_map/scan_forward/pallas_call | solution.py:325
  156.2 57.8 %mixer_fold.1 = (f32[256,2048]{1,0:T(8,128)}, bf16[256,2048]{1,0:T(8,128)(2,1)}, bf16[4,512,512]{2,1,0:T(8,128)(2,1)}, bf16[4,512,256]{2,1,0:T(8,128)(2,1)}) custom-call(bf16[2048,384]{1,0:T(8,128)(2,1)} %get-tuple-element.64.refs_0_, bf16[2048,384]{1,0:T(8,128)(2,1)} %bitcast.82, bf16[256,2048]{1,0:T(8,128)(2,1)} %refs_5_.1, ...), custom_call_target="tpu_custom_call" | custom-call | tf_op jit(solution)/shard_map/mixer_fold/pallas_call | solution.py:325
  214.0 46.6 %gather_rows.2 = (bf16[8,256,2048]{2,1,0:T(8,128)(2,1)}, bf16[4,512,512]{2,1,0:T(8,128)(2,1)}) custom-call(bf16[256,2048]{1,0:T(8,128)(2,1)} %get-tuple-element.67.refs_0_, bf16[256,1536]{1,0:T(8,128)(2,1)} %refs_1_.1), custom_call_target="tpu_custom_call" | custom-call | tf_op jit(solution)/shard_map/gather_rows/pallas_call | solution.py:325
  260.6 47.7 %feed.1 = (bf16[2048,768]{1,0:T(8,128)(2,1)}, bf16[2048,768]{1,0:T(8,128)(2,1)}, bf16[2048,768]{1,0:T(8,128)(2,1)}, bf16[2048,768]{1,0:T(8,128)(2,1)}, bf16[4,512,512]{2,1,0:T(8,128)(2,1)}) custom-call(bf16[2048,2048]{1,0:T(8,128)(2,1)} %bitcast.70, bf16[2048,2048]{1,0:T(8,128)(2,1)} %bitcast.73, bf16[2048,256]{1,0:T(8,128)(2,1)} %bitcast.84, ...), custom_call_target="tpu_custom_call" | custom-call | tf_op jit(solution)/shard_map/feed/pallas_call | solution.py:325
  308.5 52.4 %feed_fold.1 = (f32[256,2048]{1,0:T(8,128)}, bf16[256,2048]{1,0:T(8,128)(2,1)}, f32[8,2048]{1,0:T(8,128)}, bf16[2048,768]{1,0:T(8,128)(2,1)}) custom-call(bf16[2048,768]{1,0:T(8,128)(2,1)} %get-tuple-element.75.refs_0_, bf16[2048,768]{1,0:T(8,128)(2,1)} %get-tuple-element.76.refs_1_.refs_2_, bf16[2048,256]{1,0:T(8,128)(2,1)} %bitcast.85, ...), custom_call_target="tpu_custom_call" | custom-call | tf_op jit(solution)/shard_map/feed_fold/pallas_call | solution.py:325
  360.9 5.7 reduce-scatter.5.cloned.1.call-done
  366.6 40.1 %gather_rows.3 = (bf16[8,256,2048]{2,1,0:T(8,128)(2,1)}, bf16[2048,768]{1,0:T(8,128)(2,1)}) custom-call(bf16[256,2048]{1,0:T(8,128)(2,1)} %get-tuple-element.80.refs_0_, bf16[2048,2048]{1,0:T(8,128)(2,1)} %bitcast.72, bf16[2048,768]{1,0:T(8,128)(2,1)} %get-tuple-element.76.refs_1_.refs_2_), custom_call_target="tpu_custom_call" | custom-call | tf_op jit(solution)/shard_map/gather_rows/pallas_call | solution.py:325
  407.0 1.1 copy-done.1
  408.1 9.2 %convolution_convert_fusion.1 = bf16[2048,384]{1,0:T(8,128)(2,1)} fusion(bf16[2048,2048]{1,0:T(8,128)(2,1)} %bitcast.74, bf16[2048,384]{1,0:T(8,128)(2,1)S(1)} %copy-done.1), kind=kOutput, calls=%fused_computation.2 | convolution fusion | flops 3222011904 | bytes 11534336 | tf_op jit(solution)/shard_map/dot_general | solution.py:1749
  417.3 11.9 %reduce-scatter.7.cloned.1.call-done = bf16[512,768]{1,0:T(8,128)(2,1)} async-done(((bf16[2048,768]{1,0:T(8,128)(2,1)}), bf16[512,768]{1,0:T(8,128)(2,1)}) %reduce-scatter.7.cloned.1.call-update) | async-done | bytes 786448 | tf_op jit(solution)/shard_map/reduce_scatter | solution.py:1873
  429.2 40.3 %scan_backward.1 = (bf16[2048,640]{1,0:T(8,128)(2,1)}, f32[384,768]{1,0:T(8,128)}, f32[8,384]{1,0:T(8,128)}, bf16[2,256,768]{2,1,0:T(8,128)(2,1)}, bf16[2,256,768]{2,1,0:T(8,128)(2,1)}) custom-call(f32[2048,768]{1,0:T(8,128)} %get-tuple-element.62.refs_0_, bf16[2048,2048]{1,0:T(8,128)(2,1)} %bitcast.75, bf16[2048,384]{1,0:T(8,128)(2,1)} %bitcast.83, ...), custom_call_target="tpu_custom_call" | custom-call | tf_op jit(solution)/shard_map/scan_backward/pallas_call | solution.py:325
  469.5 0.9 slice.240
  470.3 0.7 convert_reduce_fusion.8
  471.3 1.3 convert.31
  474.2 9.3 %convolution_convert_fusion = bf16[2048,640]{1,0:T(8,128)(2,1)S(1)} fusion(bf16[2048,2048]{1,0:T(8,128)(2,1)} %get-tuple-element.95, bf16[2048,640]{1,0:T(8,128)(2,1)S(1)} %copy-done), kind=kOutput, calls=%fused_computation.1 | convolution fusion | flops 5370019840 | bytes 13631488 | tf_op jit(solution)/shard_map/dot_general | solution.py:1749
  483.5 3.0 pad_maximum_fusion
  487.9 1.6 copy.126
  489.6 1.3 maximum_convert_fusion
  490.9 2.7 reduce-scatter.9.cloned.1.call-done
  493.6 84.4 %last_fold.1 = (bf16[256,2048]{1,0:T(8,128)(2,1)}, bf16[256,2048]{1,0:T(8,128)(2,1)}, f32[16,256]{1,0:T(8,128)}, bf16[2,256,768]{2,1,0:T(8,128)(2,1)}) custom-call(bf16[2048,640]{1,0:T(8,128)(2,1)} %get-tuple-element.96.refs_0_, bf16[2048,640]{1,0:T(8,128)(2,1)} %bitcast.90, bf16[2048,768]{1,0:T(8,128)(2,1)} %get-tuple-element.98.refs_2_, ...), custom_call_target="tpu_custom_call" | custom-call | tf_op jit(solution)/shard_map/last_fold/pallas_call | solution.py:325
  578.0 1.4 constant_dynamic-slice_fusion
  579.4 1.3 constant_dynamic-slice_fusion.2
  580.9 1.5 collective-permute-start
  582.5 1.3 maximum_convert_fusion.1
  584.0 10.9 %collective-permute-done = bf16[256,1024]{0,1:T(8,128)(2,1)S(1)} collective-permute-done((bf16[256,1024]{0,1:T(8,128)(2,1)S(1)}, bf16[256,1024]{0,1:T(8,128)(2,1)S(1)}, u32[]{:S(2)}, u32[]{:S(2)}) %collective-permute-start) | collective-permute-done | bytes 524320 | tf_op jit(solution)/shard_map/ppermute | solution.py:1963
  596.5 0.7 copy.125
  597.5 0.7 copy.124
  598.4 1.1 copy.123
  599.6 1.1 copy.122
  600.6 0.9 maximum_bitcast_fusion
  602.7 1.0 copy.133
  603.7 1.0 copy.134
  (133 shorter events, 10.6 us)
Async XLA Ops:
  7.2 4.8 copy-start.13
  7.2 4.8 copy-start.14
  7.2 359.4 %reduce-scatter.5.cloned.1.call-start = ((), (), s32[]{:S(2)}) async-start(), calls=%async_computation.4 | async-start | bytes 3932160 | tf_op jit(solution)/shard_map/reduce_scatter | solution.py:1873
  14.3 77.5 %copy-start.12 = (s32[6]{0:T(128)S(1)}, s32[6]{0:T(128)}, u32[]{:S(2)}) copy-start(s32[6]{0:T(128)} %param.17) | copy-start | bytes 76
  89.6 4.3 copy-start.9
  91.5 3.5 copy-start.10
  91.6 4.9 copy-start.5
  95.0 3.9 slice-start
  308.4 120.8 %reduce-scatter.7.cloned.1.call-start = ((), (), s32[]{:S(2)}) async-start(), calls=%async_computation.5 | async-start | bytes 3932160 | tf_op jit(solution)/shard_map/reduce_scatter | solution.py:1873
  360.9 132.7 %reduce-scatter.9.cloned.1.call-start = ((), (), s32[]{:S(2)}) async-start(), calls=%async_computation.6 | async-start | bytes 3932160 | tf_op jit(solution)/shard_map/reduce_scatter | solution.py:1873
  406.7 1.4 copy-start.1
  406.7 172.7 %reduce-scatter.11.cloned.1.call-start = ((), (), s32[]{:S(2)}) async-start(), calls=%async_computation.7 | async-start | bytes 5242880 | tf_op jit(solution)/shard_map/reduce_scatter | solution.py:1873
  429.2 41.1 %copy-start.11 = (f32[5,384]{1,0:T(8,128)S(1)}, f32[5,384]{1,0:T(8,128)}, u32[]{:S(2)}) copy-start(f32[5,384]{1,0:T(8,128)} %copy-done.10) | copy-start | bytes 23044
  469.5 4.7 copy-start
  474.2 9.3 %copy-start.2 = (bf16[2048,384]{1,0:T(8,128)(2,1)S(1)}, bf16[2048,384]{1,0:T(8,128)(2,1)}, u32[]{:S(2)}) copy-start(bf16[2048,384]{1,0:T(8,128)(2,1)} %convolution_convert_fusion.1) | copy-start | bytes 4718596
  486.5 1.1 copy-start.7
  487.7 1.8 copy-start.6
  578.0 4.4 copy-start.8
  580.9 14.0 %collective-permute-start = (bf16[256,1024]{0,1:T(8,128)(2,1)S(1)}, bf16[256,1024]{0,1:T(8,128)(2,1)S(1)}, u32[]{:S(2)}, u32[]{:S(2)}) collective-permute-start(bf16[256,1024]{0,1:T(8,128)(2,1)S(1)} %bitcast.103), channel_id=1, source_target_pairs={{0,4},{4,0},{8,12},{12,8},{16,20},{20,16},{24,28},{28,24},{1,5},{5... | collective-permute-start | bytes 1572872 | tf_op jit(solution)/shard_map/ppermute | solution.py:1963
  599.5 3.2 copy-start.4
  599.6 4.1 copy-start.3
Sparse Core Ops, SparseCore 0:
  308.5 58.0 reduce-scatter.4
  368.9 60.2 reduce-scatter.6
  431.5 62.0 reduce-scatter.8
  495.8 77.8 reduce-scatter.10

commit v7 on v6

--- a/solution.py
+++ b/solution.py
@@ -1966,14 +1966,14 @@
             jnp.where(side == 0, other, kept).astype(F32),
         ]
 
-    lasts = swap(last_sum)
-
-    def columns(start, stop):
-        return jnp.concatenate([value[:, start:stop] for value in lasts], axis=1)
-
-    mixer_out_grad = columns(0, lanes).T
-    branch_gate_grad = columns(width, width + lanes)
-    branch_input_grad = columns(width + lanes, width + 2 * lanes)
+    lasts, branches = swap(last_sum[:, :width]), swap(last_sum[:, width:])
+
+    def columns(values, start, stop):
+        return jnp.concatenate([value[:, start:stop] for value in values], axis=1)
+
+    mixer_out_grad = columns(lasts, 0, lanes).T
+    branch_gate_grad = columns(branches, 0, lanes)
+    branch_input_grad = columns(branches, lanes, 2 * lanes)
     smalls = [value[:, lanes:width].reshape(-1)[:flat_size] for value in lasts]
     one = half_heads * piece * head_width
     tap_size = TAPS * half_heads * piece

time: 618 us -> 614 us (level)
  transfers between devices with their start and end apart: 5 -> 6, of which waited for: 4 -> 5; matrix products, arithmetic and copies ran while one was open for 5% -> 6% of each run, Pallas kernels for 35% -> 36%
where the time goes in v7:
time: 614 us; the launch traced here: 607 us
  Pallas kernels  501 us (82%)
  waiting for transfers between devices  25.3 us (4%)
  local copies, waits for them, and re-layouts  23.9 us (4%)
  other arithmetic  20.8 us (3%)
  matrix products  18.5 us (3%)
  between operations  15 us (2%)
    pallas_call x9, Pallas kernels, call(): pl.pallas_call(body, out_shape=[jax.ShapeDtypeStruct(shape, kind) for sha...  501 us
    reduce_scatter x4, waiting for transfers between devices, line_sum(): lax.psum_scatter(value, 'dp', scatter_dimension=0, axis_index_groups=line...  20.3 us
    dot_general x2, matrix products, by_rows(): lax.dot_general(left, right, TN, preferred_element_type=F32).astype(BF16)  18.5 us
  transfers between devices with their start and end apart: 6, of which 5 were waited for; matrix products, arithmetic and copies ran while one was open for 6% of the time, Pallas kernels for 36%

profile of v7, /device:TPU:0, one launch (start us, length us, event | category | flops | bytes accessed | tf_op | source)
XLA Modules:
  0.0 607.3 jit_solution(7914121170169847454)
XLA Ops:
  7.4 0.7 fusion.23
  8.3 0.9 pad_maximum_fusion.6
  9.2 1.1 copy.94
  10.6 1.1 copy.96
  12.7 1.0 pad_maximum_fusion.1.refs_2_
  14.3 75.3 %first.1 = (bf16[2048,2048]{1,0:T(8,128)(2,1)}, f32[2048,768]{1,0:T(8,128)}, bf16[8,16,256]{2,1,0:T(8,128)(2,1)}, bf16[4,512,640]{2,1,0:T(8,128)(2,1)}, bf16[4,9...) custom-call(bf16[256,2048]{1,0:T(8,128)(2,1)} %refs_5_.1, bf16[16,256]{1,0:T(8,128)(2,1)} %fusion.24.refs_1_, ...), custom_call_target="tpu_custom_call" | custom-call | tf_op jit(solution)/shard_map/first/pallas_call | solution.py:325
  89.6 1.0 slice.198
  90.7 0.8 convert_reduce_fusion
  92.9 1.0 convert_element_type.111.refs_1_.refs_8_
  94.2 0.8 pad.48.refs_5_
  95.0 0.8 fusion.44
  96.4 1.2 copy.104
  97.9 0.9 fusion.2.refs_3_.refs_10_
  98.8 0.7 maximum_maximum_fusion.refs_2_.refs_9_
  99.5 56.7 %scan_forward.1 = (f32[2048,384]{1,0:T(8,128)}, f32[2048,384]{1,0:T(8,128)}, f32[2048,384]{1,0:T(8,128)}, f32[2056,384]{1,0:T(8,128)}, bf16[2048,384]{1,0:T(8,12...) custom-call(f32[2048,768]{1,0:T(8,128)} %get-tuple-element.62.refs_0, ...), custom_call_target="tpu_custom_call" | custom-call | tf_op jit(solution)/shard_map/scan_forward/pallas_call | solution.py:325
  156.2 57.8 %mixer_fold.1 = (f32[256,2048]{1,0:T(8,128)}, bf16[256,2048]{1,0:T(8,128)(2,1)}, bf16[4,512,512]{2,1,0:T(8,128)(2,1)}, bf16[4,512,256]{2,1,0:T(8,128)(2,1)}) custom-call(bf16[2048,384]{1,0:T(8,128)(2,1)} %get-tuple-element.64.refs_0_, bf16[2048,384]{1,0:T(8,128)(2,1)} %bitcast.92, bf16[256,2048]{1,0:T(8,128)(2,1)} %refs_5_.1, ...), custom_call_target="tpu_custom_call" | custom-call | tf_op jit(solution)/shard_map/mixer_fold/pallas_call | solution.py:325
  214.0 46.6 %gather_rows.2 = (bf16[8,256,2048]{2,1,0:T(8,128)(2,1)}, bf16[4,512,512]{2,1,0:T(8,128)(2,1)}) custom-call(bf16[256,2048]{1,0:T(8,128)(2,1)} %get-tuple-element.67.refs_0_, bf16[256,1536]{1,0:T(8,128)(2,1)} %refs_1_.1), custom_call_target="tpu_custom_call" | custom-call | tf_op jit(solution)/shard_map/gather_rows/pallas_call | solution.py:325
  260.6 47.7 %feed.1 = (bf16[2048,768]{1,0:T(8,128)(2,1)}, bf16[2048,768]{1,0:T(8,128)(2,1)}, bf16[2048,768]{1,0:T(8,128)(2,1)}, bf16[2048,768]{1,0:T(8,128)(2,1)}, bf16[4,512,512]{2,1,0:T(8,128)(2,1)}) custom-call(bf16[2048,2048]{1,0:T(8,128)(2,1)} %bitcast.80, bf16[2048,2048]{1,0:T(8,128)(2,1)} %bitcast.83, bf16[2048,256]{1,0:T(8,128)(2,1)} %bitcast.94, ...), custom_call_target="tpu_custom_call" | custom-call | tf_op jit(solution)/shard_map/feed/pallas_call | solution.py:325
  308.5 52.4 %feed_fold.1 = (f32[256,2048]{1,0:T(8,128)}, bf16[256,2048]{1,0:T(8,128)(2,1)}, f32[8,2048]{1,0:T(8,128)}, bf16[2048,768]{1,0:T(8,128)(2,1)}) custom-call(bf16[2048,768]{1,0:T(8,128)(2,1)} %get-tuple-element.75.refs_0_, bf16[2048,768]{1,0:T(8,128)(2,1)} %get-tuple-element.76.refs_1_.refs_2_, bf16[2048,256]{1,0:T(8,128)(2,1)} %bitcast.95, ...), custom_call_target="tpu_custom_call" | custom-call | tf_op jit(solution)/shard_map/feed_fold/pallas_call | solution.py:325
  360.9 5.7 reduce-scatter.5.cloned.1.call-done
  366.6 40.1 %gather_rows.3 = (bf16[8,256,2048]{2,1,0:T(8,128)(2,1)}, bf16[2048,768]{1,0:T(8,128)(2,1)}) custom-call(bf16[256,2048]{1,0:T(8,128)(2,1)} %get-tuple-element.80.refs_0_, bf16[2048,2048]{1,0:T(8,128)(2,1)} %bitcast.82, bf16[2048,768]{1,0:T(8,128)(2,1)} %get-tuple-element.76.refs_1_.refs_2_), custom_call_target="tpu_custom_call" | custom-call | tf_op jit(solution)/shard_map/gather_rows/pallas_call | solution.py:325
  407.0 1.1 copy-done.1
  408.1 9.2 %convolution_convert_fusion.1 = bf16[2048,384]{1,0:T(8,128)(2,1)} fusion(bf16[2048,2048]{1,0:T(8,128)(2,1)} %bitcast.84, bf16[2048,384]{1,0:T(8,128)(2,1)S(1)} %copy-done.1), kind=kOutput, calls=%fused_computation.2 | convolution fusion | flops 3222011904 | bytes 11534336 | tf_op jit(solution)/shard_map/dot_general | solution.py:1749
  417.3 11.9 %reduce-scatter.7.cloned.1.call-done = bf16[512,768]{1,0:T(8,128)(2,1)} async-done(((bf16[2048,768]{1,0:T(8,128)(2,1)}), bf16[512,768]{1,0:T(8,128)(2,1)}) %reduce-scatter.7.cloned.1.call-update) | async-done | bytes 786448 | tf_op jit(solution)/shard_map/reduce_scatter | solution.py:1873
  429.2 40.3 %scan_backward.1 = (bf16[2048,640]{1,0:T(8,128)(2,1)}, f32[384,768]{1,0:T(8,128)}, f32[8,384]{1,0:T(8,128)}, bf16[2,256,768]{2,1,0:T(8,128)(2,1)}, bf16[2,256,768]{2,1,0:T(8,128)(2,1)}) custom-call(f32[2048,768]{1,0:T(8,128)} %get-tuple-element.62.refs_0_, bf16[2048,2048]{1,0:T(8,128)(2,1)} %bitcast.85, bf16[2048,384]{1,0:T(8,128)(2,1)} %bitcast.93, ...), custom_call_target="tpu_custom_call" | custom-call | tf_op jit(solution)/shard_map/scan_backward/pallas_call | solution.py:325
  469.5 0.9 slice.250
  470.4 0.7 convert_reduce_fusion.8
  471.3 1.3 convert.31
  474.2 9.3 %convolution_convert_fusion = bf16[2048,640]{1,0:T(8,128)(2,1)S(1)} fusion(bf16[2048,2048]{1,0:T(8,128)(2,1)} %get-tuple-element.95, bf16[2048,640]{1,0:T(8,128)(2,1)S(1)} %copy-done), kind=kOutput, calls=%fused_computation.1 | convolution fusion | flops 5370019840 | bytes 13631488 | tf_op jit(solution)/shard_map/dot_general | solution.py:1749
  483.5 3.0 pad_maximum_fusion
  487.9 1.6 copy.118
  489.6 1.3 maximum_convert_fusion
  490.9 2.7 reduce-scatter.9.cloned.1.call-done
  493.6 84.4 %last_fold.1 = (bf16[256,2048]{1,0:T(8,128)(2,1)}, bf16[256,2048]{1,0:T(8,128)(2,1)}, f32[16,256]{1,0:T(8,128)}, bf16[2,256,768]{2,1,0:T(8,128)(2,1)}) custom-call(bf16[2048,640]{1,0:T(8,128)(2,1)} %get-tuple-element.96.refs_0_, bf16[2048,640]{1,0:T(8,128)(2,1)} %bitcast.102, bf16[2048,768]{1,0:T(8,128)(2,1)} %get-tuple-element.98.refs_2_, ...), custom_call_target="tpu_custom_call" | custom-call | tf_op jit(solution)/shard_map/last_fold/pallas_call | solution.py:325
  578.1 1.2 slice_bitcast_fusion.3
  579.2 1.3 maximum_convert_fusion.1
  580.6 1.1 slice.212
  581.9 1.5 collective-permute-start.1
  583.4 1.3 constant_dynamic-slice_fusion
  585.6 4.1 collective-permute-done.1
  591.1 0.7 copy.117
  592.2 0.7 copy.116
  594.2 0.9 maximum_bitcast_fusion
  595.1 0.8 collective-permute-done
  596.3 1.0 pad_maximum_fusion.3
  597.4 1.0 pad_maximum_fusion.2
  598.4 1.0 copy.125
  599.3 1.0 copy.126
  (139 shorter events, 12.6 us)
Async XLA Ops:
  7.2 4.8 copy-start.13
  7.2 4.8 copy-start.14
  7.2 359.4 %reduce-scatter.5.cloned.1.call-start = ((), (), s32[]{:S(2)}) async-start(), calls=%async_computation.4 | async-start | bytes 3932160 | tf_op jit(solution)/shard_map/reduce_scatter | solution.py:1873
  14.3 77.5 %copy-start.12 = (s32[6]{0:T(128)S(1)}, s32[6]{0:T(128)}, u32[]{:S(2)}) copy-start(s32[6]{0:T(128)} %param.17) | copy-start | bytes 76
  89.6 4.3 copy-start.9
  91.5 3.5 copy-start.10
  91.6 4.9 copy-start.6
  95.0 3.9 slice-start
  308.4 120.8 %reduce-scatter.7.cloned.1.call-start = ((), (), s32[]{:S(2)}) async-start(), calls=%async_computation.5 | async-start | bytes 3932160 | tf_op jit(solution)/shard_map/reduce_scatter | solution.py:1873
  360.9 132.7 %reduce-scatter.9.cloned.1.call-start = ((), (), s32[]{:S(2)}) async-start(), calls=%async_computation.6 | async-start | bytes 3932160 | tf_op jit(solution)/shard_map/reduce_scatter | solution.py:1873
  406.7 1.4 copy-start.1
  406.7 173.8 %reduce-scatter.11.cloned.1.call-start = ((), (), s32[]{:S(2)}) async-start(), calls=%async_computation.7 | async-start | bytes 5242880 | tf_op jit(solution)/shard_map/reduce_scatter | solution.py:1873
  429.2 41.2 %copy-start.11 = (f32[5,384]{1,0:T(8,128)S(1)}, f32[5,384]{1,0:T(8,128)}, u32[]{:S(2)}) copy-start(f32[5,384]{1,0:T(8,128)} %copy-done.10) | copy-start | bytes 23044
  469.5 4.7 copy-start
  474.2 9.3 %copy-start.2 = (bf16[2048,384]{1,0:T(8,128)(2,1)S(1)}, bf16[2048,384]{1,0:T(8,128)(2,1)}, u32[]{:S(2)}) copy-start(bf16[2048,384]{1,0:T(8,128)(2,1)} %convolution_convert_fusion.1) | copy-start | bytes 4718596
  486.5 1.1 copy-start.8
  487.7 1.8 copy-start.7
  580.5 4.3 copy-start.3
  581.9 7.8 %collective-permute-start.1 = (bf16[256,384]{0,1:T(8,128)(2,1)S(1)}, bf16[256,384]{0,1:T(8,128)(2,1)S(1)}, u32[]{:S(2)}, u32[]{:S(2)}) collective-permute-start(bf16[256,384]{0,1:T(8,128)(2,1)S(1)} %bitcast.118), channel_id=1, source_target_pairs={{0,4},{4,0},{8,12},{12,8},{16,20},{20,16},{24,28},{28,24},{1,5},{5... | collective-permute-start | bytes 589832 | tf_op jit(solution)/shard_map/ppermute | solution.py:1963
  585.0 10.9 %collective-permute-start = (bf16[256,640]{1,0:T(8,128)(2,1)S(1)}, bf16[256,640]{1,0:T(8,128)(2,1)S(1)}, u32[]{:S(2)}, u32[]{:S(2)}) collective-permute-start(bf16[256,640]{1,0:T(8,128)(2,1)S(1)} %dynamic-slice_bitcast_fusion), channel_id=1, source_target_pairs={{0,4},{4,0},{8,12},{12,8},{16,20},{20,16},{24,28},{28,24},{1,5},{5... | collective-permute-start | bytes 983048 | tf_op jit(solution)/shard_map/ppermute | solution.py:1963
  596.2 2.2 copy-start.5
  596.3 3.0 copy-start.4
Sparse Core Ops, SparseCore 0:
  308.5 58.0 reduce-scatter.4
  368.9 60.2 reduce-scatter.6
  431.5 62.0 reduce-scatter.8
  495.8 77.8 reduce-scatter.10

commit v8 on v7

--- a/solution.py
+++ b/solution.py
@@ -1297,11 +1297,10 @@
             stream.start(r)
 
     pieces = rows // CHUNK
-    spans(0, 1, gate_chunk)
     for freight in freights:
         freight.second()
     gather.start_across()
-    spans(1, pieces, gate_chunk)
+    spans(0, pieces, gate_chunk)
     prod, total = tile_scan(prods, sums, rows, width, False)
     entering = pool(count, prod, total, outgoing, slots, send, receive, False)
     for freight in freights:

time: 614 us -> 612 us (level)
  no operation moved by 1% of the time
where the time goes in v8:
time: 612 us; the launch traced here: 607 us
  Pallas kernels  501 us (82%)
  waiting for transfers between devices  25.5 us (4%)
  local copies, waits for them, and re-layouts  23.9 us (4%)
  other arithmetic  20.8 us (3%)
  matrix products  18.5 us (3%)
  between operations  15 us (2%)
    pallas_call x9, Pallas kernels, call(): pl.pallas_call(body, out_shape=[jax.ShapeDtypeStruct(shape, kind) for sha...  501 us
    reduce_scatter x4, waiting for transfers between devices, line_sum(): lax.psum_scatter(value, 'dp', scatter_dimension=0, axis_index_groups=line...  20.5 us
    dot_general x2, matrix products, by_rows(): lax.dot_general(left, right, TN, preferred_element_type=F32).astype(BF16)  18.5 us
  transfers between devices with their start and end apart: 6, of which 5 were waited for; matrix products, arithmetic and copies ran while one was open for 6% of the time, Pallas kernels for 36%

profile of v8, /device:TPU:0, one launch (start us, length us, event | category | flops | bytes accessed | tf_op | source)
XLA Modules:
  0.0 607.0 jit_solution(6001418181467452056)
XLA Ops:
  7.4 0.7 fusion.23
  8.3 0.9 pad_maximum_fusion.6
  9.2 1.1 copy.94
  10.6 1.1 copy.96
  12.7 1.0 pad_maximum_fusion.1.refs_2_
  14.3 75.3 %first.1 = (bf16[2048,2048]{1,0:T(8,128)(2,1)}, f32[2048,768]{1,0:T(8,128)}, bf16[8,16,256]{2,1,0:T(8,128)(2,1)}, bf16[4,512,640]{2,1,0:T(8,128)(2,1)}, bf16[4,9...) custom-call(bf16[256,2048]{1,0:T(8,128)(2,1)} %refs_5_.1, bf16[16,256]{1,0:T(8,128)(2,1)} %fusion.24.refs_1_, ...), custom_call_target="tpu_custom_call" | custom-call | tf_op jit(solution)/shard_map/first/pallas_call | solution.py:325
  89.6 1.0 slice.198
  90.7 0.8 convert_reduce_fusion
  92.9 1.0 convert_element_type.111.refs_1_.refs_8_
  94.2 0.8 pad.48.refs_5_
  95.0 0.8 fusion.44
  96.4 1.2 copy.104
  97.9 0.9 fusion.2.refs_3_.refs_10_
  98.8 0.7 maximum_maximum_fusion.refs_2_.refs_9_
  99.5 56.7 %scan_forward.1 = (f32[2048,384]{1,0:T(8,128)}, f32[2048,384]{1,0:T(8,128)}, f32[2048,384]{1,0:T(8,128)}, f32[2056,384]{1,0:T(8,128)}, bf16[2048,384]{1,0:T(8,12...) custom-call(f32[2048,768]{1,0:T(8,128)} %get-tuple-element.62.refs_0, ...), custom_call_target="tpu_custom_call" | custom-call | tf_op jit(solution)/shard_map/scan_forward/pallas_call | solution.py:325
  156.2 57.8 %mixer_fold.1 = (f32[256,2048]{1,0:T(8,128)}, bf16[256,2048]{1,0:T(8,128)(2,1)}, bf16[4,512,512]{2,1,0:T(8,128)(2,1)}, bf16[4,512,256]{2,1,0:T(8,128)(2,1)}) custom-call(bf16[2048,384]{1,0:T(8,128)(2,1)} %get-tuple-element.64.refs_0_, bf16[2048,384]{1,0:T(8,128)(2,1)} %bitcast.92, bf16[256,2048]{1,0:T(8,128)(2,1)} %refs_5_.1, ...), custom_call_target="tpu_custom_call" | custom-call | tf_op jit(solution)/shard_map/mixer_fold/pallas_call | solution.py:325
  214.0 46.6 %gather_rows.2 = (bf16[8,256,2048]{2,1,0:T(8,128)(2,1)}, bf16[4,512,512]{2,1,0:T(8,128)(2,1)}) custom-call(bf16[256,2048]{1,0:T(8,128)(2,1)} %get-tuple-element.67.refs_0_, bf16[256,1536]{1,0:T(8,128)(2,1)} %refs_1_.1), custom_call_target="tpu_custom_call" | custom-call | tf_op jit(solution)/shard_map/gather_rows/pallas_call | solution.py:325
  260.6 47.7 %feed.1 = (bf16[2048,768]{1,0:T(8,128)(2,1)}, bf16[2048,768]{1,0:T(8,128)(2,1)}, bf16[2048,768]{1,0:T(8,128)(2,1)}, bf16[2048,768]{1,0:T(8,128)(2,1)}, bf16[4,512,512]{2,1,0:T(8,128)(2,1)}) custom-call(bf16[2048,2048]{1,0:T(8,128)(2,1)} %bitcast.80, bf16[2048,2048]{1,0:T(8,128)(2,1)} %bitcast.83, bf16[2048,256]{1,0:T(8,128)(2,1)} %bitcast.94, ...), custom_call_target="tpu_custom_call" | custom-call | tf_op jit(solution)/shard_map/feed/pallas_call | solution.py:325
  308.5 51.9 %feed_fold.1 = (f32[256,2048]{1,0:T(8,128)}, bf16[256,2048]{1,0:T(8,128)(2,1)}, f32[8,2048]{1,0:T(8,128)}, bf16[2048,768]{1,0:T(8,128)(2,1)}) custom-call(bf16[2048,768]{1,0:T(8,128)(2,1)} %get-tuple-element.75.refs_0_, bf16[2048,768]{1,0:T(8,128)(2,1)} %get-tuple-element.76.refs_1_.refs_2_, bf16[2048,256]{1,0:T(8,128)(2,1)} %bitcast.95, ...), custom_call_target="tpu_custom_call" | custom-call | tf_op jit(solution)/shard_map/feed_fold/pallas_call | solution.py:325
  360.4 5.8 reduce-scatter.5.cloned.1.call-done
  366.3 40.1 %gather_rows.3 = (bf16[8,256,2048]{2,1,0:T(8,128)(2,1)}, bf16[2048,768]{1,0:T(8,128)(2,1)}) custom-call(bf16[256,2048]{1,0:T(8,128)(2,1)} %get-tuple-element.80.refs_0_, bf16[2048,2048]{1,0:T(8,128)(2,1)} %bitcast.82, bf16[2048,768]{1,0:T(8,128)(2,1)} %get-tuple-element.76.refs_1_.refs_2_), custom_call_target="tpu_custom_call" | custom-call | tf_op jit(solution)/shard_map/gather_rows/pallas_call | solution.py:325
  406.7 1.1 copy-done.1
  407.8 9.2 %convolution_convert_fusion.1 = bf16[2048,384]{1,0:T(8,128)(2,1)} fusion(bf16[2048,2048]{1,0:T(8,128)(2,1)} %bitcast.84, bf16[2048,384]{1,0:T(8,128)(2,1)S(1)} %copy-done.1), kind=kOutput, calls=%fused_computation.2 | convolution fusion | flops 3222011904 | bytes 11534336 | tf_op jit(solution)/shard_map/dot_general | solution.py:1748
  416.9 12.0 %reduce-scatter.7.cloned.1.call-done = bf16[512,768]{1,0:T(8,128)(2,1)} async-done(((bf16[2048,768]{1,0:T(8,128)(2,1)}), bf16[512,768]{1,0:T(8,128)(2,1)}) %reduce-scatter.7.cloned.1.call-update) | async-done | bytes 786448 | tf_op jit(solution)/shard_map/reduce_scatter | solution.py:1872
  428.9 40.3 %scan_backward.1 = (bf16[2048,640]{1,0:T(8,128)(2,1)}, f32[384,768]{1,0:T(8,128)}, f32[8,384]{1,0:T(8,128)}, bf16[2,256,768]{2,1,0:T(8,128)(2,1)}, bf16[2,256,768]{2,1,0:T(8,128)(2,1)}) custom-call(f32[2048,768]{1,0:T(8,128)} %get-tuple-element.62.refs_0_, bf16[2048,2048]{1,0:T(8,128)(2,1)} %bitcast.85, bf16[2048,384]{1,0:T(8,128)(2,1)} %bitcast.93, ...), custom_call_target="tpu_custom_call" | custom-call | tf_op jit(solution)/shard_map/scan_backward/pallas_call | solution.py:325
  469.2 0.9 slice.250
  470.0 0.7 convert_reduce_fusion.8
  471.0 1.3 convert.31
  473.9 9.3 %convolution_convert_fusion = bf16[2048,640]{1,0:T(8,128)(2,1)S(1)} fusion(bf16[2048,2048]{1,0:T(8,128)(2,1)} %get-tuple-element.95, bf16[2048,640]{1,0:T(8,128)(2,1)S(1)} %copy-done), kind=kOutput, calls=%fused_computation.1 | convolution fusion | flops 5370019840 | bytes 13631488 | tf_op jit(solution)/shard_map/dot_general | solution.py:1748
  483.2 3.0 pad_maximum_fusion
  487.6 1.6 copy.118
  489.3 1.3 maximum_convert_fusion
  490.6 2.7 reduce-scatter.9.cloned.1.call-done
  493.3 84.4 %last_fold.1 = (bf16[256,2048]{1,0:T(8,128)(2,1)}, bf16[256,2048]{1,0:T(8,128)(2,1)}, f32[16,256]{1,0:T(8,128)}, bf16[2,256,768]{2,1,0:T(8,128)(2,1)}) custom-call(bf16[2048,640]{1,0:T(8,128)(2,1)} %get-tuple-element.96.refs_0_, bf16[2048,640]{1,0:T(8,128)(2,1)} %bitcast.102, bf16[2048,768]{1,0:T(8,128)(2,1)} %get-tuple-element.98.refs_2_, ...), custom_call_target="tpu_custom_call" | custom-call | tf_op jit(solution)/shard_map/last_fold/pallas_call | solution.py:325
  577.7 1.2 slice_bitcast_fusion.3
  578.9 1.3 maximum_convert_fusion.1
  580.2 1.1 slice.212
  581.5 1.6 collective-permute-start.1
  583.1 1.3 constant_dynamic-slice_fusion
  585.3 4.1 collective-permute-done.1
  590.8 0.7 copy.117
  591.8 0.7 copy.116
  593.9 0.9 maximum_bitcast_fusion
  594.7 0.8 collective-permute-done
  596.0 1.0 pad_maximum_fusion.3
  597.0 1.0 pad_maximum_fusion.2
  598.0 1.0 copy.125
  599.0 1.0 copy.126
  (139 shorter events, 12.6 us)
Async XLA Ops:
  7.2 4.8 copy-start.13
  7.2 4.8 copy-start.14
  7.2 359.1 %reduce-scatter.5.cloned.1.call-start = ((), (), s32[]{:S(2)}) async-start(), calls=%async_computation.4 | async-start | bytes 3932160 | tf_op jit(solution)/shard_map/reduce_scatter | solution.py:1872
  14.3 77.5 %copy-start.12 = (s32[6]{0:T(128)S(1)}, s32[6]{0:T(128)}, u32[]{:S(2)}) copy-start(s32[6]{0:T(128)} %param.17) | copy-start | bytes 76
  89.6 4.3 copy-start.9
  91.5 3.5 copy-start.10
  91.6 4.9 copy-start.6
  95.0 3.9 slice-start
  308.4 120.5 %reduce-scatter.7.cloned.1.call-start = ((), (), s32[]{:S(2)}) async-start(), calls=%async_computation.5 | async-start | bytes 3932160 | tf_op jit(solution)/shard_map/reduce_scatter | solution.py:1872
  360.4 132.9 %reduce-scatter.9.cloned.1.call-start = ((), (), s32[]{:S(2)}) async-start(), calls=%async_computation.6 | async-start | bytes 3932160 | tf_op jit(solution)/shard_map/reduce_scatter | solution.py:1872
  406.4 1.4 copy-start.1
  406.4 173.8 %reduce-scatter.11.cloned.1.call-start = ((), (), s32[]{:S(2)}) async-start(), calls=%async_computation.7 | async-start | bytes 5242880 | tf_op jit(solution)/shard_map/reduce_scatter | solution.py:1872
  428.9 41.1 %copy-start.11 = (f32[5,384]{1,0:T(8,128)S(1)}, f32[5,384]{1,0:T(8,128)}, u32[]{:S(2)}) copy-start(f32[5,384]{1,0:T(8,128)} %copy-done.10) | copy-start | bytes 23044
  469.2 4.7 copy-start
  473.9 9.3 %copy-start.2 = (bf16[2048,384]{1,0:T(8,128)(2,1)S(1)}, bf16[2048,384]{1,0:T(8,128)(2,1)}, u32[]{:S(2)}) copy-start(bf16[2048,384]{1,0:T(8,128)(2,1)} %convolution_convert_fusion.1) | copy-start | bytes 4718596
  486.2 1.1 copy-start.8
  487.4 1.8 copy-start.7
  580.2 4.3 copy-start.3
  581.5 7.8 %collective-permute-start.1 = (bf16[256,384]{0,1:T(8,128)(2,1)S(1)}, bf16[256,384]{0,1:T(8,128)(2,1)S(1)}, u32[]{:S(2)}, u32[]{:S(2)}) collective-permute-start(bf16[256,384]{0,1:T(8,128)(2,1)S(1)} %bitcast.118), channel_id=1, source_target_pairs={{0,4},{4,0},{8,12},{12,8},{16,20},{20,16},{24,28},{28,24},{1,5},{5... | collective-permute-start | bytes 589832 | tf_op jit(solution)/shard_map/ppermute | solution.py:1962
  584.7 10.9 %collective-permute-start = (bf16[256,640]{1,0:T(8,128)(2,1)S(1)}, bf16[256,640]{1,0:T(8,128)(2,1)S(1)}, u32[]{:S(2)}, u32[]{:S(2)}) collective-permute-start(bf16[256,640]{1,0:T(8,128)(2,1)S(1)} %dynamic-slice_bitcast_fusion), channel_id=1, source_target_pairs={{0,4},{4,0},{8,12},{12,8},{16,20},{20,16},{24,28},{28,24},{1,5},{5... | collective-permute-start | bytes 983048 | tf_op jit(solution)/shard_map/ppermute | solution.py:1962
  595.8 2.2 copy-start.5
  596.0 3.0 copy-start.4
Sparse Core Ops, SparseCore 0:
  308.5 57.6 reduce-scatter.4
  368.6 60.2 reduce-scatter.6
  431.2 62.0 reduce-scatter.8
  495.5 77.8 reduce-scatter.10
